TPU v7x, 32 devices: a whole 2x2x4 slice. The times are simulated.
32 devices in a mesh: prow: 4 (over x, core), pcol: 8 (over z, y).
Axes of the slice: x: 2, y: 2, z: 4, core: 2. Of those that a mesh axis runs over, the one named last changes fastest.
Arguments:
- matrix: bfloat16 [5, 2048, 2, 4096], P(None, 'prow', None, 'pcol'), may hold values from -6 to 6
- pivots: int32 [2, 512], replicated, may hold values from 0 to 10239, as said below
- lower_inverse: bfloat16 [2, 512, 512], replicated, as said below
- upper_inverse: bfloat16 [2, 512, 512], replicated, as said below
Outputs:
- factored: bfloat16 [5, 2048, 2, 4096], P(None, 'prow', None, 'pcol')
Inputs may be any that keep to these rules, and one draw needn't show every extreme that they name: `pivots`: for panel k, entry i is either k * 512 + i (the row stays) or a row from (k + 1) * 512 on; the entries of one panel are distinct; entry 511 of each panel is 10239, and entry 0 of panel 0 is 0. Each lower_inverse[k] is unit lower triangular. Each upper_inverse[k] is upper triangular with a positive diagonal.
All inputs are finite; a program needn't handle non-finite values.
Results may differ from a plain program's by a relative error of at most 0.0084.
Values may be sent and summed in bfloat16 or wider, within the bound.
No kernel may reach another device: no remote copies, remote signals or barrier semaphores. Data moves between devices by JAX's collectives and lax.ppermute only.
A program may use at most 128 MiB of HBM per device.

v0:
```python
import jax
import jax.numpy as jnp
from jax import lax
from jax.sharding import PartitionSpec as P


def from_root(value, axis, source):
    kept = jnp.where(lax.axis_index(axis) == source, value, 0).astype(value.dtype)
    return lax.psum(kept, axis)


def swap_source(pivot_list, top_start, targets, block_width):
    offset = targets - top_start
    in_top = (offset >= 0) & (offset < block_width)
    from_top = jnp.take(pivot_list, jnp.clip(offset, 0, block_width - 1))
    matches = targets[:, None] == pivot_list[None, :]
    matched = jnp.any(matches, axis=1)
    match_index = jnp.sum(
        jnp.where(matches, jnp.arange(block_width, dtype=jnp.int32)[None, :], 0), axis=1
    )
    return jnp.where(in_top, from_top, jnp.where(matched, top_start + match_index, targets))


def collect_rows(local_tiles, sources, my_row, row_devices, block_width):
    holder = sources // block_width % row_devices
    position = sources // (block_width * row_devices) * block_width + sources % block_width
    picked = jnp.take(local_tiles, position, axis=0)
    return jnp.where((holder == my_row)[:, None], picked, jnp.zeros((), picked.dtype))


def place_rows(local_tiles, targets, values, my_row, row_devices, block_width):
    holder = targets // block_width % row_devices
    position = targets // (block_width * row_devices) * block_width + targets % block_width
    position = jnp.where(holder == my_row, position, local_tiles.shape[0])
    return local_tiles.at[position].set(values, mode="drop")


def body(matrix, pivots, lower_inverse, upper_inverse):
    row_blocks, block_width, col_blocks, _ = matrix.shape
    steps_count = pivots.shape[0]
    row_devices = lax.axis_size("prow")
    col_devices = lax.axis_size("pcol")
    my_row = lax.axis_index("prow")
    my_col = lax.axis_index("pcol")
    local_tiles = matrix.reshape(row_blocks * block_width, col_blocks * block_width)
    row_slot = jnp.arange(row_blocks * block_width, dtype=jnp.int32)
    global_rows = (
        row_slot // block_width * row_devices + my_row
    ) * block_width + row_slot % block_width
    col_slot = jnp.arange(col_blocks * block_width, dtype=jnp.int32)
    global_cols = (
        col_slot // block_width * col_devices + my_col
    ) * block_width + col_slot % block_width
    top_offsets = jnp.arange(block_width, dtype=jnp.int32)
    for panel_step in range(steps_count):
        top_start = panel_step * block_width
        next_start = top_start + block_width
        row_start = panel_step // row_devices * block_width
        targets = jnp.concatenate([top_start + top_offsets, pivots[panel_step]])
        sources = swap_source(pivots[panel_step], top_start, targets, block_width)
        picked_rows = collect_rows(local_tiles, sources, my_row, row_devices, block_width)
        moved_rows = lax.psum(picked_rows.astype(jnp.float32).astype(jnp.bfloat16), "prow")
        local_tiles = place_rows(local_tiles, targets, moved_rows, my_row, row_devices, block_width)
        top_rows = moved_rows[:block_width]
        col_root = panel_step % col_devices
        col_start = panel_step // col_devices * block_width
        panel_cols = local_tiles[:, col_start : col_start + block_width]
        factor = jnp.dot(
            panel_cols, upper_inverse[panel_step], preferred_element_type=jnp.float32
        ).astype(jnp.bfloat16)
        factor = from_root(factor, "pcol", col_root)
        top_product = jnp.dot(
            lower_inverse[panel_step], top_rows, preferred_element_type=jnp.float32
        ).astype(jnp.bfloat16)
        below_mask = global_rows >= next_start
        right_mask = global_cols >= next_start
        update = jnp.dot(factor, top_product, preferred_element_type=jnp.float32)
        trailing = (local_tiles.astype(jnp.float32) - update).astype(jnp.bfloat16)
        local_tiles = jnp.where(below_mask[:, None] & right_mask[None, :], trailing, local_tiles)
        top_here = my_row == panel_step % row_devices
        old_top = local_tiles[row_start : row_start + block_width]
        new_top = jnp.where(top_here & right_mask[None, :], top_product, old_top)
        local_tiles = local_tiles.at[row_start : row_start + block_width].set(new_top)
        col_here = my_col == col_root
        old_panel = local_tiles[:, col_start : col_start + block_width]
        new_panel = jnp.where(col_here & below_mask[:, None], factor, old_panel)
        local_tiles = local_tiles.at[:, col_start : col_start + block_width].set(new_panel)
    return local_tiles.reshape(matrix.shape)


def solution(mesh):
    placed = (P(None, "prow", None, "pcol"), P(), P(), P())
    return jax.shard_map(
        body, mesh=mesh, in_specs=placed, out_specs=P(None, "prow", None, "pcol"), check_vma=False
    )
```

profile of v0, /device:TPU:0, one launch (start us, length us, event | category | flops | bytes accessed | tf_op | source)
XLA Modules:
  0.0 462.4 jit_solution(3164352334252855741)
XLA Ops:
  6.5 0.0 all-reduce.5.cloned.1.call-start
  6.5 0.8 fusion.66
  7.3 0.4 fusion.6
  7.8 0.4 compare_reduce_fusion.1
  8.2 6.9 %gather_fusion = s32[1024]{0:T(1024)S(1)} fusion(s32[512]{0:T(512)S(1)} %bitcast.40, s32[1024]{0:T(1024)S(1)} %get-tuple-element.69), kind=kCustom, calls=%fused_computation.clone | custom fusion | bytes 12288 | tf_op jit(solution)/shard_map/jit(_take)/gather | solution.py:15
  15.2 6.5 %copy.13 = bf16[320,8,2,512]{3,1,2,0:T(8,128)(2,1)} copy(bf16[320,8,2,512]{3,2,1,0:T(2,128)(2,1)} %bitcast.44) | data formatting | bytes 10485760
  21.7 8.1 %gather_fusion.1 = bf16[1024,1024]{1,0:T(8,128)(2,1)S(1)} fusion(bf16[2560,1024]{1,0:T(8,128)(2,1)} %bitcast.42, s32[1024]{0:T(1024)S(1)} %broadcast_clamp_fusion.1), kind=kCustom, calls=%fused_computation.1.clone | custom fusion | bytes 4198400 | tf_op jit(solution)/shard_map/jit(_take)/gather | solution.py:27
  29.8 1.8 select_select_fusion.3
  31.7 0.0 all-reduce.5.cloned.1.call-update
  31.7 0.0 all-reduce.7.cloned.1.call-start
  31.8 0.1 compare_select_fusion.3
  31.8 54.1 %all-reduce.5.cloned.1.call-done = bf16[1024,1024]{1,0:T(8,128)(2,1)} async-done(((bf16[1024,1024]{1,0:T(8,128)(2,1)}), bf16[1024,1024]{1,0:T(8,128)(2,1)}) %all-reduce.5.cloned.1.call-update) | async-done | bytes 2097168 | tf_op jit(solution)/shard_map/psum | solution.py:62
  85.9 0.0 copy-start.4
  85.9 11.8 %scatter_fusion = bf16[2560,1024]{1,0:T(8,128)(2,1)} fusion(bf16[2560,1024]{1,0:T(8,128)(2,1)} %bitcast.43, s32[1024]{0:T(1024)S(1)} %bitcast.46, bf16[1024,1024]{1,0:T(8,128)(2,1)} %all-reduce.5.cloned.1.call-done), kind=kCustom, calls=%fused_computation.4 | custom fusion | bytes 6295552 | tf_op jit(solution)/shard_map/scatter | solution.py:35
  97.7 0.0 copy-done.4
  97.7 4.8 %fusion = bf16[2560,512]{1,0:T(8,128)(2,1)} fusion(bf16[2560,1024]{1,0:T(8,128)(2,1)} %scatter_fusion, pred[]{:T(512)S(6)} %eq.93, bf16[2,512,512]{2,1,0:T(8,128)(2,1)S(1)} %copy-done.4), kind=kOutput, calls=%fused_computation.14 | convolution fusion | flops 1344798720 | bytes 5767169 | tf_op jit(solution)/shard_map/dot_general | solution.py:68
  102.5 0.0 all-reduce.7.cloned.1.call-update
  102.5 0.0 copy-start.2
  102.5 0.2 all-reduce.9.cloned.1.call-start
  102.8 6.9 %gather_fusion.2 = s32[1024]{0:T(1024)S(1)} fusion(s32[512]{0:T(512)S(1)} %bitcast.33, s32[1024]{0:T(1024)S(1)} %get-tuple-element.63), kind=kCustom, calls=%fused_computation.2.clone | custom fusion | bytes 12288 | tf_op jit(solution)/shard_map/jit(_take)/gather | solution.py:15
  109.7 0.7 compare_reduce_fusion.2
  110.4 0.4 compare_reduce_fusion
  110.9 0.4 fusion.7
  111.4 0.0 copy-done.2
  111.4 1.8 convolution_convert_fusion.3
  113.2 105.4 %all-reduce.7.cloned.1.call-done = bf16[2560,512]{1,0:T(8,128)(2,1)} async-done(((bf16[2560,512]{1,0:T(8,128)(2,1)}), bf16[2560,512]{1,0:T(8,128)(2,1)}) %all-reduce.7.cloned.1.call-update) | async-done | bytes 2621456 | tf_op jit(solution)/shard_map/psum | solution.py:9
  218.6 10.0 %and_select_fusion = bf16[2560,1024]{1,0:T(8,128)(2,1)} fusion(bf16[2560,1024]{1,0:T(8,128)(2,1)} %scatter_fusion, bf16[2560,512]{1,0:T(8,128)(2,1)} %all-reduce.7.cloned.1.call-done, bf16[1024,512]{0,1:T(8,128)(2,1)S(1)} %convolution_convert_fusion.3, pred[1024]{0:T(1024)(128)(4,1)S(1)} %get-tuple-element.75, pred[2560]{0:T(1024)(128)(4,1)S(1)} %get-tuple-element.73), kind=kOutput, calls=%fused_computation.8 | convolution fusion | flops 2697461760 | bytes 14159360 | tf_op jit(solution)/shard_map/dot_general | solution.py:77
  228.6 2.6 fusion.10
  231.3 0.0 copy-done
  231.3 4.5 fusion.2
  235.7 8.1 %gather_fusion.3 = bf16[1024,1024]{1,0:T(8,128)(2,1)S(1)} fusion(bf16[2560,1024]{1,0:T(8,128)(2,1)} %fusion.2, s32[1024]{0:T(1024)S(1)} %broadcast_clamp_fusion), kind=kCustom, calls=%fused_computation.3.clone | custom fusion | bytes 4198400 | tf_op jit(solution)/shard_map/jit(_take)/gather | solution.py:27
  243.9 1.8 select_select_fusion.2
  245.7 0.0 all-reduce.9.cloned.1.call-update
  245.7 0.0 all-reduce.11.cloned.1.call-start
  245.8 0.1 compare_select_fusion.2
  245.9 50.5 %all-reduce.9.cloned.1.call-done = bf16[1024,1024]{1,0:T(8,128)(2,1)} async-done(((bf16[1024,1024]{1,0:T(8,128)(2,1)}), bf16[1024,1024]{1,0:T(8,128)(2,1)}) %all-reduce.9.cloned.1.call-update) | async-done | bytes 2097168 | tf_op jit(solution)/shard_map/psum | solution.py:62
  296.3 11.8 %scatter_fusion.1 = bf16[2560,1024]{1,0:T(8,128)(2,1)} fusion(bf16[2560,1024]{1,0:T(8,128)(2,1)} %fusion.2, s32[1024]{0:T(1024)S(1)} %bitcast.47, bf16[1024,1024]{1,0:T(8,128)(2,1)} %all-reduce.9.cloned.1.call-done), kind=kCustom, calls=%fused_computation.5 | custom fusion | bytes 6295552 | tf_op jit(solution)/shard_map/scatter | solution.py:35
  308.1 0.0 copy-done.5
  308.1 4.8 %fusion.1 = bf16[2560,512]{1,0:T(8,128)(2,1)} fusion(bf16[2560,1024]{1,0:T(8,128)(2,1)} %scatter_fusion.1, pred[]{:T(512)S(6)} %eq.100, bf16[2,512,512]{2,1,0:T(8,128)(2,1)S(1)} %copy-done.5), kind=kOutput, calls=%fused_computation.15 | convolution fusion | flops 1344798720 | bytes 5767169 | tf_op jit(solution)/shard_map/dot_general | solution.py:68
  312.9 0.0 all-reduce.11.cloned.1.call-update
  313.0 1.5 copy-done.3
  314.5 1.8 convolution_convert_fusion.2
  316.3 112.7 %all-reduce.11.cloned.1.call-done = bf16[2560,512]{1,0:T(8,128)(2,1)} async-done(((bf16[2560,512]{1,0:T(8,128)(2,1)}), bf16[2560,512]{1,0:T(8,128)(2,1)}) %all-reduce.11.cloned.1.call-update) | async-done | bytes 2621456 | tf_op jit(solution)/shard_map/psum | solution.py:9
  428.9 10.1 %and_select_fusion.1 = bf16[2560,1024]{1,0:T(8,128)(2,1)} fusion(bf16[2560,1024]{1,0:T(8,128)(2,1)} %scatter_fusion.1, bf16[2560,512]{1,0:T(8,128)(2,1)} %all-reduce.11.cloned.1.call-done, bf16[1024,512]{0,1:T(8,128)(2,1)S(1)} %convolution_convert_fusion.2, pred[1024]{0:T(1024)(128)(4,1)S(1)} %broadcast_compare_fusion.2, ...), kind=kOutput, calls=%fused_computation.9 | convolution fusion | flops 2697461760 | bytes 14159360 | tf_op jit(solution)/shard_map/dot_general | solution.py:77
  439.1 2.8 fusion.8
  441.9 0.0 copy-done.1
  441.9 4.5 fusion.3
  446.4 9.5 %reshape.673 = bf16[5,512,2,512]{3,2,1,0:T(2,128)(2,1)} reshape(bf16[2560,1024]{1,0:T(8,128)(2,1)} %fusion.3) | data formatting | bytes 10485760 | tf_op jit(solution)/shard_map/reshape | solution.py:88
  (20 shorter events, 0.2 us)
Async XLA Ops:
  6.5 79.4 %all-reduce.5.cloned.1.call-start = ((), (), s32[]{:S(2)}) async-start(), calls=%async_computation | async-start | bytes 4194304 | tf_op jit(solution)/shard_map/psum | solution.py:62
  31.7 186.9 %all-reduce.7.cloned.1.call-start = ((), (), s32[]{:S(2)}) async-start(), calls=%async_computation.1 | async-start | bytes 5242880 | tf_op jit(solution)/shard_map/psum | solution.py:9
  85.9 11.8 %copy-start.4 = (bf16[2,512,512]{2,1,0:T(8,128)(2,1)S(1)}, bf16[2,512,512]{2,1,0:T(8,128)(2,1)}, u32[]{:S(2)}) copy-start(bf16[2,512,512]{2,1,0:T(8,128)(2,1)} %param.19) | copy-start | bytes 3145732
  102.5 8.8 %copy-start.2 = (bf16[1024,1024]{1,0:T(8,128)(2,1)S(1)}, bf16[1024,1024]{1,0:T(8,128)(2,1)}, u32[]{:S(2)}) copy-start(bf16[1024,1024]{1,0:T(8,128)(2,1)} %all-reduce.5.cloned.1.call-done) | copy-start | bytes 6291460
  102.5 193.8 %all-reduce.9.cloned.1.call-start = ((), (), s32[]{:S(2)}) async-start(), calls=%async_computation.2 | async-start | bytes 4194304 | tf_op jit(solution)/shard_map/psum | solution.py:62
  228.6 2.7 copy-start
  245.7 183.2 %all-reduce.11.cloned.1.call-start = ((), (), s32[]{:S(2)}) async-start(), calls=%async_computation.3 | async-start | bytes 5242880 | tf_op jit(solution)/shard_map/psum | solution.py:9
  296.3 11.8 %copy-start.5 = (bf16[2,512,512]{2,1,0:T(8,128)(2,1)S(1)}, bf16[2,512,512]{2,1,0:T(8,128)(2,1)}, u32[]{:S(2)}) copy-start(bf16[2,512,512]{2,1,0:T(8,128)(2,1)} %param.19) | copy-start | bytes 3145732
  312.9 1.6 copy-start.3
  439.1 2.8 copy-start.1
Sparse Core Ops, SparseCore 0:
  31.8 54.0 all-reduce.4
  102.7 115.8 all-reduce.6
  245.9 50.4 all-reduce.8
  313.0 115.8 all-reduce.10
where the time goes:
time: 463 us; the launch traced here: 462 us
  waiting for transfers between devices  323 us (70%)
  local copies, waits for them, and re-layouts  71.9 us (16%)
  matrix products  33.3 us (7%)
  other arithmetic  20.9 us (5%)
  between operations  13.3 us (3%)
    psum x2, waiting for transfers between devices, from_root(): return lax.psum(kept, axis)  218 us
    psum x2, waiting for transfers between devices, body(): lax.psum(picked_rows.astype(jnp.float32).astype(jnp.bfloat16), 'prow')  105 us
    scatter x2, local copies, waits for them, and re-layouts, place_rows(): return local_tiles.at[position].set(values, mode='drop')  23.6 us
    dot_general x2, matrix products, body(): update = jnp.dot(factor, top_product, preferred_element_type=jnp.float32)  20.2 us
    gather x2, local copies, waits for them, and re-layouts, collect_rows(): picked = jnp.take(local_tiles, position, axis=0)  16.3 us
    gather x2, local copies, waits for them, and re-layouts, swap_source(): from_top = jnp.take(pivot_list, jnp.clip(offset, 0, block_width - 1))  13.8 us
    dot_general x2, matrix products, body(): jnp.dot(panel_cols, upper_inverse[panel_step], preferred_element_type=jnp...  9.56 us
    reshape x1, local copies, waits for them, and re-layouts, body(): return local_tiles.reshape(matrix.shape)  9.46 us
  transfers between devices with their start and end apart: 4, of which 4 were waited for; matrix products, arithmetic and copies ran while one was open for 3% of the time, Pallas kernels for 0%

commit v1 on v0

v1 whole, which is shorter than its diff:
```python
import functools

import jax
import jax.numpy as jnp
from jax import lax
from jax.experimental import pallas as pl
from jax.experimental.pallas import tpu as pltpu
from jax.sharding import PartitionSpec as P

BF16 = jnp.bfloat16
F32 = jnp.float32
VMEM_LIMIT = 48 * 1024 * 1024


def swapped(pivot_list, top_start, rows):
    tops = top_start + jnp.arange(pivot_list.shape[0], dtype=jnp.int32)
    at_top = (rows[:, None] == tops[None, :]).astype(jnp.int32)
    at_pivot = (rows[:, None] == pivot_list[None, :]).astype(jnp.int32)
    return rows + jnp.sum((at_top - at_pivot) * (pivot_list - tops)[None, :], axis=1)


def dot(a, b):
    return jnp.dot(a, b, preferred_element_type=F32)


def gather_kernel(keep_index, send_index, tiles, keep, send):
    def copy(i, carry):
        keep[i] = tiles[keep_index[i]]
        send[i] = tiles[send_index[i]]
        return carry

    lax.fori_loop(0, keep.shape[0], copy, 0, unroll=8)


def gather_rows(keep_index, send_index, tiles):
    count = keep_index.shape[0]
    shape = jax.ShapeDtypeStruct((count,) + tiles.shape[1:], tiles.dtype)
    smem = pl.BlockSpec(memory_space=pltpu.SMEM)
    vmem = pl.BlockSpec(memory_space=pltpu.VMEM)
    return pl.pallas_call(
        gather_kernel,
        out_shape=(shape, shape),
        in_specs=[smem, smem, vmem],
        out_specs=(vmem, vmem),
        compiler_params=pltpu.CompilerParams(vmem_limit_bytes=VMEM_LIMIT),
    )(keep_index, send_index, tiles)


def scatter_kernel(*refs):
    sources = (len(refs) - 2) // 2
    indices, values = refs[:sources], refs[sources : 2 * sources]
    tiles, out = refs[2 * sources], refs[2 * sources + 1]
    out[0 : tiles.shape[0]] = tiles[...]
    for index, value in zip(indices, values):

        def copy(i, carry, index=index, value=value):
            out[index[i]] = value[i]
            return carry

        lax.fori_loop(0, value.shape[0], copy, 0, unroll=8)


def scatter_rows(indices, values, tiles):
    smem = pl.BlockSpec(memory_space=pltpu.SMEM)
    vmem = pl.BlockSpec(memory_space=pltpu.VMEM)
    rows = tiles.shape[0] + 8
    return pl.pallas_call(
        scatter_kernel,
        out_shape=jax.ShapeDtypeStruct((rows,) + tiles.shape[1:], tiles.dtype),
        in_specs=[smem] * len(indices) + [vmem] * (len(values) + 1),
        out_specs=vmem,
        compiler_params=pltpu.CompilerParams(vmem_limit_bytes=VMEM_LIMIT),
    )(*indices, *values, tiles)


def prep_kernel(meta, first, second, head0, head1, lower, upper, up0, up1, up0_panel, top):
    half = first.shape[1]
    core, column = meta[1], meta[2]
    odd = lax.rem(column, 2) == 1

    def rows_of(block, j):
        wanted_first = odd if block == 0 else jnp.logical_not(odd)
        low_a, high_a = first[core, :, j, :], first[1 - core, :, j, :]
        low_b, high_b = second[core, :, j, :], second[1 - core, :, j, :]
        low = jnp.where(wanted_first, low_a.astype(F32), low_b.astype(F32))
        high = jnp.where(wanted_first, high_a.astype(F32), high_b.astype(F32))
        return jnp.concatenate([low, high], axis=0)

    nb = 2 * half
    cb = first.shape[2]
    up0_panel[...] = dot(lower[0], head0[...]).astype(BF16)
    factor = dot(head1[...], upper[0]).astype(BF16)
    for j in range(cb):
        cols = slice(j * nb, (j + 1) * nb)
        old = rows_of(0, j)
        product = dot(lower[0], old.astype(BF16))
        in_panel = (column == 0) if j == 0 else False
        next_panel = (column == 1) if j == 0 else False
        if j == 0:
            top[0:nb, j, :] = jnp.where(in_panel, old, product).astype(BF16)
            product = jnp.where(in_panel, 0.0, product)
        else:
            top[0:nb, j, :] = product.astype(BF16)
        product = product.astype(BF16)
        up0[:, cols] = product
        updated = (rows_of(1, j) - dot(factor, product)).astype(BF16)
        last = dot(lower[1], updated)
        if j == 0:
            kept = jnp.where(next_panel, updated.astype(F32), last)
            kept = jnp.where(in_panel, factor.astype(F32), kept)
            top[nb : 2 * nb, j, :] = kept.astype(BF16)
            last = jnp.where(jnp.logical_or(in_panel, next_panel), 0.0, last)
        else:
            top[nb : 2 * nb, j, :] = last.astype(BF16)
        up1[:, cols] = last.astype(BF16)


def prep(meta, first, second, head0, head1, lower, upper):
    _, half, cb, nb = first.shape
    smem = pl.BlockSpec(memory_space=pltpu.SMEM)
    vmem = pl.BlockSpec(memory_space=pltpu.VMEM)
    return pl.pallas_call(
        prep_kernel,
        out_shape=(
            jax.ShapeDtypeStruct((nb, cb * nb), BF16),
            jax.ShapeDtypeStruct((nb, cb * nb), BF16),
            jax.ShapeDtypeStruct((nb, nb), BF16),
            jax.ShapeDtypeStruct((2 * nb, cb, nb), BF16),
        ),
        in_specs=[smem] + [vmem] * 6,
        out_specs=(vmem,) * 4,
        compiler_params=pltpu.CompilerParams(vmem_limit_bytes=VMEM_LIMIT),
    )(meta, first, second, head0, head1, lower, upper)


def update_kernel(
    per_block, meta, position, panel0, panel1, tiles, old_mine, old_sibling, upper,
    up0, up1, up0_panel, top, out,
):
    row, column, row_devices = meta[0], meta[2], meta[3]
    step = pl.program_id(0)
    chunk, cb, nb = out.shape
    block = step // per_block * row_devices + row

    @pl.when(block < 2)
    def _():
        begin = block * nb + lax.rem(step, per_block) * chunk
        out[...] = top[pl.ds(begin, chunk)]

    @pl.when(block >= 2)
    def _():
        place = position[...]
        moved = place >= 0
        slots = lax.broadcasted_iota(jnp.int32, (chunk, 2 * nb), 1)
        pick = jnp.where(slots == place, 1.0, 0.0).astype(BF16)
        fixed = []
        for k, panel in enumerate((panel0, panel1)):
            brought = dot(pick[:, :nb], old_mine[k]) + dot(pick[:, nb:], old_sibling[k])
            fixed.append(jnp.where(moved, brought, panel[0, 0].astype(F32)))
        factor0 = dot(fixed[0].astype(BF16), upper[0]).astype(BF16)
        below = (fixed[1] - dot(factor0, up0_panel[...])).astype(BF16)
        factor1 = dot(below, upper[1]).astype(BF16)
        for j in range(cb):
            cols = slice(j * nb, (j + 1) * nb)
            value = tiles[:, j, :].astype(F32) - dot(factor0, up0[:, cols])
            value = value.astype(BF16).astype(F32) - dot(factor1, up1[:, cols])
            if j == 0:
                value = jnp.where(column == 0, factor0.astype(F32), value)
                value = jnp.where(column == 1, factor1.astype(F32), value)
            out[:, j, :] = value.astype(BF16)


def update(meta, position, panels, skip, tiles, old_mine, old_sibling, upper, up0, up1, up0_panel, top, rows):
    chunk, nb = panels.shape[2:]
    cb = tiles.shape[1]
    whole = lambda a: pl.BlockSpec(a.shape, lambda s: (0,) * a.ndim)
    return pl.pallas_call(
        functools.partial(update_kernel, nb // chunk),
        grid=(rows // chunk,),
        out_shape=jax.ShapeDtypeStruct((rows, cb, nb), BF16),
        in_specs=[
            pl.BlockSpec(memory_space=pltpu.SMEM),
            pl.BlockSpec((chunk, 1), lambda s: (s, 0)),
            pl.BlockSpec((1, 1, chunk, nb), lambda s: (0, s + skip, 0, 0)),
            pl.BlockSpec((1, 1, chunk, nb), lambda s: (1, s + skip, 0, 0)),
            pl.BlockSpec((chunk, cb, nb), lambda s: (s, 0, 0)),
            whole(old_mine), whole(old_sibling), whole(upper), whole(up0), whole(up1), whole(up0_panel), whole(top),
        ],
        out_specs=pl.BlockSpec((chunk, cb, nb), lambda s: (s, 0, 0)),
        compiler_params=pltpu.CompilerParams(vmem_limit_bytes=VMEM_LIMIT),
    )(meta, position, panels, panels, tiles, old_mine, old_sibling, upper, up0, up1, up0_panel, top)


def body(matrix, pivots, lower_inverse, upper_inverse):
    rb, nb, cb, _ = matrix.shape
    rows = rb * nb
    row_devices = lax.axis_size("prow")
    col_devices = lax.axis_size("pcol")
    chips = row_devices // 2
    line = col_devices // 2
    row = lax.axis_index("prow").astype(jnp.int32)
    column = lax.axis_index("pcol").astype(jnp.int32)
    core, chip = row % 2, row // 2
    place_in_line, side = column // 2, column % 2
    meta = jnp.stack([row, core, column, jnp.int32(row_devices)])
    tiles = matrix.reshape(rows, cb, nb)

    sibling = [(r, r ^ 1) for r in range(row_devices)]
    neighbour = [(c, c ^ 1) for c in range(col_devices)]
    onward = [(c, c + 2) for c in range(col_devices - 2)]

    chunk = nb // 2
    per_block = nb // chunk
    pieces = rows // chunk
    skip = line - 1
    panels = jnp.zeros((2, pieces + 2 * skip, chunk, nb), BF16)
    held = tiles[0:chunk, 0, :]
    after_block = None
    for step in range(pieces + line - 1):
        if step:
            held = lax.ppermute(held, "pcol", onward)
            if step < pieces:
                own = tiles[step * chunk : (step + 1) * chunk, 0, :]
                held = jnp.where(place_in_line == 0, own, held)
        other = lax.ppermute(held, "pcol", neighbour)
        slot = step - place_in_line + skip
        panels = lax.dynamic_update_slice(panels, held[None, None], (side, slot, 0, 0))
        panels = lax.dynamic_update_slice(panels, other[None, None], (1 - side, slot, 0, 0))
        if step == per_block - 1 + skip:
            after_block = panels[:, skip : skip + per_block].reshape(2, nb, nb)

    old_mine = after_block
    for hop in range(1, chips):
        came = lax.ppermute(after_block, "prow", [(0, 2 * hop), (1, 2 * hop + 1)])
        old_mine = jnp.where(chip == hop, came, old_mine)
    old_sibling = lax.ppermute(old_mine, "prow", sibling)

    def source_of(index):
        return swapped(pivots[0], 0, swapped(pivots[1], nb, index))

    def target_of(index):
        return swapped(pivots[1], nb, swapped(pivots[0], 0, index))

    def holder(index):
        return index // nb % row_devices

    def local(index):
        return index // (nb * row_devices) * nb + index % nb

    def placed(index, valid):
        mine = valid & (holder(index) == row) & (index >= 2 * nb)
        return jnp.where(mine, local(index), rows)

    half = nb // 2
    indices, values = [], []
    new_top = []
    head = None
    for turn in range(2):
        begin = jnp.where((side == 0) == (turn == 0), nb, 0)
        kept_slots = begin + core * half + jnp.arange(half, dtype=jnp.int32)
        sent_slots = begin + (1 - core) * half + jnp.arange(half, dtype=jnp.int32)
        source_all = source_of(jnp.concatenate([kept_slots, sent_slots]))
        source_kept, source_sent = source_all[:half], source_all[half:]
        second_all = source_of(source_all)
        on_chip = holder(source_all) // 2 == chip
        wanted = jnp.where(on_chip, source_all, second_all)
        here = local(wanted)
        keep, send = gather_rows(here[:half], here[half:], tiles)
        from_sibling = lax.ppermute(send, "prow", sibling)
        is_mine = (holder(wanted[:half]) == row)[:, None, None]
        joined = jnp.where(is_mine, keep, from_sibling)
        top_here, brought = joined, None
        for hop in range(1, chips):
            came = lax.ppermute(
                joined, "prow", [(r, (r + 2 * hop) % row_devices) for r in range(row_devices)]
            )
            from_chip = (chip - hop) % chips
            theirs = (holder(source_kept) // 2 == from_chip)[:, None, None]
            top_here = jnp.where(theirs, came, top_here)
            brought = came if brought is None else jnp.where(from_chip == 0, came, brought)
        if brought is None:
            brought = joined
        both = jnp.stack([top_here, brought])
        theirs = lax.ppermute(both, "prow", sibling)
        new_top.append(jnp.stack([top_here, theirs[0]]))
        away = chip != 0
        for value, source in ((brought, source_kept), (theirs[1], source_sent)):
            indices.append(placed(source, away))
            values.append(value)
        if turn == 0:
            part = nb // row_devices
            full = jnp.concatenate([top_here[:, 0, :], theirs[0][:, 0, :]])
            at = (row * part + core * half) % nb
            head = lax.dynamic_slice(full, (at, 0), (part, nb))

    block0 = tiles[:nb]
    sibling_block0 = lax.ppermute(block0, "prow", sibling)
    tops = jnp.arange(nb, dtype=jnp.int32)
    for value, first_row in ((block0, core * nb), (sibling_block0, (1 - core) * nb)):
        indices.append(placed(target_of(first_row + tops), chip == 0))
        values.append(value)
    moved_tiles = scatter_rows(indices, values, tiles)

    for _ in range(line - 1):
        head = jnp.where(place_in_line == 0, head, lax.ppermute(head, "pcol", onward))
    head_other = lax.ppermute(head, "pcol", neighbour)
    head = jnp.where(side == 1, jnp.stack([head, head_other]), jnp.stack([head_other, head]))
    heads = jnp.zeros((2, row_devices) + head.shape[1:], BF16)
    around = [(chip, head)]
    for hop in range(1, chips):
        came = lax.ppermute(head, "prow", [(r, (r + 2 * hop) % row_devices) for r in range(row_devices)])
        around.append(((chip - hop) % chips, came))
    for at, piece in around:
        heads = lax.dynamic_update_slice(heads, piece[:, None], (0, 2 * at + core, 0, 0))
    packed = jnp.stack([piece for _, piece in around])
    packed = lax.ppermute(packed, "prow", sibling)
    for i, (at, _) in enumerate(around):
        heads = lax.dynamic_update_slice(heads, packed[i][:, None], (0, 2 * at + 1 - core, 0, 0))
    heads = heads.reshape(2, nb, nb)

    up0, up1, up0_panel, top = prep(meta, new_top[0], new_top[1], heads[0], heads[1], lower_inverse, upper_inverse)

    slot = jnp.arange(rows, dtype=jnp.int32)
    mine = (slot // nb * row_devices + row) * nb + slot % nb
    source = source_of(mine)
    same_core = source // nb == core
    position = jnp.where(same_core, source % nb, nb + source % nb)
    position = jnp.where((source < 2 * nb) & (mine >= 2 * nb), position, -1)
    result = update(
        meta, position[:, None], panels, skip, moved_tiles, old_mine, old_sibling, upper_inverse,
        up0, up1, up0_panel, top, rows,
    )
    return result.reshape(matrix.shape)


def solution(mesh):
    placed = (P(None, "prow", None, "pcol"), P(), P(), P())
    return jax.shard_map(
        body, mesh=mesh, in_specs=placed, out_specs=P(None, "prow", None, "pcol"), check_vma=False
    )
```

time: 463 us -> 243 us (0.52)
  waiting for transfers between devices: 323 us -> 22.4 us
  starting transfers between devices: 0.31 us -> 80 us
  Pallas kernels: 0 us -> 47.1 us
  matrix products: 33.3 us -> 0 us
  local copies, waits for them, and re-layouts: 71.9 us -> 46.8 us
  other arithmetic: 20.9 us -> 43.2 us
  between operations: 13.3 us -> 0.91 us
    psum x4 -> x0, waiting for transfers between devices: 323 us -> none  [the longest x2 218 us: from_root(): return lax.psum(kept, axis)]
    ppermute x0 -> x40, starting transfers between devices: none -> 80 us  [the longest x12 49.5 us: body(): held = lax.ppermute(held, 'pcol', onward)]
    pallas_call x0 -> x5, Pallas kernels: none -> 47.1 us  [the longest x1 23 us: update(): pl.pallas_call(functools.partial(update_kernel, nb // chunk), grid=(rows...]
    dot_general x6 -> x0, matrix products: 33.3 us -> none  [the longest x2 20.2 us: body(): update = jnp.dot(factor, top_product, preferred_element_type=jnp.float32)]
    gather x4 -> x0, local copies, waits for them, and re-layouts: 30 us -> none  [the longest x2 16.3 us: collect_rows(): picked = jnp.take(local_tiles, position, axis=0)]
    scatter x2 -> x0, local copies, waits for them, and re-layouts: 23.6 us -> none  [place_rows(): return local_tiles.at[position].set(values, mode='drop')]
    ppermute x0 -> x40, waiting for transfers between devices: none -> 22.4 us  [the longest x13 10.9 us: body(): other = lax.ppermute(held, 'pcol', neighbour)]
    dynamic_update_slice x0 -> x10, other arithmetic: none -> 15.7 us  [the longest x9 15.7 us: body(): lax.dynamic_update_slice(panels, held[None, None], (side, slot, 0, 0))]
  transfers between devices with their start and end apart: 4 -> 40, of which waited for: 4 -> 11; matrix products, arithmetic and copies ran while one was open for 3% -> 33% of each run, Pallas kernels for 0% -> 10%
where the time goes in v1:
time: 243 us; the launch traced here: 240 us
  starting transfers between devices  80 us (33%)
  Pallas kernels  47.1 us (19%)
  local copies, waits for them, and re-layouts  46.8 us (19%)
  other arithmetic  43.2 us (18%)
  waiting for transfers between devices  22.4 us (9%)
    ppermute x12, starting transfers between devices, body(): held = lax.ppermute(held, 'pcol', onward)  49.5 us
    pallas_call x1, Pallas kernels, update(): pl.pallas_call(functools.partial(update_kernel, nb // chunk), grid=(rows...  23 us
    dynamic_update_slice x9, other arithmetic, body(): lax.dynamic_update_slice(panels, held[None, None], (side, slot, 0, 0))  15.7 us
    ppermute x13, starting transfers between devices, body(): other = lax.ppermute(held, 'pcol', neighbour)  14 us
    dynamic_update_slice x13, local copies, waits for them, and re-layouts, body(): lax.dynamic_update_slice(panels, other[None, None], (1 - side, slot, 0, 0))  12.4 us
    ppermute x13, waiting for transfers between devices, body(): other = lax.ppermute(held, 'pcol', neighbour)  10.9 us
    reshape x1, local copies, waits for them, and re-layouts, body(): tiles = matrix.reshape(rows, cb, nb)  10.8 us
    unnamed x21, local copies, waits for them, and re-layouts  10.3 us
  transfers between devices with their start and end apart: 40, of which 11 were waited for; matrix products, arithmetic and copies ran while one was open for 33% of the time, Pallas kernels for 10%

profile of v1, /device:TPU:0, one launch (start us, length us, event | category | flops | bytes accessed | tf_op | source)
XLA Modules:
  0.0 240.4 jit_solution(14952274967198369848)
XLA Ops:
  0.0 3.4 %copy.38 = bf16[5,512,2,512]{3,1,0,2:T(8,128)(2,1)S(1)} copy(bf16[5,512,2,512]{3,2,1,0:T(2,128)(2,1)} %param.4) | data formatting | bytes 10485760 | tf_op args[0]
  3.4 2.3 copy-done.2
  6.5 3.0 %collective-permute-start = (bf16[256,512]{1,0:T(8,128)(2,1)}, bf16[256,512]{1,0:T(8,128)(2,1)}, u32[]{:S(2)}, u32[]{:S(2)}) collective-permute-start(bf16[256,512]{1,0:T(8,128)(2,1)} %slice_bitcast_fusion.14), channel_id=1, source_target_pairs={{0,1},{1,0},{2,3},{3,2},{4,5},{5,4},{6,7},{7,6},{8,9},{9,8},{10,11... | collective-permute-start | bytes 786440 | tf_op jit(solution)/shard_map/ppermute | solution.py:225
  9.5 3.5 %collective-permute-start.1 = (bf16[256,512]{1,0:T(8,128)(2,1)}, bf16[256,512]{1,0:T(8,128)(2,1)S(1)}, u32[]{:S(2)}, u32[]{:S(2)}) collective-permute-start(bf16[256,512]{1,0:T(8,128)(2,1)} %slice_bitcast_fusion.14), channel_id=1, source_target_pairs={{0,2},{1,3},{2,4},{3,5},{4,6},{5,7},{8,10},{9,11},{10,12},{11,13},... | collective-permute-start | bytes 786440 | tf_op jit(solution)/shard_map/ppermute | solution.py:221
  13.1 10.8 %copy.39.tiles.refs_12_ = bf16[2560,2,512]{2,1,0:T(2,128)(2,1)} copy(bf16[2560,2,512]{2,0,1:T(8,128)(2,1)} %bitcast.159) | data formatting | bytes 10485760 | tf_op jit(solution)/shard_map/reshape | solution.py:206
  28.2 3.9 %shard_map.46 = (bf16[256,2,512]{2,1,0:T(2,128)(2,1)S(1)}, bf16[256,2,512]{2,1,0:T(2,128)(2,1)}) custom-call(s32[256]{0:T(256)S(1)} %get-tuple-element.73.keep_index, s32[256]{0:T(256)S(1)} %get-tuple-element.72.send_index, bf16[2560,2,512]{2,1,0:T(2,128)(2,1)} %copy.39.tiles.refs_12_), custom_call_target="tpu_custom_call" | custom-call | tf_op jit(solution)/shard_map/pallas_call | solution.py:40
  32.1 4.0 %shard_map.47 = (bf16[256,2,512]{2,1,0:T(2,128)(2,1)S(1)}, bf16[256,2,512]{2,1,0:T(2,128)(2,1)}) custom-call(s32[256]{0:T(256)S(1)} %get-tuple-element.71.keep_index, s32[256]{0:T(256)S(1)} %get-tuple-element.70.send_index, bf16[2560,2,512]{2,1,0:T(2,128)(2,1)} %copy.39.tiles.refs_12_), custom_call_target="tpu_custom_call" | custom-call | tf_op jit(solution)/shard_map/pallas_call | solution.py:40
  36.5 1.9 slice_bitcast_fusion.refs_10_
  38.6 2.1 multiply_reduce_fusion.1
  40.7 2.2 multiply_reduce_fusion
  43.0 3.9 %fusion.11.position = s32[2560,1]{1,0:T(8,128)} fusion(s32[2560]{0:T(1024)S(1)} %multiply_reduce_fusion, s32[2560]{0:T(1024)S(1)} %multiply_reduce_fusion.1, s32[]{:T(128)} %select_n.504, s32[]{:T(128)} %axis_index.23), kind=kLoop, calls=%fused_computation.24 | loop fusion | flops 112640 | bytes 30728 | tf_op jit(solution)/shard_map/jit(_where)/select_n | solution.py:328
  48.8 3.3 %copy-done.1 = bf16[2,16,256,512]{3,2,1,0:T(8,128)(2,1)} copy-done((bf16[2,16,256,512]{3,2,1,0:T(8,128)(2,1)}, bf16[2,16,256,512]{3,2,1,0:T(8,128)(2,1)S(1)}, u32[]{:S(2)}) %copy-start.1) | copy-done | bytes 8388632
  53.9 1.8 bitcast_dynamic-update-slice_fusion.24
  56.2 4.2 %collective-permute-start.3 = (bf16[256,512]{1,0:T(8,128)(2,1)}, bf16[256,512]{1,0:T(8,128)(2,1)}, u32[]{:S(2)}, u32[]{:S(2)}) collective-permute-start(bf16[256,512]{1,0:T(8,128)(2,1)} %get-tuple-element.58), channel_id=1, source_target_pairs={{0,2},{1,3},{2,4},{3,5},{4,6},{5,7},{8,10},{9,11},{10,12},{11,13},... | collective-permute-start | bytes 786440 | tf_op jit(solution)/shard_map/ppermute | solution.py:221
  60.5 4.1 %collective-permute-done.2 = bf16[256,512]{1,0:T(8,128)(2,1)S(1)} collective-permute-done((bf16[256,512]{1,0:T(8,128)(2,1)}, bf16[256,512]{1,0:T(8,128)(2,1)S(1)}, u32[]{:S(2)}, u32[]{:S(2)}) %collective-permute-start.2) | collective-permute-done | bytes 262176 | tf_op jit(solution)/shard_map/ppermute | solution.py:225
  69.2 5.2 %collective-permute-start.5 = (bf16[256,512]{1,0:T(8,128)(2,1)S(1)}, bf16[256,512]{1,0:T(8,128)(2,1)}, u32[]{:S(2)}, u32[]{:S(2)}) collective-permute-start(bf16[256,512]{1,0:T(8,128)(2,1)S(1)} %get-tuple-element.56), channel_id=1, source_target_pairs={{0,2},{1,3},{2,4},{3,5},{4,6},{5,7},{8,10},{9,11},{10,12},{11,13},... | collective-permute-start | bytes 786440 | tf_op jit(solution)/shard_map/ppermute | solution.py:221
  78.5 1.7 bitcast_dynamic-update-slice_fusion.20
  80.7 4.6 %collective-permute-start.7 = (bf16[256,512]{1,0:T(8,128)(2,1)S(1)}, bf16[256,512]{1,0:T(8,128)(2,1)S(1)}, u32[]{:S(2)}, u32[]{:S(2)}) collective-permute-start(bf16[256,512]{1,0:T(8,128)(2,1)S(1)} %get-tuple-element.54), channel_id=1, source_target_pairs={{0,2},{1,3},{2,4},{3,5},{4,6},{5,7},{8,10},{9,11},{10,12},{11,13},... | collective-permute-start | bytes 786440 | tf_op jit(solution)/shard_map/ppermute | solution.py:221
  85.3 2.1 broadcast_select_fusion.3
  89.7 1.7 bitcast_dynamic-update-slice_fusion.18
  92.9 4.0 %collective-permute-start.9 = (bf16[256,512]{1,0:T(8,128)(2,1)S(1)}, bf16[256,512]{1,0:T(8,128)(2,1)S(1)}, u32[]{:S(2)}, u32[]{:S(2)}) collective-permute-start(bf16[256,512]{1,0:T(8,128)(2,1)S(1)} %get-tuple-element.52), channel_id=1, source_target_pairs={{0,2},{1,3},{2,4},{3,5},{4,6},{5,7},{8,10},{9,11},{10,12},{11,13},... | collective-permute-start | bytes 786440 | tf_op jit(solution)/shard_map/ppermute | solution.py:221
  97.0 2.1 broadcast_select_fusion.1
  101.3 2.3 slice.167
  103.6 1.7 bitcast_dynamic-update-slice_fusion.16
  107.0 3.4 %collective-permute-start.11 = (bf16[256,512]{1,0:T(8,128)(2,1)S(1)}, bf16[256,512]{1,0:T(8,128)(2,1)S(1)}, u32[]{:S(2)}, u32[]{:S(2)}) collective-permute-start(bf16[256,512]{1,0:T(8,128)(2,1)S(1)} %get-tuple-element.50), channel_id=1, source_target_pairs={{0,2},{1,3},{2,4},{3,5},{4,6},{5,7},{8,10},{9,11},{10,12},{11,13},... | collective-permute-start | bytes 786440 | tf_op jit(solution)/shard_map/ppermute | solution.py:221
  110.5 2.6 %pad_maximum_fusion = bf16[2,256,2,512]{3,2,1,0:T(2,128)(2,1)} fusion(bf16[1,256,2,512]{3,2,1,0:T(2,128)(2,1)S(1)} %bitcast.154, bf16[1,256,2,512]{3,2,1,0:T(2,128)(2,1)S(1)} %bitcast.170), kind=kLoop, calls=%fused_computation.31 | loop fusion | flops 524288 | bytes 2097152 | tf_op jit(solution)/shard_map/stack | solution.py:283
  114.3 1.7 bitcast_dynamic-update-slice_fusion.14
  117.6 4.4 %collective-permute-start.13 = (bf16[256,512]{1,0:T(8,128)(2,1)S(1)}, bf16[256,512]{1,0:T(8,128)(2,1)S(1)}, u32[]{:S(2)}, u32[]{:S(2)}) collective-permute-start(bf16[256,512]{1,0:T(8,128)(2,1)S(1)} %get-tuple-element.48), channel_id=1, source_target_pairs={{0,2},{1,3},{2,4},{3,5},{4,6},{5,7},{8,10},{9,11},{10,12},{11,13},... | collective-permute-start | bytes 786440 | tf_op jit(solution)/shard_map/ppermute | solution.py:221
  128.2 2.5 %pad_maximum_fusion.1 = bf16[2,256,2,512]{3,2,1,0:T(2,128)(2,1)} fusion(bf16[1,256,2,512]{3,2,1,0:T(2,128)(2,1)S(1)} %bitcast.155, bf16[1,256,2,512]{3,2,1,0:T(2,128)(2,1)S(1)} %fusion.15), kind=kLoop, calls=%fused_computation.32 | loop fusion | flops 524288 | bytes 2097152 | tf_op jit(solution)/shard_map/stack | solution.py:283
  130.7 4.9 %collective-permute-start.15 = (bf16[256,512]{1,0:T(8,128)(2,1)S(1)}, bf16[256,512]{1,0:T(8,128)(2,1)}, u32[]{:S(2)}, u32[]{:S(2)}) collective-permute-start(bf16[256,512]{1,0:T(8,128)(2,1)S(1)} %get-tuple-element.46), channel_id=1, source_target_pairs={{0,2},{1,3},{2,4},{3,5},{4,6},{5,7},{8,10},{9,11},{10,12},{11,13},... | collective-permute-start | bytes 786440 | tf_op jit(solution)/shard_map/ppermute | solution.py:221
  137.0 2.6 %collective-permute-start.32 = (bf16[2,512,512]{2,1,0:T(8,128)(2,1)}, bf16[2,512,512]{2,1,0:T(8,128)(2,1)S(1)}, u32[]{:S(2)}, u32[]{:S(2)}) collective-permute-start(bf16[2,512,512]{2,1,0:T(8,128)(2,1)} %bitcast.173), channel_id=1, source_target_pairs={{0,16},{8,24},{1,17},{9,25},{2,18},{10,26},{3,19},{11,27},{4,20},{... | collective-permute-start | bytes 3145736 | tf_op jit(solution)/shard_map/ppermute | solution.py:234
  141.3 1.7 bitcast_dynamic-update-slice_fusion.10
  144.5 4.6 %collective-permute-start.17 = (bf16[256,512]{1,0:T(8,128)(2,1)S(1)}, bf16[256,512]{1,0:T(8,128)(2,1)S(1)}, u32[]{:S(2)}, u32[]{:S(2)}) collective-permute-start(bf16[256,512]{1,0:T(8,128)(2,1)S(1)} %get-tuple-element.44), channel_id=1, source_target_pairs={{0,2},{1,3},{2,4},{3,5},{4,6},{5,7},{8,10},{9,11},{10,12},{11,13},... | collective-permute-start | bytes 786440 | tf_op jit(solution)/shard_map/ppermute | solution.py:221
  149.0 2.1 slice_bitcast_fusion.15
  152.9 2.8 %collective-permute-start.34 = (bf16[128,512]{1,0:T(8,128)(2,1)S(1)}, bf16[128,512]{1,0:T(8,128)(2,1)S(1)}, u32[]{:S(2)}, u32[]{:S(2)}) collective-permute-start(bf16[128,512]{1,0:T(8,128)(2,1)S(1)} %fusion.28), channel_id=1, source_target_pairs={{0,2},{1,3},{2,4},{3,5},{4,6},{5,7},{8,10},{9,11},{10,12},{11,13},... | collective-permute-start | bytes 393224 | tf_op jit(solution)/shard_map/ppermute | solution.py:305
  155.6 1.9 fusion.107
  159.1 8.8 %shard_map.48.tiles = bf16[2568,2,512]{2,1,0:T(2,128)(2,1)} custom-call(s32[256]{0:T(256)S(1)} %get-tuple-element.82.refs_0_, s32[256]{0:T(256)S(1)} %get-tuple-element.83.refs_1_, s32[256]{0:T(256)S(1)} %get-tuple-element.75.refs_2_, s32[256]{0:T(256)S(1)} %get-tuple-element.74.refs_3_, s32[512]{0:T(512)S(1)} %get-tuple-element.78.refs_4_, ...), custom_call_target="tpu_custom_call" | custom-call | tf_op jit(solution)/shard_map/pallas_call | solution.py:67
  168.0 2.2 collective-permute-start.35
  173.1 1.9 collective-permute-start.19
  175.1 2.0 collective-permute-start.36
  177.3 4.9 %collective-permute-done.36 = bf16[128,512]{1,0:T(8,128)(2,1)S(1)} collective-permute-done((bf16[128,512]{1,0:T(8,128)(2,1)S(1)}, bf16[128,512]{1,0:T(8,128)(2,1)S(1)}, u32[]{:S(2)}, u32[]{:S(2)}) %collective-permute-start.36) | collective-permute-done | bytes 131104 | tf_op jit(solution)/shard_map/ppermute | solution.py:305
  182.2 1.8 collective-permute-start.37
  184.3 4.4 %collective-permute-start.21 = (bf16[256,512]{1,0:T(8,128)(2,1)S(1)}, bf16[256,512]{1,0:T(8,128)(2,1)S(1)}, u32[]{:S(2)}, u32[]{:S(2)}) collective-permute-start(bf16[256,512]{1,0:T(8,128)(2,1)S(1)} %collective-permute-done.19), channel_id=1, source_target_pairs={{0,2},{1,3},{2,4},{3,5},{4,6},{5,7},{8,10},{9,11},{10,12},{11,13},... | collective-permute-start | bytes 786440 | tf_op jit(solution)/shard_map/ppermute | solution.py:221
  194.3 4.4 %collective-permute-start.23 = (bf16[256,512]{1,0:T(8,128)(2,1)S(1)}, bf16[256,512]{1,0:T(8,128)(2,1)S(1)}, u32[]{:S(2)}, u32[]{:S(2)}) collective-permute-start(bf16[256,512]{1,0:T(8,128)(2,1)S(1)} %collective-permute-done.21), channel_id=1, source_target_pairs={{0,2},{1,3},{2,4},{3,5},{4,6},{5,7},{8,10},{9,11},{10,12},{11,13},... | collective-permute-start | bytes 786440 | tf_op jit(solution)/shard_map/ppermute | solution.py:221
  200.3 2.2 collective-permute-done.23
  204.3 4.8 %collective-permute-done.24 = bf16[256,512]{1,0:T(8,128)(2,1)S(1)} collective-permute-done((bf16[256,512]{1,0:T(8,128)(2,1)S(1)}, bf16[256,512]{1,0:T(8,128)(2,1)S(1)}, u32[]{:S(2)}, u32[]{:S(2)}) %collective-permute-start.24) | collective-permute-done | bytes 262176 | tf_op jit(solution)/shard_map/ppermute | solution.py:225
  210.0 7.4 %shard_map.49 = (bf16[512,1024]{1,0:T(8,128)(2,1)S(1)}, bf16[512,1024]{1,0:T(8,128)(2,1)S(1)}, bf16[512,512]{1,0:T(8,128)(2,1)S(1)}, bf16[1024,2,512]{2,1,0:T(2,128)(2,1)}) custom-call(s32[4]{0:T(128)S(1)} %pad_add_fusion.2.meta, bf16[2,256,2,512]{3,2,1,0:T(2,128)(2,1)S(1)} %pad_maximum_fusion.2.first, ...), custom_call_target="tpu_custom_call" | custom-call | tf_op jit(solution)/shard_map/pallas_call | solution.py:122
  217.4 23.0 %shard_map.50 = bf16[2560,2,512]{2,1,0:T(2,128)(2,1)} custom-call(s32[4]{0:T(128)S(1)} %pad_add_fusion.2.meta, s32[2560,1]{1,0:T(8,128)} %fusion.11.position, bf16[2,16,256,512]{3,2,1,0:T(8,128)(2,1)} %bitcast_dynamic-update-slice_fusion.1.panel0.panel1, bf16[2,16,256,512]{3,2,1,0:T(8,128)(2,1)} %bitcast_dynamic-update-slice_fusion.1.panel0.panel1, ...), custom_call_target="tpu_custom_call" | custom-call | tf_op jit(solution)/shard_map/pallas_call | solution.py:177
  (150 shorter events, 56.6 us)
Async XLA Ops:
  6.5 45.6 %collective-permute-start = (bf16[256,512]{1,0:T(8,128)(2,1)}, bf16[256,512]{1,0:T(8,128)(2,1)}, u32[]{:S(2)}, u32[]{:S(2)}) collective-permute-start(bf16[256,512]{1,0:T(8,128)(2,1)} %slice_bitcast_fusion.14), channel_id=1, source_target_pairs={{0,1},{1,0},{2,3},{3,2},{4,5},{5,4},{6,7},{7,6},{8,9},{9,8},{10,11... | collective-permute-start | bytes 786440 | tf_op jit(solution)/shard_map/ppermute | solution.py:225
  9.5 44.4 %collective-permute-start.1 = (bf16[256,512]{1,0:T(8,128)(2,1)}, bf16[256,512]{1,0:T(8,128)(2,1)S(1)}, u32[]{:S(2)}, u32[]{:S(2)}) collective-permute-start(bf16[256,512]{1,0:T(8,128)(2,1)} %slice_bitcast_fusion.14), channel_id=1, source_target_pairs={{0,2},{1,3},{2,4},{3,5},{4,6},{5,7},{8,10},{9,11},{10,12},{11,13},... | collective-permute-start | bytes 786440 | tf_op jit(solution)/shard_map/ppermute | solution.py:221
  13.1 10.8 %copy-start.8 = (s32[2,512]{1,0:T(2,128)S(1)}, s32[2,512]{1,0:T(2,128)}, u32[]{:S(2)}) copy-start(s32[2,512]{1,0:T(2,128)} %param.5) | copy-start | bytes 12292
  32.1 53.2 %collective-permute-start.25 = (bf16[256,2,512]{2,1,0:T(2,128)(2,1)}, bf16[256,2,512]{2,1,0:T(2,128)(2,1)}, u32[]{:S(2)}, u32[]{:S(2)}) collective-permute-start(bf16[256,2,512]{2,1,0:T(2,128)(2,1)} %get-tuple-element.14), channel_id=1, source_target_pairs={{0,8},{8,0},{16,24},{24,16},{1,9},{9,1},{17,25},{25,17},{2,10},{10... | collective-permute-start | bytes 1572872 | tf_op jit(solution)/shard_map/ppermute | solution.py:269
  36.0 60.9 %collective-permute-start.28 = (bf16[256,2,512]{2,1,0:T(2,128)(2,1)}, bf16[256,2,512]{2,1,0:T(2,128)(2,1)}, u32[]{:S(2)}, u32[]{:S(2)}) collective-permute-start(bf16[256,2,512]{2,1,0:T(2,128)(2,1)} %get-tuple-element.16), channel_id=1, source_target_pairs={{0,8},{8,0},{16,24},{24,16},{1,9},{9,1},{17,25},{25,17},{2,10},{10... | collective-permute-start | bytes 1572872 | tf_op jit(solution)/shard_map/ppermute | solution.py:269
  38.5 120.6 %collective-permute-start.31 = (bf16[512,2,512]{2,1,0:T(2,128)(2,1)S(1)}, bf16[512,2,512]{2,1,0:T(2,128)(2,1)S(1)}, u32[]{:S(2)}, u32[]{:S(2)}) collective-permute-start(bf16[512,2,512]{2,1,0:T(2,128)(2,1)S(1)} %slice_bitcast_fusion.refs_10_), channel_id=1, source_target_pairs={{0,8},{8,0},{16,24},{24,16},{1,9},{9,1},{17,25},{25,17},{2,10},{10... | collective-permute-start | bytes 3145736 | tf_op jit(solution)/shard_map/ppermute | solution.py:297
  48.8 3.3 %copy-start.1 = (bf16[2,16,256,512]{3,2,1,0:T(8,128)(2,1)}, bf16[2,16,256,512]{3,2,1,0:T(8,128)(2,1)S(1)}, u32[]{:S(2)}) copy-start(bf16[2,16,256,512]{3,2,1,0:T(8,128)(2,1)S(1)} %bitcast_dynamic-update-slice_fusion.26) | copy-start | bytes 25165828
  55.7 8.9 %collective-permute-start.2 = (bf16[256,512]{1,0:T(8,128)(2,1)}, bf16[256,512]{1,0:T(8,128)(2,1)S(1)}, u32[]{:S(2)}, u32[]{:S(2)}) collective-permute-start(bf16[256,512]{1,0:T(8,128)(2,1)} %get-tuple-element.58), channel_id=1, source_target_pairs={{0,1},{1,0},{2,3},{3,2},{4,5},{5,4},{6,7},{7,6},{8,9},{9,8},{10,11... | collective-permute-start | bytes 786440 | tf_op jit(solution)/shard_map/ppermute | solution.py:225
  56.2 9.7 %collective-permute-start.3 = (bf16[256,512]{1,0:T(8,128)(2,1)}, bf16[256,512]{1,0:T(8,128)(2,1)}, u32[]{:S(2)}, u32[]{:S(2)}) collective-permute-start(bf16[256,512]{1,0:T(8,128)(2,1)} %get-tuple-element.58), channel_id=1, source_target_pairs={{0,2},{1,3},{2,4},{3,5},{4,6},{5,7},{8,10},{9,11},{10,12},{11,13},... | collective-permute-start | bytes 786440 | tf_op jit(solution)/shard_map/ppermute | solution.py:221
  67.7 7.7 %collective-permute-start.4 = (bf16[256,512]{1,0:T(8,128)(2,1)S(1)}, bf16[256,512]{1,0:T(8,128)(2,1)}, u32[]{:S(2)}, u32[]{:S(2)}) collective-permute-start(bf16[256,512]{1,0:T(8,128)(2,1)S(1)} %get-tuple-element.56), channel_id=1, source_target_pairs={{0,1},{1,0},{2,3},{3,2},{4,5},{5,4},{6,7},{7,6},{8,9},{9,8},{10,11... | collective-permute-start | bytes 786440 | tf_op jit(solution)/shard_map/ppermute | solution.py:225
  69.2 9.3 %collective-permute-start.5 = (bf16[256,512]{1,0:T(8,128)(2,1)S(1)}, bf16[256,512]{1,0:T(8,128)(2,1)}, u32[]{:S(2)}, u32[]{:S(2)}) collective-permute-start(bf16[256,512]{1,0:T(8,128)(2,1)S(1)} %get-tuple-element.56), channel_id=1, source_target_pairs={{0,2},{1,3},{2,4},{3,5},{4,6},{5,7},{8,10},{9,11},{10,12},{11,13},... | collective-permute-start | bytes 786440 | tf_op jit(solution)/shard_map/ppermute | solution.py:221
  80.2 8.7 %collective-permute-start.6 = (bf16[256,512]{1,0:T(8,128)(2,1)S(1)}, bf16[256,512]{1,0:T(8,128)(2,1)S(1)}, u32[]{:S(2)}, u32[]{:S(2)}) collective-permute-start(bf16[256,512]{1,0:T(8,128)(2,1)S(1)} %get-tuple-element.54), channel_id=1, source_target_pairs={{0,1},{1,0},{2,3},{3,2},{4,5},{5,4},{6,7},{7,6},{8,9},{9,8},{10,11... | collective-permute-start | bytes 786440 | tf_op jit(solution)/shard_map/ppermute | solution.py:225
  80.7 9.0 %collective-permute-start.7 = (bf16[256,512]{1,0:T(8,128)(2,1)S(1)}, bf16[256,512]{1,0:T(8,128)(2,1)S(1)}, u32[]{:S(2)}, u32[]{:S(2)}) collective-permute-start(bf16[256,512]{1,0:T(8,128)(2,1)S(1)} %get-tuple-element.54), channel_id=1, source_target_pairs={{0,2},{1,3},{2,4},{3,5},{4,6},{5,7},{8,10},{9,11},{10,12},{11,13},... | collective-permute-start | bytes 786440 | tf_op jit(solution)/shard_map/ppermute | solution.py:221
  87.4 18.5 %collective-permute-start.26 = (bf16[256,2,512]{2,1,0:T(2,128)(2,1)S(1)}, bf16[256,2,512]{2,1,0:T(2,128)(2,1)S(1)}, u32[]{:S(2)}, u32[]{:S(2)}) collective-permute-start(bf16[256,2,512]{2,1,0:T(2,128)(2,1)S(1)} %broadcast_select_fusion.3), channel_id=1, source_target_pairs={{0,16},{8,24},{16,0},{24,8},{1,17},{9,25},{17,1},{25,9},{2,18},{10... | collective-permute-start | bytes 1572872 | tf_op jit(solution)/shard_map/ppermute | solution.py:274
  91.4 9.2 %collective-permute-start.8 = (bf16[256,512]{1,0:T(8,128)(2,1)S(1)}, bf16[256,512]{1,0:T(8,128)(2,1)S(1)}, u32[]{:S(2)}, u32[]{:S(2)}) collective-permute-start(bf16[256,512]{1,0:T(8,128)(2,1)S(1)} %get-tuple-element.52), channel_id=1, source_target_pairs={{0,1},{1,0},{2,3},{3,2},{4,5},{5,4},{6,7},{7,6},{8,9},{9,8},{10,11... | collective-permute-start | bytes 786440 | tf_op jit(solution)/shard_map/ppermute | solution.py:225
  92.9 10.7 %collective-permute-start.9 = (bf16[256,512]{1,0:T(8,128)(2,1)S(1)}, bf16[256,512]{1,0:T(8,128)(2,1)S(1)}, u32[]{:S(2)}, u32[]{:S(2)}) collective-permute-start(bf16[256,512]{1,0:T(8,128)(2,1)S(1)} %get-tuple-element.52), channel_id=1, source_target_pairs={{0,2},{1,3},{2,4},{3,5},{4,6},{5,7},{8,10},{9,11},{10,12},{11,13},... | collective-permute-start | bytes 786440 | tf_op jit(solution)/shard_map/ppermute | solution.py:221
  99.0 23.0 %collective-permute-start.29 = (bf16[256,2,512]{2,1,0:T(2,128)(2,1)S(1)}, bf16[256,2,512]{2,1,0:T(2,128)(2,1)S(1)}, u32[]{:S(2)}, u32[]{:S(2)}) collective-permute-start(bf16[256,2,512]{2,1,0:T(2,128)(2,1)S(1)} %broadcast_select_fusion.1), channel_id=1, source_target_pairs={{0,16},{8,24},{16,0},{24,8},{1,17},{9,25},{17,1},{25,9},{2,18},{10... | collective-permute-start | bytes 1572872 | tf_op jit(solution)/shard_map/ppermute | solution.py:274
  105.3 7.7 %collective-permute-start.10 = (bf16[256,512]{1,0:T(8,128)(2,1)S(1)}, bf16[256,512]{1,0:T(8,128)(2,1)S(1)}, u32[]{:S(2)}, u32[]{:S(2)}) collective-permute-start(bf16[256,512]{1,0:T(8,128)(2,1)S(1)} %get-tuple-element.50), channel_id=1, source_target_pairs={{0,1},{1,0},{2,3},{3,2},{4,5},{5,4},{6,7},{7,6},{8,9},{9,8},{10,11... | collective-permute-start | bytes 786440 | tf_op jit(solution)/shard_map/ppermute | solution.py:225
  107.0 28.6 %copy-start.3 = (bf16[256,2,512]{2,1,0:T(2,128)(2,1)}, bf16[256,2,512]{2,1,0:T(2,128)(2,1)S(1)}, u32[]{:S(2)}) copy-start(bf16[256,2,512]{2,1,0:T(2,128)(2,1)S(1)} %broadcast_select_fusion.2) | copy-start | bytes 1572868
  107.0 7.3 %collective-permute-start.11 = (bf16[256,512]{1,0:T(8,128)(2,1)S(1)}, bf16[256,512]{1,0:T(8,128)(2,1)S(1)}, u32[]{:S(2)}, u32[]{:S(2)}) collective-permute-start(bf16[256,512]{1,0:T(8,128)(2,1)S(1)} %get-tuple-element.50), channel_id=1, source_target_pairs={{0,2},{1,3},{2,4},{3,5},{4,6},{5,7},{8,10},{9,11},{10,12},{11,13},... | collective-permute-start | bytes 786440 | tf_op jit(solution)/shard_map/ppermute | solution.py:221
  113.0 31.4 %collective-permute-start.27 = (bf16[2,256,2,512]{3,2,1,0:T(2,128)(2,1)}, bf16[2,256,2,512]{3,2,1,0:T(2,128)(2,1)}, u32[]{:S(2)}, u32[]{:S(2)}) collective-permute-start(bf16[2,256,2,512]{3,2,1,0:T(2,128)(2,1)} %pad_maximum_fusion), channel_id=1, source_target_pairs={{0,8},{8,0},{16,24},{24,16},{1,9},{9,1},{17,25},{25,17},{2,10},{10... | collective-permute-start | bytes 3145736 | tf_op jit(solution)/shard_map/ppermute | solution.py:284
  116.1 8.2 %collective-permute-start.12 = (bf16[256,512]{1,0:T(8,128)(2,1)S(1)}, bf16[256,512]{1,0:T(8,128)(2,1)S(1)}, u32[]{:S(2)}, u32[]{:S(2)}) collective-permute-start(bf16[256,512]{1,0:T(8,128)(2,1)S(1)} %get-tuple-element.48), channel_id=1, source_target_pairs={{0,1},{1,0},{2,3},{3,2},{4,5},{5,4},{6,7},{7,6},{8,9},{9,8},{10,11... | collective-permute-start | bytes 786440 | tf_op jit(solution)/shard_map/ppermute | solution.py:225
  117.6 8.2 %collective-permute-start.13 = (bf16[256,512]{1,0:T(8,128)(2,1)S(1)}, bf16[256,512]{1,0:T(8,128)(2,1)S(1)}, u32[]{:S(2)}, u32[]{:S(2)}) collective-permute-start(bf16[256,512]{1,0:T(8,128)(2,1)S(1)} %get-tuple-element.48), channel_id=1, source_target_pairs={{0,2},{1,3},{2,4},{3,5},{4,6},{5,7},{8,10},{9,11},{10,12},{11,13},... | collective-permute-start | bytes 786440 | tf_op jit(solution)/shard_map/ppermute | solution.py:221
  123.2 12.5 %copy-start.5 = (bf16[1,256,2,512]{3,2,1,0:T(2,128)(2,1)}, bf16[1,256,2,512]{3,2,1,0:T(2,128)(2,1)S(1)}, u32[]{:S(2)}) copy-start(bf16[1,256,2,512]{3,2,1,0:T(2,128)(2,1)S(1)} %fusion.15) | copy-start | bytes 1572868
  127.6 9.4 %collective-permute-start.14 = (bf16[256,512]{1,0:T(8,128)(2,1)S(1)}, bf16[256,512]{1,0:T(8,128)(2,1)}, u32[]{:S(2)}, u32[]{:S(2)}) collective-permute-start(bf16[256,512]{1,0:T(8,128)(2,1)S(1)} %get-tuple-element.46), channel_id=1, source_target_pairs={{0,1},{1,0},{2,3},{3,2},{4,5},{5,4},{6,7},{7,6},{8,9},{9,8},{10,11... | collective-permute-start | bytes 786440 | tf_op jit(solution)/shard_map/ppermute | solution.py:225
  130.7 22.1 %collective-permute-start.30 = (bf16[2,256,2,512]{3,2,1,0:T(2,128)(2,1)}, bf16[2,256,2,512]{3,2,1,0:T(2,128)(2,1)}, u32[]{:S(2)}, u32[]{:S(2)}) collective-permute-start(bf16[2,256,2,512]{3,2,1,0:T(2,128)(2,1)} %pad_maximum_fusion.1), channel_id=1, source_target_pairs={{0,8},{8,0},{16,24},{24,16},{1,9},{9,1},{17,25},{25,17},{2,10},{10... | collective-permute-start | bytes 3145736 | tf_op jit(solution)/shard_map/ppermute | solution.py:284
  130.7 10.5 %collective-permute-start.15 = (bf16[256,512]{1,0:T(8,128)(2,1)S(1)}, bf16[256,512]{1,0:T(8,128)(2,1)}, u32[]{:S(2)}, u32[]{:S(2)}) collective-permute-start(bf16[256,512]{1,0:T(8,128)(2,1)S(1)} %get-tuple-element.46), channel_id=1, source_target_pairs={{0,2},{1,3},{2,4},{3,5},{4,6},{5,7},{8,10},{9,11},{10,12},{11,13},... | collective-permute-start | bytes 786440 | tf_op jit(solution)/shard_map/ppermute | solution.py:221
  135.8 15.6 %copy-start.4 = (bf16[256,2,512]{2,1,0:T(2,128)(2,1)S(1)}, bf16[256,2,512]{2,1,0:T(2,128)(2,1)}, u32[]{:S(2)}) copy-start(bf16[256,2,512]{2,1,0:T(2,128)(2,1)} %copy-done.3) | copy-start | bytes 1572868
  135.8 21.8 %copy-start.6 = (bf16[1,256,2,512]{3,2,1,0:T(2,128)(2,1)S(1)}, bf16[1,256,2,512]{3,2,1,0:T(2,128)(2,1)}, u32[]{:S(2)}) copy-start(bf16[1,256,2,512]{3,2,1,0:T(2,128)(2,1)} %copy-done.5) | copy-start | bytes 1572868
  137.0 40.1 %collective-permute-start.32 = (bf16[2,512,512]{2,1,0:T(8,128)(2,1)}, bf16[2,512,512]{2,1,0:T(8,128)(2,1)S(1)}, u32[]{:S(2)}, u32[]{:S(2)}) collective-permute-start(bf16[2,512,512]{2,1,0:T(8,128)(2,1)} %bitcast.173), channel_id=1, source_target_pairs={{0,16},{8,24},{1,17},{9,25},{2,18},{10,26},{3,19},{11,27},{4,20},{... | collective-permute-start | bytes 3145736 | tf_op jit(solution)/shard_map/ppermute | solution.py:234
  143.0 27.2 %collective-permute-start.16 = (bf16[256,512]{1,0:T(8,128)(2,1)S(1)}, bf16[256,512]{1,0:T(8,128)(2,1)S(1)}, u32[]{:S(2)}, u32[]{:S(2)}) collective-permute-start(bf16[256,512]{1,0:T(8,128)(2,1)S(1)} %get-tuple-element.44), channel_id=1, source_target_pairs={{0,1},{1,0},{2,3},{3,2},{4,5},{5,4},{6,7},{7,6},{8,9},{9,8},{10,11... | collective-permute-start | bytes 786440 | tf_op jit(solution)/shard_map/ppermute | solution.py:225
  144.5 26.4 %collective-permute-start.17 = (bf16[256,512]{1,0:T(8,128)(2,1)S(1)}, bf16[256,512]{1,0:T(8,128)(2,1)S(1)}, u32[]{:S(2)}, u32[]{:S(2)}) collective-permute-start(bf16[256,512]{1,0:T(8,128)(2,1)S(1)} %get-tuple-element.44), channel_id=1, source_target_pairs={{0,2},{1,3},{2,4},{3,5},{4,6},{5,7},{8,10},{9,11},{10,12},{11,13},... | collective-permute-start | bytes 786440 | tf_op jit(solution)/shard_map/ppermute | solution.py:221
  152.9 15.1 %collective-permute-start.34 = (bf16[128,512]{1,0:T(8,128)(2,1)S(1)}, bf16[128,512]{1,0:T(8,128)(2,1)S(1)}, u32[]{:S(2)}, u32[]{:S(2)}) collective-permute-start(bf16[128,512]{1,0:T(8,128)(2,1)S(1)} %fusion.28), channel_id=1, source_target_pairs={{0,2},{1,3},{2,4},{3,5},{4,6},{5,7},{8,10},{9,11},{10,12},{11,13},... | collective-permute-start | bytes 393224 | tf_op jit(solution)/shard_map/ppermute | solution.py:305
  159.1 18.0 %copy-start.7 = (bf16[2,2,256,512]{3,2,1,0:T(8,128)(2,1)S(1)}, bf16[2,2,256,512]{3,2,1,0:T(8,128)(2,1)}, u32[]{:S(2)}) copy-start(bf16[2,2,256,512]{3,2,1,0:T(8,128)(2,1)} %slice.167) | copy-start | bytes 3145732
  168.0 7.1 %collective-permute-start.35 = (bf16[128,512]{1,0:T(8,128)(2,1)S(1)}, bf16[128,512]{1,0:T(8,128)(2,1)S(1)}, u32[]{:S(2)}, u32[]{:S(2)}) collective-permute-start(bf16[128,512]{1,0:T(8,128)(2,1)S(1)} %broadcast_select_fusion.7), channel_id=1, source_target_pairs={{0,2},{1,3},{2,4},{3,5},{4,6},{5,7},{8,10},{9,11},{10,12},{11,13},... | collective-permute-start | bytes 393224 | tf_op jit(solution)/shard_map/ppermute | solution.py:305
  172.6 16.1 %collective-permute-start.18 = (bf16[256,512]{1,0:T(8,128)(2,1)S(1)}, bf16[256,512]{1,0:T(8,128)(2,1)S(1)}, u32[]{:S(2)}, u32[]{:S(2)}) collective-permute-start(bf16[256,512]{1,0:T(8,128)(2,1)S(1)} %get-tuple-element.42), channel_id=1, source_target_pairs={{0,1},{1,0},{2,3},{3,2},{4,5},{5,4},{6,7},{7,6},{8,9},{9,8},{10,11... | collective-permute-start | bytes 786440 | tf_op jit(solution)/shard_map/ppermute | solution.py:225
  173.1 10.9 %collective-permute-start.19 = (bf16[256,512]{1,0:T(8,128)(2,1)S(1)}, bf16[256,512]{1,0:T(8,128)(2,1)S(1)}, u32[]{:S(2)}, u32[]{:S(2)}) collective-permute-start(bf16[256,512]{1,0:T(8,128)(2,1)S(1)} %get-tuple-element.42), channel_id=1, source_target_pairs={{0,2},{1,3},{2,4},{3,5},{4,6},{5,7},{8,10},{9,11},{10,12},{11,13},... | collective-permute-start | bytes 786440 | tf_op jit(solution)/shard_map/ppermute | solution.py:221
  175.1 7.2 %collective-permute-start.36 = (bf16[128,512]{1,0:T(8,128)(2,1)S(1)}, bf16[128,512]{1,0:T(8,128)(2,1)S(1)}, u32[]{:S(2)}, u32[]{:S(2)}) collective-permute-start(bf16[128,512]{1,0:T(8,128)(2,1)S(1)} %broadcast_select_fusion.6), channel_id=1, source_target_pairs={{0,2},{1,3},{2,4},{3,5},{4,6},{5,7},{8,10},{9,11},{10,12},{11,13},... | collective-permute-start | bytes 393224 | tf_op jit(solution)/shard_map/ppermute | solution.py:305
  177.2 40.2 %collective-permute-start.33 = (bf16[2,512,512]{2,1,0:T(8,128)(2,1)S(1)}, bf16[2,512,512]{2,1,0:T(8,128)(2,1)S(1)}, u32[]{:S(2)}, u32[]{:S(2)}) collective-permute-start(bf16[2,512,512]{2,1,0:T(8,128)(2,1)S(1)} %broadcast_select_fusion.4.old_mine), channel_id=1, source_target_pairs={{0,8},{8,0},{16,24},{24,16},{1,9},{9,1},{17,25},{25,17},{2,10},{10... | collective-permute-start | bytes 3145736 | tf_op jit(solution)/shard_map/ppermute | solution.py:236
  182.2 8.0 %collective-permute-start.37 = (bf16[128,512]{1,0:T(8,128)(2,1)S(1)}, bf16[128,512]{1,0:T(8,128)(2,1)S(1)}, u32[]{:S(2)}, u32[]{:S(2)}) collective-permute-start(bf16[128,512]{1,0:T(8,128)(2,1)S(1)} %broadcast_select_fusion.5), channel_id=1, source_target_pairs={{0,1},{1,0},{2,3},{3,2},{4,5},{5,4},{6,7},{7,6},{8,9},{9,8},{10,11... | collective-permute-start | bytes 393224 | tf_op jit(solution)/shard_map/ppermute | solution.py:306
  184.0 14.7 %collective-permute-start.20 = (bf16[256,512]{1,0:T(8,128)(2,1)S(1)}, bf16[256,512]{1,0:T(8,128)(2,1)S(1)}, u32[]{:S(2)}, u32[]{:S(2)}) collective-permute-start(bf16[256,512]{1,0:T(8,128)(2,1)S(1)} %collective-permute-done.19), channel_id=1, source_target_pairs={{0,1},{1,0},{2,3},{3,2},{4,5},{5,4},{6,7},{7,6},{8,9},{9,8},{10,11... | collective-permute-start | bytes 786440 | tf_op jit(solution)/shard_map/ppermute | solution.py:225
  184.3 8.3 %collective-permute-start.21 = (bf16[256,512]{1,0:T(8,128)(2,1)S(1)}, bf16[256,512]{1,0:T(8,128)(2,1)S(1)}, u32[]{:S(2)}, u32[]{:S(2)}) collective-permute-start(bf16[256,512]{1,0:T(8,128)(2,1)S(1)} %collective-permute-done.19), channel_id=1, source_target_pairs={{0,2},{1,3},{2,4},{3,5},{4,6},{5,7},{8,10},{9,11},{10,12},{11,13},... | collective-permute-start | bytes 786440 | tf_op jit(solution)/shard_map/ppermute | solution.py:221
  190.2 9.9 %collective-permute-start.38 = (bf16[2,128,512]{2,1,0:T(8,128)(2,1)S(1)}, bf16[2,128,512]{2,1,0:T(8,128)(2,1)S(1)}, u32[]{:S(2)}, u32[]{:S(2)}) collective-permute-start(bf16[2,128,512]{2,1,0:T(8,128)(2,1)S(1)} %maximum_select_fusion.1), channel_id=1, source_target_pairs={{0,16},{8,24},{16,0},{24,8},{1,17},{9,25},{17,1},{25,9},{2,18},{10... | collective-permute-start | bytes 786440 | tf_op jit(solution)/shard_map/ppermute | solution.py:311
  192.6 10.3 %collective-permute-start.22 = (bf16[256,512]{1,0:T(8,128)(2,1)S(1)}, bf16[256,512]{1,0:T(8,128)(2,1)S(1)}, u32[]{:S(2)}, u32[]{:S(2)}) collective-permute-start(bf16[256,512]{1,0:T(8,128)(2,1)S(1)} %collective-permute-done.21), channel_id=1, source_target_pairs={{0,1},{1,0},{2,3},{3,2},{4,5},{5,4},{6,7},{7,6},{8,9},{9,8},{10,11... | collective-permute-start | bytes 786440 | tf_op jit(solution)/shard_map/ppermute | solution.py:225
  194.3 8.3 %collective-permute-start.23 = (bf16[256,512]{1,0:T(8,128)(2,1)S(1)}, bf16[256,512]{1,0:T(8,128)(2,1)S(1)}, u32[]{:S(2)}, u32[]{:S(2)}) collective-permute-start(bf16[256,512]{1,0:T(8,128)(2,1)S(1)} %collective-permute-done.21), channel_id=1, source_target_pairs={{0,2},{1,3},{2,4},{3,5},{4,6},{5,7},{8,10},{9,11},{10,12},{11,13},... | collective-permute-start | bytes 786440 | tf_op jit(solution)/shard_map/ppermute | solution.py:221
  200.2 17.2 %copy-start = (bf16[2,512,512]{2,1,0:T(8,128)(2,1)S(1)}, bf16[2,512,512]{2,1,0:T(8,128)(2,1)}, u32[]{:S(2)}) copy-start(bf16[2,512,512]{2,1,0:T(8,128)(2,1)} %upper.3) | copy-start | bytes 3145732
  200.2 9.6 %collective-permute-start.39 = (bf16[2,2,128,512]{3,2,1,0:T(8,128)(2,1)S(1)}, bf16[2,2,128,512]{3,2,1,0:T(8,128)(2,1)S(1)}, u32[]{:S(2)}, u32[]{:S(2)}) collective-permute-start(bf16[2,2,128,512]{3,2,1,0:T(8,128)(2,1)S(1)} %pad_maximum_fusion.4), channel_id=1, source_target_pairs={{0,8},{8,0},{16,24},{24,16},{1,9},{9,1},{17,25},{25,17},{2,10},{10... | collective-permute-start | bytes 1572872 | tf_op jit(solution)/shard_map/ppermute | solution.py:316
  202.5 6.6 %collective-permute-start.24 = (bf16[256,512]{1,0:T(8,128)(2,1)S(1)}, bf16[256,512]{1,0:T(8,128)(2,1)S(1)}, u32[]{:S(2)}, u32[]{:S(2)}) collective-permute-start(bf16[256,512]{1,0:T(8,128)(2,1)S(1)} %collective-permute-done.23), channel_id=1, source_target_pairs={{0,1},{1,0},{2,3},{3,2},{4,5},{5,4},{6,7},{7,6},{8,9},{9,8},{10,11... | collective-permute-start | bytes 786440 | tf_op jit(solution)/shard_map/ppermute | solution.py:225
  (1 other events, 2.4 us)

commit v2 on v0

v2 whole, which is shorter than its diff:
```python
import functools

import jax
import jax.numpy as jnp
from jax import lax
from jax.experimental import pallas as pl
from jax.experimental.pallas import tpu as pltpu
from jax.sharding import PartitionSpec as P

BF16 = jnp.bfloat16
F32 = jnp.float32
I32 = jnp.int32
SMEM = pl.BlockSpec(memory_space=pltpu.SMEM)
VMEM = pl.BlockSpec(memory_space=pltpu.VMEM)
PARAMS = pltpu.CompilerParams(vmem_limit_bytes=48 * 1024 * 1024)


def dot(a, b):
    return jnp.dot(a, b, preferred_element_type=F32)


def flat(rows):
    return rows.reshape(rows.shape[0], rows.shape[1] * rows.shape[2])


def index_kernel(nb, rows, meta, pivots, fetch, join, arrive, goal, hops):
    row, core, row_devices = meta[0], meta[1], meta[3]
    chip, chips = row // 2, row_devices // 2
    slots = lax.broadcasted_iota(I32, (1, 2 * nb), 1)

    def swapped(panel, index):
        def add(i, total):
            begin = pl.multiple_of(i * 8, 8)
            pivot = pivots[pl.ds(begin, 8), panel : panel + 1]
            top = panel * nb + begin + lax.broadcasted_iota(I32, (8, 1), 0)
            step = pivot - top
            total = total + jnp.where(index == top, step, 0)
            return total - jnp.where(index == pivot, step, 0)

        total = lax.fori_loop(0, nb // 8, add, jnp.zeros((8, 2 * nb), I32), unroll=4)
        return index + jnp.sum(total, axis=0, keepdims=True)

    def source_of(index):
        return swapped(0, swapped(1, index))

    def holder(index):
        return lax.rem(lax.div(index, nb), row_devices)

    def local(index):
        return lax.div(index, nb * row_devices) * nb + lax.rem(index, nb)

    def placed(index):
        mine = (holder(index) == row) & (index >= 2 * nb)
        return jnp.where(mine, local(index), rows)

    source = source_of(slots)
    second = source_of(source)
    target = swapped(1, swapped(0, slots))
    from_chip = lax.div(holder(source), 2)
    wanted = jnp.where(from_chip == chip, source, second)
    fetch[...] = local(wanted)
    join[...] = jnp.where(holder(wanted) == row, lax.rem(slots, nb), nb)
    arrive[...] = placed(source)
    goal[...] = placed(target)
    hops[...] = lax.rem(chip + chips - from_chip, chips)


def make_indices(meta, pivots, nb, rows):
    steps = pivots.shape[0]
    shape = jax.ShapeDtypeStruct((1, steps * nb), I32)
    return pl.pallas_call(
        functools.partial(index_kernel, nb, rows),
        out_shape=(shape,) * 5,
        in_specs=[SMEM, VMEM],
        out_specs=(VMEM,) * 5,
        compiler_params=PARAMS,
    )(meta, pivots.T)


def split_kernel(tiles, *panels):
    nb = panels[0].shape[0]
    for b, panel in enumerate(panels):
        panel[...] = flat(tiles[b * nb : (b + 1) * nb])[:, :nb]


def split_panels(tiles, nb):
    count = tiles.shape[0] // nb
    return pl.pallas_call(
        split_kernel,
        out_shape=(jax.ShapeDtypeStruct((nb, nb), BF16),) * count,
        in_specs=[VMEM],
        out_specs=(VMEM,) * count,
        compiler_params=PARAMS,
    )(tiles)


def send_kernel(meta, fetch, tiles, send, block0):
    count = send.shape[0]
    begin = (1 - meta[1]) * count

    def copy(i, carry):
        send[i] = tiles[fetch[0, begin + i]]
        return carry

    lax.fori_loop(0, count, copy, 0, unroll=16)
    block0[...] = tiles[0:count]


def gather_sent(meta, fetch, tiles, nb):
    shape = jax.ShapeDtypeStruct((nb,) + tiles.shape[1:], BF16)
    return pl.pallas_call(
        send_kernel,
        out_shape=(shape, shape),
        in_specs=[SMEM, SMEM, VMEM],
        out_specs=(VMEM, VMEM),
        compiler_params=PARAMS,
    )(meta, fetch, tiles)


def join_kernel(meta, fetch, join, tiles, came, joined, work):
    count = came.shape[0]
    begin = meta[1] * count
    work[0:count] = came[...]

    def copy(i, carry):
        work[join[0, begin + i]] = tiles[fetch[0, begin + i]]
        return carry

    lax.fori_loop(0, count, copy, 0, unroll=16)
    joined[...] = work[0:count]


def join_rows(meta, fetch, join, tiles, came):
    nb = came.shape[0]
    return pl.pallas_call(
        join_kernel,
        out_shape=jax.ShapeDtypeStruct(came.shape, BF16),
        in_specs=[SMEM, SMEM, SMEM, VMEM, VMEM],
        out_specs=VMEM,
        scratch_shapes=[pltpu.VMEM((nb + 8,) + came.shape[1:], BF16)],
        compiler_params=PARAMS,
    )(meta, fetch, join, tiles, came)


def scatter_kernel(meta, arrive, goal, came, came_sibling, old, old_sibling, tiles, out):
    core, chip = meta[1], meta[0] // 2
    count = old.shape[0]
    out[0 : tiles.shape[0]] = tiles[...]

    def scatter(index, values, begin):
        def copy(i, carry):
            out[index[0, begin + i]] = values[i]
            return carry

        lax.fori_loop(0, count, copy, 0, unroll=16)

    @pl.when(chip == 0)
    def _():
        scatter(goal, old, core * count)
        scatter(goal, old_sibling, (1 - core) * count)

    @pl.when(chip != 0)
    def _():
        scatter(arrive, came, core * count)
        scatter(arrive, came_sibling, (1 - core) * count)


def scatter_rows(meta, arrive, goal, came, came_sibling, old, old_sibling, tiles):
    rows = tiles.shape[0] + 8
    return pl.pallas_call(
        scatter_kernel,
        out_shape=jax.ShapeDtypeStruct((rows,) + tiles.shape[1:], BF16),
        in_specs=[SMEM] * 3 + [VMEM] * 5,
        out_specs=VMEM,
        compiler_params=PARAMS,
    )(meta, arrive, goal, came, came_sibling, old, old_sibling, tiles)


def choose(hop, choices):
    value = flat(choices[0]).astype(F32)
    for h, other in enumerate(choices[1:], 1):
        value = jnp.where(hop == h, flat(other).astype(F32), value)
    return value.astype(BF16)


def head_kernel(meta, hops, *refs):
    *choices, out = refs
    part = out.shape[0]
    nb = hops.shape[0] // 2
    core, begin = meta[1], meta[0] // 2 * part
    hop = hops[pl.ds(core * nb + begin, part)]
    out[...] = choose(hop, [c[pl.ds(begin, part)] for c in choices])[:, : out.shape[1]]


def head_part(meta, hops, choices, part):
    nb = choices[0].shape[2]
    return pl.pallas_call(
        head_kernel,
        out_shape=jax.ShapeDtypeStruct((part, nb), BF16),
        in_specs=[SMEM] + [VMEM] * (1 + len(choices)),
        out_specs=VMEM,
        compiler_params=PARAMS,
    )(meta, hops, *choices)


def prep_kernel(chips, meta, hops, lower, upper, *refs):
    mine, sibling = refs[:chips], refs[chips : 2 * chips]
    heads, heads_sibling = refs[2 * chips : 3 * chips], refs[3 * chips : 4 * chips]
    up0, up1, up0_panel, top, fresh, head = refs[4 * chips :]
    core, column, chip = meta[1], meta[2], meta[0] // 2
    nb = head.shape[1]
    part = heads[0].shape[0]
    for who, choices in ((core, mine), (1 - core, sibling)):
        fresh[who] = choose(hops[pl.ds(who * nb, nb)], [c[0:nb] for c in choices])
    for who, pieces in ((core, heads), (1 - core, heads_sibling)):
        for h, piece in enumerate(pieces):
            head[who, pl.ds(lax.rem(chip + chips - h, chips) * part, part)] = piece[...]
    up0_panel[...] = dot(lower[0], head[0]).astype(BF16)
    factor = dot(head[1], upper[0]).astype(BF16)
    in_panel, next_panel = column == 0, column == 1
    tops = [[], []]
    for j in range(fresh.shape[2] // nb):
        cols = slice(j * nb, (j + 1) * nb)
        product = dot(lower[0], fresh[0, :, cols])
        shown = product
        if j == 0:
            shown = jnp.where(in_panel, fresh[0, :, cols].astype(F32), product)
            product = jnp.where(in_panel, 0.0, product)
        product = product.astype(BF16)
        up0[:, cols] = product
        updated = (fresh[1, :, cols].astype(F32) - dot(factor, product)).astype(BF16)
        last = dot(lower[1], updated)
        kept = last
        if j == 0:
            kept = jnp.where(next_panel, updated.astype(F32), kept)
            kept = jnp.where(in_panel, factor.astype(F32), kept)
            last = jnp.where(in_panel | next_panel, 0.0, last)
        up1[:, cols] = last.astype(BF16)
        tops[0].append(shown.astype(BF16))
        tops[1].append(kept.astype(BF16))
    for k in range(2):
        top[k * nb : (k + 1) * nb] = jnp.concatenate(tops[k], axis=1).reshape(nb, len(tops[k]), nb)


def prep(meta, hops, lower, upper, mine, sibling, heads, heads_sibling):
    cb, nb = mine[0].shape[1:]
    chips = len(mine)
    return pl.pallas_call(
        functools.partial(prep_kernel, chips),
        out_shape=(
            jax.ShapeDtypeStruct((nb, cb * nb), BF16),
            jax.ShapeDtypeStruct((nb, cb * nb), BF16),
            jax.ShapeDtypeStruct((nb, nb), BF16),
            jax.ShapeDtypeStruct((2 * nb, cb, nb), BF16),
        ),
        in_specs=[SMEM] + [VMEM] * (3 + 4 * chips),
        out_specs=(VMEM,) * 4,
        scratch_shapes=[pltpu.VMEM((2, nb, cb * nb), BF16), pltpu.VMEM((2, nb, nb), BF16)],
        compiler_params=PARAMS,
    )(meta, hops, lower, upper, *mine, *sibling, *heads, *heads_sibling)


def update_kernel(
    block, meta, goal, held, other, tiles, old, old_sibling, upper, up0, up1, up0_panel, top, *rest
):
    out = rest[-1]
    row, core, column = meta[0], meta[1], meta[2]
    side = lax.rem(column, 2)
    chunk, cb, nb = out.shape
    begin = pl.program_id(0) * chunk

    def from_top():
        out[...] = top[pl.ds(row * nb + begin, chunk)]

    def from_factors():
        here = block * nb + begin + lax.broadcasted_iota(I32, (chunk, nb), 0)
        pick = jnp.where(here == goal[pl.ds(core, 1), :], 1.0, 0.0)
        pick_sibling = jnp.where(here == goal[pl.ds(1 - core, 1), :], 1.0, 0.0)
        moved = jnp.sum(pick + pick_sibling, axis=1, keepdims=True) > 0.5
        pick, pick_sibling = pick.astype(BF16), pick_sibling.astype(BF16)
        mine, theirs = held[...].astype(F32), other[...].astype(F32)
        raw = (jnp.where(side == 0, mine, theirs), jnp.where(side == 0, theirs, mine))
        panels = []
        for k in range(2):
            which = lax.rem(k + side, 2)
            brought = dot(pick, old[which]) + dot(pick_sibling, old_sibling[which])
            panels.append(jnp.where(moved, brought, raw[k]))
        factor0 = dot(panels[0].astype(BF16), upper[0]).astype(BF16)
        below = (panels[1] - dot(factor0, up0_panel[...])).astype(BF16)
        factor1 = dot(below, upper[1]).astype(BF16)
        values = flat(tiles[...])
        results = []
        for j in range(cb):
            cols = slice(j * nb, (j + 1) * nb)
            value = values[:, cols].astype(F32) - dot(factor0, up0[:, cols])
            value = value.astype(BF16).astype(F32) - dot(factor1, up1[:, cols])
            if j == 0:
                value = jnp.where(column == 0, factor0.astype(F32), value)
                value = jnp.where(column == 1, factor1.astype(F32), value)
            results.append(value.astype(BF16))
        out[...] = jnp.concatenate(results, axis=1).reshape(chunk, cb, nb)

    if block == 0:
        pl.when(row < 2)(from_top)
        pl.when(row >= 2)(from_factors)
    else:
        from_factors()


def update(block, meta, goal, held, other, tiles, old, old_sibling, upper, up0, up1, up0_panel, top, rows, done):
    nb = held.shape[0]
    chunk = nb // 2
    cb = tiles.shape[1]
    whole = lambda a: pl.BlockSpec(a.shape, lambda s: (0,) * a.ndim)
    at_block = lambda s: (block * (nb // chunk) + s, 0, 0)
    operands = [meta, goal, held, other, tiles, old, old_sibling, upper, up0, up1, up0_panel, top]
    in_specs = [
        SMEM,
        whole(goal),
        pl.BlockSpec((chunk, nb), lambda s: (s, 0)),
        pl.BlockSpec((chunk, nb), lambda s: (s, 0)),
        pl.BlockSpec((chunk, cb, nb), at_block),
    ] + [whole(a) for a in operands[5:]]
    aliases = {}
    if done is not None:
        aliases = {len(operands): 0}
        operands.append(done)
        in_specs.append(pl.BlockSpec(memory_space=pl.ANY))
    steps = nb // chunk
    return pl.pallas_call(
        functools.partial(update_kernel, block),
        grid=(steps,),
        out_shape=jax.ShapeDtypeStruct((rows, cb, nb), BF16),
        in_specs=in_specs,
        out_specs=pl.BlockSpec((chunk, cb, nb), at_block),
        input_output_aliases=aliases,
        compiler_params=PARAMS,
        cost_estimate=pl.CostEstimate(
            flops=2 * nb**3 * (7 + 2 * cb), bytes_accessed=16 * nb * nb * 2, transcendentals=0
        ),
    )(*operands)


def body(matrix, pivots, lower_inverse, upper_inverse):
    rb, nb, cb, _ = matrix.shape
    rows = rb * nb
    row_devices = lax.axis_size("prow")
    col_devices = lax.axis_size("pcol")
    chips = row_devices // 2
    line = col_devices // 2
    row = lax.axis_index("prow").astype(I32)
    column = lax.axis_index("pcol").astype(I32)
    core, chip = row % 2, row // 2
    place = column // 2
    meta = jnp.stack([row, core, column, jnp.int32(row_devices)])
    tiles = matrix.reshape(rows, cb, nb)

    sibling = [(r, r ^ 1) for r in range(row_devices)]
    neighbour = [(c, c ^ 1) for c in range(col_devices)]

    def chip_hop(h):
        return [(r, (r + 2 * h) % row_devices) for r in range(row_devices)]

    def line_hop(h):
        return [(2 * h - 2, 2 * h), (2 * h - 1, 2 * h + 1)]

    def along_line(value, axes, hop_pairs):
        held = value
        for h in range(1, line):
            value = lax.ppermute(value, axes, hop_pairs(h))
            held = jnp.where(place == h, value, held)
        return held

    own = split_panels(tiles, nb)
    hops_done = [list(own)]
    for h in range(1, line):
        came = []
        for b in range(rb):
            sent = hops_done[-1][b]
            if b >= 2:
                sent, _ = lax.optimization_barrier((sent, came[b - 2]))
            came.append(lax.ppermute(sent, "pcol", line_hop(h)))
        hops_done.append(came)
    held, other = [], []
    for b in range(rb):
        value = own[b]
        for h in range(1, line):
            value = jnp.where(place == h, hops_done[h][b], value)
        held.append(value)
        other.append(lax.ppermute(value, "pcol", neighbour))

    fetch, join, arrive, goal, hops = make_indices(meta, pivots, nb, rows)
    hops = hops.reshape(2 * nb, 1)
    send, block0 = gather_sent(meta, fetch, tiles, nb)
    from_sibling = lax.ppermute(send, "prow", sibling)
    joined = join_rows(meta, fetch, join, tiles, from_sibling)
    mine = [joined] + [lax.ppermute(joined, "prow", chip_hop(h)) for h in range(1, chips)]
    block0_sibling = lax.ppermute(block0, "prow", sibling)
    theirs = [lax.ppermute(value, "prow", sibling) for value in mine]

    part = nb // chips
    head = head_part(meta, hops, mine, part)
    flat_index = lambda r, c: r * col_devices + c
    senders = [[r for r in range(row_devices) if r % 2 != s] for s in range(2)]

    def head_pairs(h):
        return [(flat_index(r, a), flat_index(r, b)) for a, b in line_hop(h) for r in senders[a % 2]]

    both = ("prow", "pcol")
    head = along_line(head, both, head_pairs)
    swap_pairs = [(flat_index(r, c), flat_index(r, c ^ 1)) for c in range(col_devices) for r in senders[c % 2]]
    head = jnp.where(column % 2 != core, head, lax.ppermute(head, both, swap_pairs))
    heads = [head] + [lax.ppermute(head, "prow", chip_hop(h)) for h in range(1, chips)]
    heads_sibling = [lax.ppermute(value, "prow", sibling) for value in heads]
    up0, up1, up0_panel, top = prep(
        meta, hops, lower_inverse, upper_inverse, mine, theirs, heads, heads_sibling
    )

    def from_first_chip(values):
        value = values[-1]
        for h in range(1, chips - 1):
            value = jnp.where(chip == h, values[h], value)
        return value

    moved_tiles = scatter_rows(
        meta, arrive, goal, from_first_chip(mine), from_first_chip(theirs), block0, block0_sibling, tiles
    )

    old = jnp.stack([held[0], other[0]])
    first_old = old
    for h in range(1, chips):
        came = lax.ppermute(first_old, "prow", [(0, 2 * h), (1, 2 * h + 1)])
        old = jnp.where(chip == h, came, old)
    old_sibling = lax.ppermute(old, "prow", sibling)

    goal = goal.reshape(2, nb)
    result = None
    for b in range(rb):
        result = update(
            b, meta, goal, held[b], other[b], moved_tiles, old, old_sibling, upper_inverse,
            up0, up1, up0_panel, top, rows, result,
        )
    return result.reshape(matrix.shape)


def solution(mesh):
    placed = (P(None, "prow", None, "pcol"), P(), P(), P())
    return jax.shard_map(
        body, mesh=mesh, in_specs=placed, out_specs=P(None, "prow", None, "pcol"), check_vma=False
    )
```

time: 463 us -> 197 us (0.43)
  the two profiles are of different devices: /device:TPU:0 before, /device:TPU:30 now
where the time goes in v2:
time: 197 us; the launch traced here: 196 us
  Pallas kernels  78.8 us (40%)
  waiting for transfers between devices  66.7 us (34%)
  starting transfers between devices  37.4 us (19%)
  other arithmetic  9.76 us (5%)
  local copies, waits for them, and re-layouts  2.96 us (2%)
    ppermute x15, waiting for transfers between devices, body(): came.append(lax.ppermute(sent, 'pcol', line_hop(h)))  58.4 us
    pallas_call x5, Pallas kernels, update(): pl.pallas_call(functools.partial(update_kernel, block), grid=(steps,), ou...  38.2 us
    ppermute x15, starting transfers between devices, body(): came.append(lax.ppermute(sent, 'pcol', line_hop(h)))  21.1 us
    pallas_call x1, Pallas kernels, make_indices(): pl.pallas_call(functools.partial(index_kernel, nb, rows), out_shape=(shap...  12.1 us
    pallas_call x1, Pallas kernels, prep(): pl.pallas_call(functools.partial(prep_kernel, chips), out_shape=(jax.Shap...  9.28 us
    pallas_call x1, Pallas kernels, scatter_rows(): pl.pallas_call(scatter_kernel, out_shape=jax.ShapeDtypeStruct((rows,) + t...  7.41 us
    ppermute x5, waiting for transfers between devices, body(): other.append(lax.ppermute(value, 'pcol', neighbour))  5.9 us
    select_n x5, other arithmetic, body(): value = jnp.where(place == h, hops_done[h][b], value)  5.3 us
  transfers between devices with their start and end apart: 34, of which 8 were waited for; matrix products, arithmetic and copies ran while one was open for 5% of the time, Pallas kernels for 34%

profile of v2, /device:TPU:30, one launch (start us, length us, event | category | flops | bytes accessed | tf_op | source)
XLA Modules:
  0.0 195.9 jit_solution(9299667716596249693)
XLA Ops:
  0.0 3.9 %shard_map.47 = (bf16[512,512]{1,0:T(8,128)(2,1)S(1)}, bf16[512,512]{1,0:T(8,128)(2,1)}, bf16[512,512]{1,0:T(8,128)(2,1)}, bf16[512,512]{1,0:T(8,128)(2,1)S(1)}, bf16[512,512]{1,0:T(8,128)(2,1)}) custom-call(bf16[2560,2,512]{2,1,0:T(2,128)(2,1)} %bitcast.13), custom_call_target="tpu_custom_call" | custom-call | tf_op jit(solution)/shard_map/pallas_call | solution.py:88
  3.9 1.5 collective-permute-start
  5.6 12.1 %shard_map.46 = (s32[1,1024]{1,0:T(1,128)S(1)}, s32[1,1024]{1,0:T(1,128)S(1)}, s32[1,1024]{1,0:T(1,128)S(1)}, s32[1,1024]{1,0:T(1,128)S(1)}, s32[1,1024]{1,0:T(1,128)S(1)}) custom-call(s32[4]{0:T(128)S(1)} %pad_add_fusion.meta, s32[512,2]{1,0:T(8,128)S(1)} %bitcast.11), custom_call_target="tpu_custom_call" | custom-call | tf_op jit(solution)/shard_map/pallas_call | solution.py:71
  17.7 3.4 %shard_map.48 = (bf16[512,2,512]{2,1,0:T(2,128)(2,1)S(1)}, bf16[512,2,512]{2,1,0:T(2,128)(2,1)S(1)}) custom-call(s32[4]{0:T(128)S(1)} %pad_add_fusion.meta, s32[1,1024]{1,0:T(1,128)S(1)} %get-tuple-element.41.fetch, bf16[2560,2,512]{2,1,0:T(2,128)(2,1)} %bitcast.14), custom_call_target="tpu_custom_call" | custom-call | tf_op jit(solution)/shard_map/pallas_call | solution.py:111
  22.0 1.5 collective-permute-start.3
  23.5 1.5 collective-permute-start.25
  25.0 1.3 collective-permute-start.6
  26.3 3.8 %shard_map.49.refs_0_ = bf16[512,2,512]{2,1,0:T(2,128)(2,1)S(1)} custom-call(s32[4]{0:T(128)S(1)} %pad_add_fusion.meta, s32[1,1024]{1,0:T(1,128)S(1)} %get-tuple-element.41.fetch, s32[1,1024]{1,0:T(1,128)S(1)} %get-tuple-element.42.join, bf16[2560,2,512]{2,1,0:T(2,128)(2,1)} %bitcast.15, bf16[512,2,512]{2,1,0:T(2,128)(2,1)S(1)} %collective-permute-done.10.came), custom_call_target="tpu_custom_call" | custom-call | tf_op jit(solution)/shard_map/pallas_call | solution.py:135
  30.7 1.5 collective-permute-start.1
  32.2 1.5 collective-permute-start.26
  33.7 1.5 collective-permute-start.27
  35.1 17.3 %collective-permute-done.6 = bf16[512,512]{1,0:T(8,128)(2,1)} collective-permute-done((bf16[512,512]{1,0:T(8,128)(2,1)}, bf16[512,512]{1,0:T(8,128)(2,1)}, u32[]{:S(2)}, u32[]{:S(2)}) %collective-permute-start.6) | collective-permute-done | bytes 524320 | tf_op jit(solution)/shard_map/ppermute | solution.py:382
  52.4 1.3 select_select_fusion.3.held
  54.3 1.5 collective-permute-start.2
  55.8 1.5 collective-permute-start.4
  57.2 1.5 collective-permute-start.28
  58.7 1.3 collective-permute-start.29
  61.0 5.9 %collective-permute-done.14.other = bf16[512,512]{1,0:T(8,128)(2,1)} collective-permute-done((bf16[512,512]{1,0:T(8,128)(2,1)S(1)}, bf16[512,512]{1,0:T(8,128)(2,1)}, u32[]{:S(2)}, u32[]{:S(2)}) %collective-permute-start.14) | collective-permute-done | bytes 524320 | tf_op jit(solution)/shard_map/ppermute | solution.py:390
  66.9 1.3 collective-permute-start.18
  68.2 2.1 %pad_maximum_fusion = bf16[2,512,512]{2,1,0:T(8,128)(2,1)} fusion(bf16[1,512,512]{2,1,0:T(8,128)(2,1)} %bitcast.6, bf16[1,512,512]{2,1,0:T(8,128)(2,1)S(1)} %bitcast.9), kind=kLoop, calls=%fused_computation | loop fusion | flops 524288 | bytes 2097152 | tf_op jit(solution)/shard_map/stack | solution.py:429
  70.3 1.3 collective-permute-start.15
  71.6 1.4 collective-permute-start.19
  73.0 1.5 collective-permute-start.5
  74.5 1.3 collective-permute-start.7
  75.8 6.6 %collective-permute-done.29 = bf16[512,512]{1,0:T(8,128)(2,1)} collective-permute-done((bf16[512,512]{1,0:T(8,128)(2,1)}, bf16[512,512]{1,0:T(8,128)(2,1)}, u32[]{:S(2)}, u32[]{:S(2)}) %collective-permute-start.29) | collective-permute-done | bytes 524320 | tf_op jit(solution)/shard_map/ppermute | solution.py:382
  83.6 1.4 collective-permute-start.20
  85.0 1.3 select_select_fusion.held
  86.4 20.8 %collective-permute-done.7 = bf16[512,512]{1,0:T(8,128)(2,1)} collective-permute-done((bf16[512,512]{1,0:T(8,128)(2,1)}, bf16[512,512]{1,0:T(8,128)(2,1)}, u32[]{:S(2)}, u32[]{:S(2)}) %collective-permute-start.7) | collective-permute-done | bytes 524320 | tf_op jit(solution)/shard_map/ppermute | solution.py:382
  107.2 1.3 collective-permute-start.30
  108.5 1.4 collective-permute-done.20
  110.0 3.5 %collective-permute-start.21 = (bf16[256,512]{1,0:T(8,128)(2,1)S(1)}, bf16[256,512]{1,0:T(8,128)(2,1)S(1)}, u32[]{:S(2)}, u32[]{:S(2)}) collective-permute-start(bf16[256,512]{1,0:T(8,128)(2,1)S(1)} %select_select_fusion.5), channel_id=1, source_target_pairs={{8,9},{24,25},{1,0},{17,16},{10,11},{26,27},{3,2},{19,18},{12,13},... | collective-permute-start | bytes 786440 | tf_op jit(solution)/shard_map/ppermute | solution.py:412
  113.5 1.5 broadcast_select_fusion.old
  115.1 1.3 select_select_fusion.1.held
  117.3 1.3 collective-permute-start.8
  118.7 4.1 %collective-permute-done.30 = bf16[512,512]{1,0:T(8,128)(2,1)S(1)} collective-permute-done((bf16[512,512]{1,0:T(8,128)(2,1)}, bf16[512,512]{1,0:T(8,128)(2,1)S(1)}, u32[]{:S(2)}, u32[]{:S(2)}) %collective-permute-start.30) | collective-permute-done | bytes 524320 | tf_op jit(solution)/shard_map/ppermute | solution.py:382
  122.7 1.5 collective-permute-start.22
  124.4 9.6 %collective-permute-done.8 = bf16[512,512]{1,0:T(8,128)(2,1)S(1)} collective-permute-done((bf16[512,512]{1,0:T(8,128)(2,1)}, bf16[512,512]{1,0:T(8,128)(2,1)S(1)}, u32[]{:S(2)}, u32[]{:S(2)}) %collective-permute-start.8) | collective-permute-done | bytes 524320 | tf_op jit(solution)/shard_map/ppermute | solution.py:382
  135.0 1.2 select_select_fusion.4.held
  136.2 7.4 %shard_map.50.tiles = bf16[2568,2,512]{2,1,0:T(2,128)(2,1)} custom-call(s32[4]{0:T(128)S(1)} %pad_add_fusion.meta, s32[1,1024]{1,0:T(1,128)S(1)} %get-tuple-element.40.arrive, s32[1,1024]{1,0:T(1,128)S(1)} %get-tuple-element.30.goal, bf16[512,2,512]{2,1,0:T(2,128)(2,1)S(1)} %collective-permute-done.11.came.refs_1_, ...), custom_call_target="tpu_custom_call" | custom-call | tf_op jit(solution)/shard_map/pallas_call | solution.py:170
  143.7 1.7 collective-permute-start.32
  145.8 1.6 collective-permute-start.9
  147.4 9.3 %shard_map.52 = (bf16[512,1024]{1,0:T(8,128)(2,1)S(1)}, bf16[512,1024]{1,0:T(8,128)(2,1)S(1)}, bf16[512,512]{1,0:T(8,128)(2,1)S(1)}, bf16[1024,2,512]{2,1,0:T(2,128)(2,1)}) custom-call(s32[4]{0:T(128)S(1)} %pad_add_fusion.meta, s32[1024,1]{1,0:T(8,128)S(1)} %copy.12.hops, bf16[2,512,512]{2,1,0:T(8,128)(2,1)S(1)} %copy-done.5, bf16[2,512,512]{2,1,0:T(8,128)(2,1)} %upper.11, ...), custom_call_target="tpu_custom_call" | custom-call | tf_op jit(solution)/shard_map/pallas_call | solution.py:248
  156.7 1.0 copy-done.1
  157.7 7.9 %shard_map.53.rest_0_ = bf16[2560,2,512]{2,1,0:T(2,128)(2,1)} custom-call(s32[4]{0:T(128)S(1)} %pad_add_fusion.meta, s32[2,512]{1,0:T(2,128)S(1)} %reshape.12.goal, bf16[512,512]{1,0:T(8,128)(2,1)S(1)} %select_select_fusion.3.held, bf16[512,512]{1,0:T(8,128)(2,1)} %collective-permute-done.14.other, bf16[2568,2,512]{2,1,0:T(2,128)(2,1)} %shard_map.50.tiles, ...), custom_call_target="tpu_custom_call" | custom-call | flops 2952790016 | bytes 8388608 | tf_op jit(solution)/shard_map/pallas_call | solution.py:330
  165.6 7.6 %shard_map.54.rest_0_ = bf16[2560,2,512]{2,1,0:T(2,128)(2,1)} custom-call(s32[4]{0:T(128)S(1)} %pad_add_fusion.meta, s32[2,512]{1,0:T(2,128)S(1)} %reshape.12.goal, bf16[512,512]{1,0:T(8,128)(2,1)S(1)} %select_select_fusion.held, bf16[512,512]{1,0:T(8,128)(2,1)S(1)} %collective-permute-done.33.other, ...), custom_call_target="tpu_custom_call", output_to_operand_aliasing={{}: (12, {})} | custom-call | flops 2952790016 | bytes 8388608 | tf_op jit(solution)/shard_map/pallas_call | solution.py:330
  173.2 7.6 %shard_map.55.rest_0_ = bf16[2560,2,512]{2,1,0:T(2,128)(2,1)} custom-call(s32[4]{0:T(128)S(1)} %pad_add_fusion.meta, s32[2,512]{1,0:T(2,128)S(1)} %reshape.12.goal, bf16[512,512]{1,0:T(8,128)(2,1)S(1)} %select_select_fusion.1.held, bf16[512,512]{1,0:T(8,128)(2,1)S(1)} %collective-permute-done.32.other, ...), custom_call_target="tpu_custom_call", output_to_operand_aliasing={{}: (12, {})} | custom-call | flops 2952790016 | bytes 8388608 | tf_op jit(solution)/shard_map/pallas_call | solution.py:330
  180.8 7.6 %shard_map.56.rest_0_ = bf16[2560,2,512]{2,1,0:T(2,128)(2,1)} custom-call(s32[4]{0:T(128)S(1)} %pad_add_fusion.meta, s32[2,512]{1,0:T(2,128)S(1)} %reshape.12.goal, bf16[512,512]{1,0:T(8,128)(2,1)S(1)} %select_select_fusion.2.held, bf16[512,512]{1,0:T(8,128)(2,1)S(1)} %collective-permute-done.31.other, ...), custom_call_target="tpu_custom_call", output_to_operand_aliasing={{}: (12, {})} | custom-call | flops 2952790016 | bytes 8388608 | tf_op jit(solution)/shard_map/pallas_call | solution.py:330
  188.3 7.6 %shard_map.57 = bf16[2560,2,512]{2,1,0:T(2,128)(2,1)} custom-call(s32[4]{0:T(128)S(1)} %pad_add_fusion.meta, s32[2,512]{1,0:T(2,128)S(1)} %reshape.12.goal, bf16[512,512]{1,0:T(8,128)(2,1)S(1)} %select_select_fusion.4.held, bf16[512,512]{1,0:T(8,128)(2,1)S(1)} %collective-permute-done.9.other, ...), custom_call_target="tpu_custom_call", output_to_operand_aliasing={{}: (12, {})} | custom-call | flops 2952790016 | bytes 8388608 | tf_op jit(solution)/shard_map/pallas_call | solution.py:330
  (73 shorter events, 7.4 us)
Async XLA Ops:
  0.0 5.3 %copy-start.12 = (s32[2,512]{1,0:T(2,128)S(1)}, s32[2,512]{1,0:T(2,128)}, u32[]{:S(2)}) copy-start(s32[2,512]{1,0:T(2,128)} %param.5) | copy-start | bytes 12292
  3.9 22.4 %copy-start.10 = (bf16[512,512]{1,0:T(8,128)(2,1)}, bf16[512,512]{1,0:T(8,128)(2,1)S(1)}, u32[]{:S(2)}) copy-start(bf16[512,512]{1,0:T(8,128)(2,1)S(1)} %get-tuple-element.33) | copy-start | bytes 1572868
  3.9 28.3 %copy-start.8 = (bf16[512,512]{1,0:T(8,128)(2,1)}, bf16[512,512]{1,0:T(8,128)(2,1)S(1)}, u32[]{:S(2)}) copy-start(bf16[512,512]{1,0:T(8,128)(2,1)S(1)} %get-tuple-element.52) | copy-start | bytes 1572868
  3.9 18.2 %collective-permute-start = (bf16[512,512]{1,0:T(8,128)(2,1)S(1)}, bf16[512,512]{1,0:T(8,128)(2,1)}, u32[]{:S(2)}, u32[]{:S(2)}) collective-permute-start(bf16[512,512]{1,0:T(8,128)(2,1)S(1)} %get-tuple-element.33), channel_id=1, source_target_pairs={{0,2},{1,3},{8,10},{9,11},{16,18},{17,19},{24,26},{25,27}} | collective-permute-start | bytes 1572872 | tf_op jit(solution)/shard_map/ppermute | solution.py:382
  21.1 1.0 copy-start.6
  22.0 4.2 %collective-permute-start.10 = (bf16[512,2,512]{2,1,0:T(2,128)(2,1)S(1)}, bf16[512,2,512]{2,1,0:T(2,128)(2,1)S(1)}, u32[]{:S(2)}, u32[]{:S(2)}) collective-permute-start(bf16[512,2,512]{2,1,0:T(2,128)(2,1)S(1)} %get-tuple-element.43), channel_id=1, source_target_pairs={{0,8},{8,0},{16,24},{24,16},{1,9},{9,1},{17,25},{25,17},{2,10},{10... | collective-permute-start | bytes 3145736 | tf_op jit(solution)/shard_map/ppermute | solution.py:395
  22.0 2.9 %collective-permute-start.3 = (bf16[512,512]{1,0:T(8,128)(2,1)}, bf16[512,512]{1,0:T(8,128)(2,1)}, u32[]{:S(2)}, u32[]{:S(2)}) collective-permute-start(bf16[512,512]{1,0:T(8,128)(2,1)} %collective-permute-done), channel_id=1, source_target_pairs={{2,4},{3,5},{10,12},{11,13},{18,20},{19,21},{26,28},{27,29}} | collective-permute-start | bytes 1572872 | tf_op jit(solution)/shard_map/ppermute | solution.py:382
  23.5 8.7 %collective-permute-start.25 = (bf16[512,512]{1,0:T(8,128)(2,1)}, bf16[512,512]{1,0:T(8,128)(2,1)}, u32[]{:S(2)}, u32[]{:S(2)}) collective-permute-start(bf16[512,512]{1,0:T(8,128)(2,1)} %get-tuple-element.51), channel_id=1, source_target_pairs={{0,2},{1,3},{8,10},{9,11},{16,18},{17,19},{24,26},{25,27}} | collective-permute-start | bytes 1572872 | tf_op jit(solution)/shard_map/ppermute | solution.py:382
  25.0 27.4 %collective-permute-start.6 = (bf16[512,512]{1,0:T(8,128)(2,1)}, bf16[512,512]{1,0:T(8,128)(2,1)}, u32[]{:S(2)}, u32[]{:S(2)}) collective-permute-start(bf16[512,512]{1,0:T(8,128)(2,1)} %collective-permute-done.3), channel_id=1, source_target_pairs={{4,6},{5,7},{12,14},{13,15},{20,22},{21,23},{28,30},{29,31}} | collective-permute-start | bytes 1572872 | tf_op jit(solution)/shard_map/ppermute | solution.py:382
  30.1 56.2 %copy-start.3 = (bf16[512,2,512]{2,1,0:T(2,128)(2,1)}, bf16[512,2,512]{2,1,0:T(2,128)(2,1)S(1)}, u32[]{:S(2)}) copy-start(bf16[512,2,512]{2,1,0:T(2,128)(2,1)S(1)} %shard_map.49.refs_0_) | copy-start | bytes 3145732
  30.1 28.6 %collective-permute-start.11 = (bf16[512,2,512]{2,1,0:T(2,128)(2,1)S(1)}, bf16[512,2,512]{2,1,0:T(2,128)(2,1)S(1)}, u32[]{:S(2)}, u32[]{:S(2)}) collective-permute-start(bf16[512,2,512]{2,1,0:T(2,128)(2,1)S(1)} %shard_map.49.refs_0_), channel_id=1, source_target_pairs={{0,16},{8,24},{16,0},{24,8},{1,17},{9,25},{17,1},{25,9},{2,18},{10... | collective-permute-start | bytes 3145736 | tf_op jit(solution)/shard_map/ppermute | solution.py:397
  30.7 23.5 %collective-permute-start.1 = (bf16[512,512]{1,0:T(8,128)(2,1)}, bf16[512,512]{1,0:T(8,128)(2,1)}, u32[]{:S(2)}, u32[]{:S(2)}) collective-permute-start(bf16[512,512]{1,0:T(8,128)(2,1)} %get-tuple-element.34), channel_id=1, source_target_pairs={{0,2},{1,3},{8,10},{9,11},{16,18},{17,19},{24,26},{25,27}} | collective-permute-start | bytes 1572872 | tf_op jit(solution)/shard_map/ppermute | solution.py:382
  32.2 23.6 %collective-permute-start.26 = (bf16[512,512]{1,0:T(8,128)(2,1)S(1)}, bf16[512,512]{1,0:T(8,128)(2,1)}, u32[]{:S(2)}, u32[]{:S(2)}) collective-permute-start(bf16[512,512]{1,0:T(8,128)(2,1)S(1)} %get-tuple-element.52), channel_id=1, source_target_pairs={{0,2},{1,3},{8,10},{9,11},{16,18},{17,19},{24,26},{25,27}} | collective-permute-start | bytes 1572872 | tf_op jit(solution)/shard_map/ppermute | solution.py:382
  33.7 23.6 %collective-permute-start.27 = (bf16[512,512]{1,0:T(8,128)(2,1)}, bf16[512,512]{1,0:T(8,128)(2,1)}, u32[]{:S(2)}, u32[]{:S(2)}) collective-permute-start(bf16[512,512]{1,0:T(8,128)(2,1)} %collective-permute-done.25), channel_id=1, source_target_pairs={{2,4},{3,5},{10,12},{11,13},{18,20},{19,21},{26,28},{27,29}} | collective-permute-start | bytes 1572872 | tf_op jit(solution)/shard_map/ppermute | solution.py:382
  53.7 13.2 %collective-permute-start.14 = (bf16[512,512]{1,0:T(8,128)(2,1)S(1)}, bf16[512,512]{1,0:T(8,128)(2,1)}, u32[]{:S(2)}, u32[]{:S(2)}) collective-permute-start(bf16[512,512]{1,0:T(8,128)(2,1)S(1)} %select_select_fusion.3.held), channel_id=1, source_target_pairs={{0,1},{1,0},{2,3},{3,2},{4,5},{5,4},{6,7},{7,6},{8,9},{9,8},{10,11... | collective-permute-start | bytes 1572872 | tf_op jit(solution)/shard_map/ppermute | solution.py:390
  54.3 16.0 %collective-permute-start.2 = (bf16[512,512]{1,0:T(8,128)(2,1)}, bf16[512,512]{1,0:T(8,128)(2,1)}, u32[]{:S(2)}, u32[]{:S(2)}) collective-permute-start(bf16[512,512]{1,0:T(8,128)(2,1)} %get-tuple-element.35), channel_id=1, source_target_pairs={{0,2},{1,3},{8,10},{9,11},{16,18},{17,19},{24,26},{25,27}} | collective-permute-start | bytes 1572872 | tf_op jit(solution)/shard_map/ppermute | solution.py:382
  55.8 17.2 %collective-permute-start.4 = (bf16[512,512]{1,0:T(8,128)(2,1)}, bf16[512,512]{1,0:T(8,128)(2,1)}, u32[]{:S(2)}, u32[]{:S(2)}) collective-permute-start(bf16[512,512]{1,0:T(8,128)(2,1)} %collective-permute-done.1), channel_id=1, source_target_pairs={{2,4},{3,5},{10,12},{11,13},{18,20},{19,21},{26,28},{27,29}} | collective-permute-start | bytes 1572872 | tf_op jit(solution)/shard_map/ppermute | solution.py:382
  57.2 17.3 %collective-permute-start.28 = (bf16[512,512]{1,0:T(8,128)(2,1)}, bf16[512,512]{1,0:T(8,128)(2,1)}, u32[]{:S(2)}, u32[]{:S(2)}) collective-permute-start(bf16[512,512]{1,0:T(8,128)(2,1)} %collective-permute-done.26), channel_id=1, source_target_pairs={{2,4},{3,5},{10,12},{11,13},{18,20},{19,21},{26,28},{27,29}} | collective-permute-start | bytes 1572872 | tf_op jit(solution)/shard_map/ppermute | solution.py:382
  58.7 77.5 %copy-start.2 = (bf16[512,2,512]{2,1,0:T(2,128)(2,1)}, bf16[512,2,512]{2,1,0:T(2,128)(2,1)S(1)}, u32[]{:S(2)}) copy-start(bf16[512,2,512]{2,1,0:T(2,128)(2,1)S(1)} %collective-permute-done.11.came.refs_1_) | copy-start | bytes 3145732
  58.7 23.6 %collective-permute-start.29 = (bf16[512,512]{1,0:T(8,128)(2,1)}, bf16[512,512]{1,0:T(8,128)(2,1)}, u32[]{:S(2)}, u32[]{:S(2)}) collective-permute-start(bf16[512,512]{1,0:T(8,128)(2,1)} %collective-permute-done.27), channel_id=1, source_target_pairs={{4,6},{5,7},{12,14},{13,15},{20,22},{21,23},{28,30},{29,31}} | collective-permute-start | bytes 1572872 | tf_op jit(solution)/shard_map/ppermute | solution.py:382
  66.9 4.8 %collective-permute-start.18 = (bf16[256,512]{1,0:T(8,128)(2,1)S(1)}, bf16[256,512]{1,0:T(8,128)(2,1)}, u32[]{:S(2)}, u32[]{:S(2)}) collective-permute-start(bf16[256,512]{1,0:T(8,128)(2,1)S(1)} %shard_map.51), channel_id=1, source_target_pairs={{8,10},{24,26},{1,3},{17,19}} | collective-permute-start | bytes 786440 | tf_op jit(solution)/shard_map/ppermute | solution.py:370
  70.3 39.7 %collective-permute-start.15 = (bf16[2,512,512]{2,1,0:T(8,128)(2,1)}, bf16[2,512,512]{2,1,0:T(8,128)(2,1)}, u32[]{:S(2)}, u32[]{:S(2)}) collective-permute-start(bf16[2,512,512]{2,1,0:T(8,128)(2,1)} %pad_maximum_fusion), channel_id=1, source_target_pairs={{0,16},{8,24},{1,17},{9,25},{2,18},{10,26},{3,19},{11,27},{4,20},{... | collective-permute-start | bytes 3145736 | tf_op jit(solution)/shard_map/ppermute | solution.py:432
  71.6 11.9 %collective-permute-start.19 = (bf16[256,512]{1,0:T(8,128)(2,1)}, bf16[256,512]{1,0:T(8,128)(2,1)}, u32[]{:S(2)}, u32[]{:S(2)}) collective-permute-start(bf16[256,512]{1,0:T(8,128)(2,1)} %collective-permute-done.18), channel_id=1, source_target_pairs={{10,12},{26,28},{3,5},{19,21}} | collective-permute-start | bytes 786440 | tf_op jit(solution)/shard_map/ppermute | solution.py:370
  73.0 13.3 %collective-permute-start.5 = (bf16[512,512]{1,0:T(8,128)(2,1)}, bf16[512,512]{1,0:T(8,128)(2,1)}, u32[]{:S(2)}, u32[]{:S(2)}) collective-permute-start(bf16[512,512]{1,0:T(8,128)(2,1)} %collective-permute-done.2), channel_id=1, source_target_pairs={{2,4},{3,5},{10,12},{11,13},{18,20},{19,21},{26,28},{27,29}} | collective-permute-start | bytes 1572872 | tf_op jit(solution)/shard_map/ppermute | solution.py:382
  74.5 32.7 %collective-permute-start.7 = (bf16[512,512]{1,0:T(8,128)(2,1)}, bf16[512,512]{1,0:T(8,128)(2,1)}, u32[]{:S(2)}, u32[]{:S(2)}) collective-permute-start(bf16[512,512]{1,0:T(8,128)(2,1)} %collective-permute-done.4), channel_id=1, source_target_pairs={{4,6},{5,7},{12,14},{13,15},{20,22},{21,23},{28,30},{29,31}} | collective-permute-start | bytes 1572872 | tf_op jit(solution)/shard_map/ppermute | solution.py:382
  82.3 32.7 %collective-permute-start.13 = (bf16[512,2,512]{2,1,0:T(2,128)(2,1)}, bf16[512,2,512]{2,1,0:T(2,128)(2,1)}, u32[]{:S(2)}, u32[]{:S(2)}) collective-permute-start(bf16[512,2,512]{2,1,0:T(2,128)(2,1)} %copy-done.6), channel_id=1, source_target_pairs={{0,8},{8,0},{16,24},{24,16},{1,9},{9,1},{17,25},{25,17},{2,10},{10... | collective-permute-start | bytes 3145736 | tf_op jit(solution)/shard_map/ppermute | solution.py:398
  83.5 40.7 %copy-start.9 = (bf16[512,512]{1,0:T(8,128)(2,1)S(1)}, bf16[512,512]{1,0:T(8,128)(2,1)}, u32[]{:S(2)}) copy-start(bf16[512,512]{1,0:T(8,128)(2,1)} %copy-done.8) | copy-start | bytes 1572868
  83.6 26.3 %collective-permute-start.20 = (bf16[256,512]{1,0:T(8,128)(2,1)}, bf16[256,512]{1,0:T(8,128)(2,1)S(1)}, u32[]{:S(2)}, u32[]{:S(2)}) collective-permute-start(bf16[256,512]{1,0:T(8,128)(2,1)} %collective-permute-done.19), channel_id=1, source_target_pairs={{12,14},{28,30},{5,7},{21,23}} | collective-permute-start | bytes 786440 | tf_op jit(solution)/shard_map/ppermute | solution.py:370
  86.3 57.3 %collective-permute-start.17 = (bf16[512,2,512]{2,1,0:T(2,128)(2,1)S(1)}, bf16[512,2,512]{2,1,0:T(2,128)(2,1)S(1)}, u32[]{:S(2)}, u32[]{:S(2)}) collective-permute-start(bf16[512,2,512]{2,1,0:T(2,128)(2,1)S(1)} %shard_map.49.refs_0_), channel_id=1, source_target_pairs={{0,8},{8,0},{16,24},{24,16},{1,9},{9,1},{17,25},{25,17},{2,10},{10... | collective-permute-start | bytes 3145736 | tf_op jit(solution)/shard_map/ppermute | solution.py:399
  107.2 15.6 %collective-permute-start.30 = (bf16[512,512]{1,0:T(8,128)(2,1)}, bf16[512,512]{1,0:T(8,128)(2,1)S(1)}, u32[]{:S(2)}, u32[]{:S(2)}) collective-permute-start(bf16[512,512]{1,0:T(8,128)(2,1)} %collective-permute-done.28), channel_id=1, source_target_pairs={{4,6},{5,7},{12,14},{13,15},{20,22},{21,23},{28,30},{29,31}} | collective-permute-start | bytes 1572872 | tf_op jit(solution)/shard_map/ppermute | solution.py:382
  109.9 24.6 %collective-permute-start.12 = (bf16[512,2,512]{2,1,0:T(2,128)(2,1)S(1)}, bf16[512,2,512]{2,1,0:T(2,128)(2,1)S(1)}, u32[]{:S(2)}, u32[]{:S(2)}) collective-permute-start(bf16[512,2,512]{2,1,0:T(2,128)(2,1)S(1)} %collective-permute-done.11.came.refs_1_), channel_id=1, source_target_pairs={{0,8},{8,0},{16,24},{24,16},{1,9},{9,1},{17,25},{25,17},{2,10},{10... | collective-permute-start | bytes 3145736 | tf_op jit(solution)/shard_map/ppermute | solution.py:399
  110.0 26.3 %copy-start.7 = (bf16[512,2,512]{2,1,0:T(2,128)(2,1)S(1)}, bf16[512,2,512]{2,1,0:T(2,128)(2,1)}, u32[]{:S(2)}) copy-start(bf16[512,2,512]{2,1,0:T(2,128)(2,1)} %copy-done.6) | copy-start | bytes 3145732
  110.0 7.3 %collective-permute-start.21 = (bf16[256,512]{1,0:T(8,128)(2,1)S(1)}, bf16[256,512]{1,0:T(8,128)(2,1)S(1)}, u32[]{:S(2)}, u32[]{:S(2)}) collective-permute-start(bf16[256,512]{1,0:T(8,128)(2,1)S(1)} %select_select_fusion.5), channel_id=1, source_target_pairs={{8,9},{24,25},{1,0},{17,16},{10,11},{26,27},{3,2},{19,18},{12,13},... | collective-permute-start | bytes 786440 | tf_op jit(solution)/shard_map/ppermute | solution.py:412
  115.0 42.7 %collective-permute-start.16 = (bf16[2,512,512]{2,1,0:T(8,128)(2,1)S(1)}, bf16[2,512,512]{2,1,0:T(8,128)(2,1)S(1)}, u32[]{:S(2)}, u32[]{:S(2)}) collective-permute-start(bf16[2,512,512]{2,1,0:T(8,128)(2,1)S(1)} %broadcast_select_fusion.old), channel_id=1, source_target_pairs={{0,8},{8,0},{16,24},{24,16},{1,9},{9,1},{17,25},{25,17},{2,10},{10... | collective-permute-start | bytes 3145736 | tf_op jit(solution)/shard_map/ppermute | solution.py:434
  117.3 16.7 %collective-permute-start.8 = (bf16[512,512]{1,0:T(8,128)(2,1)}, bf16[512,512]{1,0:T(8,128)(2,1)S(1)}, u32[]{:S(2)}, u32[]{:S(2)}) collective-permute-start(bf16[512,512]{1,0:T(8,128)(2,1)} %collective-permute-done.5), channel_id=1, source_target_pairs={{4,6},{5,7},{12,14},{13,15},{20,22},{21,23},{28,30},{29,31}} | collective-permute-start | bytes 1572872 | tf_op jit(solution)/shard_map/ppermute | solution.py:382
  122.7 11.8 %collective-permute-start.22 = (bf16[256,512]{1,0:T(8,128)(2,1)S(1)}, bf16[256,512]{1,0:T(8,128)(2,1)S(1)}, u32[]{:S(2)}, u32[]{:S(2)}) collective-permute-start(bf16[256,512]{1,0:T(8,128)(2,1)S(1)} %broadcast_select_fusion.1.refs_4_), channel_id=1, source_target_pairs={{0,16},{8,24},{16,0},{24,8},{1,17},{9,25},{17,1},{25,9},{2,18},{10... | collective-permute-start | bytes 786440 | tf_op jit(solution)/shard_map/ppermute | solution.py:413
  134.1 31.5 %collective-permute-start.33 = (bf16[512,512]{1,0:T(8,128)(2,1)S(1)}, bf16[512,512]{1,0:T(8,128)(2,1)S(1)}, u32[]{:S(2)}, u32[]{:S(2)}) collective-permute-start(bf16[512,512]{1,0:T(8,128)(2,1)S(1)} %select_select_fusion.held), channel_id=1, source_target_pairs={{0,1},{1,0},{2,3},{3,2},{4,5},{5,4},{6,7},{7,6},{8,9},{9,8},{10,11... | collective-permute-start | bytes 1572872 | tf_op jit(solution)/shard_map/ppermute | solution.py:390
  134.5 9.2 %copy-start.4 = (bf16[512,2,512]{2,1,0:T(2,128)(2,1)}, bf16[512,2,512]{2,1,0:T(2,128)(2,1)S(1)}, u32[]{:S(2)}) copy-start(bf16[512,2,512]{2,1,0:T(2,128)(2,1)S(1)} %collective-permute-done.12.came_sibling.refs_3_) | copy-start | bytes 3145732
  134.5 10.9 %collective-permute-start.23 = (bf16[256,512]{1,0:T(8,128)(2,1)S(1)}, bf16[256,512]{1,0:T(8,128)(2,1)S(1)}, u32[]{:S(2)}, u32[]{:S(2)}) collective-permute-start(bf16[256,512]{1,0:T(8,128)(2,1)S(1)} %broadcast_select_fusion.1.refs_4_), channel_id=1, source_target_pairs={{0,8},{8,0},{16,24},{24,16},{1,9},{9,1},{17,25},{25,17},{2,10},{10... | collective-permute-start | bytes 786440 | tf_op jit(solution)/shard_map/ppermute | solution.py:414
  134.5 11.3 %collective-permute-start.24 = (bf16[256,512]{1,0:T(8,128)(2,1)S(1)}, bf16[256,512]{1,0:T(8,128)(2,1)S(1)}, u32[]{:S(2)}, u32[]{:S(2)}) collective-permute-start(bf16[256,512]{1,0:T(8,128)(2,1)S(1)} %collective-permute-done.22.refs_5_), channel_id=1, source_target_pairs={{0,8},{8,0},{16,24},{24,16},{1,9},{9,1},{17,25},{25,17},{2,10},{10... | collective-permute-start | bytes 786440 | tf_op jit(solution)/shard_map/ppermute | solution.py:414
  136.2 11.2 %copy-start.5 = (bf16[2,512,512]{2,1,0:T(8,128)(2,1)S(1)}, bf16[2,512,512]{2,1,0:T(8,128)(2,1)}, u32[]{:S(2)}) copy-start(bf16[2,512,512]{2,1,0:T(8,128)(2,1)} %lower.1) | copy-start | bytes 3145732
  143.7 14.1 %copy-start = (bf16[2,512,512]{2,1,0:T(8,128)(2,1)S(1)}, bf16[2,512,512]{2,1,0:T(8,128)(2,1)}, u32[]{:S(2)}) copy-start(bf16[2,512,512]{2,1,0:T(8,128)(2,1)} %upper.11) | copy-start | bytes 3145732
  143.7 3.7 %copy-start.11 = (bf16[512,2,512]{2,1,0:T(2,128)(2,1)}, bf16[512,2,512]{2,1,0:T(2,128)(2,1)S(1)}, u32[]{:S(2)}) copy-start(bf16[512,2,512]{2,1,0:T(2,128)(2,1)S(1)} %collective-permute-done.17.refs_2_) | copy-start | bytes 3145732
  143.7 29.5 %collective-permute-start.32 = (bf16[512,512]{1,0:T(8,128)(2,1)S(1)}, bf16[512,512]{1,0:T(8,128)(2,1)S(1)}, u32[]{:S(2)}, u32[]{:S(2)}) collective-permute-start(bf16[512,512]{1,0:T(8,128)(2,1)S(1)} %select_select_fusion.1.held), channel_id=1, source_target_pairs={{0,1},{1,0},{2,3},{3,2},{4,5},{5,4},{6,7},{7,6},{8,9},{9,8},{10,11... | collective-permute-start | bytes 1572872 | tf_op jit(solution)/shard_map/ppermute | solution.py:390
  145.3 35.4 %collective-permute-start.31 = (bf16[512,512]{1,0:T(8,128)(2,1)S(1)}, bf16[512,512]{1,0:T(8,128)(2,1)S(1)}, u32[]{:S(2)}, u32[]{:S(2)}) collective-permute-start(bf16[512,512]{1,0:T(8,128)(2,1)S(1)} %select_select_fusion.2.held), channel_id=1, source_target_pairs={{0,1},{1,0},{2,3},{3,2},{4,5},{5,4},{6,7},{7,6},{8,9},{9,8},{10,11... | collective-permute-start | bytes 1572872 | tf_op jit(solution)/shard_map/ppermute | solution.py:390
  145.8 42.6 %collective-permute-start.9 = (bf16[512,512]{1,0:T(8,128)(2,1)S(1)}, bf16[512,512]{1,0:T(8,128)(2,1)S(1)}, u32[]{:S(2)}, u32[]{:S(2)}) collective-permute-start(bf16[512,512]{1,0:T(8,128)(2,1)S(1)} %select_select_fusion.4.held), channel_id=1, source_target_pairs={{0,1},{1,0},{2,3},{3,2},{4,5},{5,4},{6,7},{7,6},{8,9},{9,8},{10,11... | collective-permute-start | bytes 1572872 | tf_op jit(solution)/shard_map/ppermute | solution.py:390
  156.7 1.0 copy-start.1

commit v3 on v0

v3 whole, which is shorter than its diff:
```python
import functools

import jax
import jax.numpy as jnp
from jax import lax
from jax.experimental import pallas as pl
from jax.experimental.pallas import tpu as pltpu
from jax.sharding import PartitionSpec as P

BF16 = jnp.bfloat16
F32 = jnp.float32
I32 = jnp.int32
SMEM = pl.BlockSpec(memory_space=pltpu.SMEM)
VMEM = pl.BlockSpec(memory_space=pltpu.VMEM)
ANY = pl.BlockSpec(memory_space=pl.ANY)
DMA = pltpu.SemaphoreType.DMA


def dot(a, b):
    return jnp.dot(a, b, preferred_element_type=F32)


def flat(rows):
    return rows.reshape(rows.shape[0], rows.shape[1] * rows.shape[2])


def bf16(*shape):
    return jax.ShapeDtypeStruct(shape, BF16)


def call(kernel, operands, outs, after=(), scratch=(), aliases=None, flops=0, moved=0):
    count = len(operands)

    def ordered(*refs):
        kernel(*refs[:count], *refs[count + len(after) :])

    return pl.pallas_call(
        ordered,
        out_shape=tuple(shape for shape, _ in outs),
        in_specs=[spec for _, spec in operands] + [ANY] * len(after),
        out_specs=tuple(spec for _, spec in outs),
        scratch_shapes=list(scratch),
        input_output_aliases=aliases or {},
        compiler_params=pltpu.CompilerParams(vmem_limit_bytes=24 * 1024 * 1024),
        cost_estimate=pl.CostEstimate(flops=flops, bytes_accessed=moved, transcendentals=0),
    )(*[array for array, _ in operands], *after)


def fill_indices(nb, rows, meta, pivots, spread, fetch, join, arrive, goal, hops):
    row, row_devices = meta[0], meta[3]
    chip, chips = row // 2, row_devices // 2
    lanes = spread.shape[2]
    tiles = nb // lanes
    slot = lax.broadcasted_iota(I32, (1, nb), 1)
    pivot0, pivot1 = pivots[0:1, :], pivots[1:2, :]

    def lookup(keys, entry, value):
        parts = [keys[:, t * lanes : (t + 1) * lanes] for t in range(tiles)]

        def add(i, totals):
            begin = pl.multiple_of(i * 8, 8)
            at = begin + lax.broadcasted_iota(I32, (8, lanes), 0)
            here, give = entry(begin, at), value(begin, at)
            return tuple(t + jnp.where(p == here, give, 0) for t, p in zip(totals, parts))

        zero = jnp.zeros((8, lanes), I32)
        totals = lax.fori_loop(0, nb // 8, add, (zero,) * tiles, unroll=8)
        return jnp.concatenate([jnp.sum(t, axis=0, keepdims=True) for t in totals], axis=1)

    def pivot_of(panel):
        return lambda begin, at: spread[panel, pl.ds(begin, 8), :]

    place = lambda begin, at: at + 1
    in_pivots0 = lookup(pivot1, pivot_of(0), place)
    in_pivots1 = lookup(pivot0, pivot_of(1), place)
    top1_in_pivots0 = lookup(nb + slot, pivot_of(0), place)
    over_top1 = lookup(pivot0, lambda begin, at: nb + at, pivot_of(1))
    chained = lookup(nb + in_pivots1 - 1, pivot_of(0), place)

    source0 = pivot0
    source1 = jnp.where(in_pivots0 > 0, in_pivots0 - 1, pivot1)
    second0 = jnp.where(in_pivots1 > 0, jnp.where(chained > 0, chained - 1, nb + in_pivots1 - 1), slot)
    second1 = jnp.where(top1_in_pivots0 > 0, top1_in_pivots0 - 1, nb + slot)
    target0 = jnp.where(over_top1 > 0, over_top1, jnp.where(in_pivots1 > 0, nb + in_pivots1 - 1, pivot0))
    target1 = jnp.where(top1_in_pivots0 > 0, top1_in_pivots0 - 1, pivot1)

    def holder(index):
        return lax.rem(lax.div(index, nb), row_devices)

    def local(index):
        return lax.div(index, nb * row_devices) * nb + lax.rem(index, nb)

    def placed(index):
        mine = (holder(index) == row) & (index >= 2 * nb)
        return jnp.where(mine, local(index), rows)

    for k, (source, second, target) in enumerate(((source0, second0, target0), (source1, second1, target1))):
        from_chip = lax.div(holder(source), 2)
        wanted = jnp.where(from_chip == chip, source, second)
        at = (slice(k, k + 1), slice(None))
        fetch[at] = local(wanted)
        join[at] = jnp.where(holder(wanted) == row, slot, nb)
        arrive[at] = placed(source)
        goal[at] = placed(target)
        hops[at] = lax.rem(chip + chips - from_chip, chips)


def copy_rows(count, target, target_at, origin, origin_at):
    def copy(i, carry):
        target[target_at(i)] = origin[origin_at(i)]
        return carry

    lax.fori_loop(0, count, copy, 0, unroll=16)


def split_kernel(tiles, *pieces):
    chunk, nb = pieces[0].shape
    for i, piece in enumerate(pieces):
        piece[...] = flat(tiles[i * chunk : (i + 1) * chunk])[:, :nb]


def gather_kernel(
    meta, pivots, spread, tiles, send, keep, block0, join, arrive, goal, hops,
    loaded, fetch, fetch_table, load_sem, table_sem,
):
    nb = send.shape[0]
    core = meta[1]
    load = pltpu.make_async_copy(tiles, loaded, load_sem)
    load.start()
    fill_indices(nb, tiles.shape[0], meta, pivots, spread, fetch, join, arrive, goal, hops)
    table = pltpu.make_async_copy(fetch, fetch_table, table_sem)
    table.start()
    table.wait()
    load.wait()
    copy_rows(nb, send, lambda i: i, loaded, lambda i: fetch_table[1 - core, i])
    copy_rows(nb, keep, lambda i: i, loaded, lambda i: fetch_table[core, i])
    block0[...] = loaded[0:nb]


def join_kernel(meta, join, keep, came, joined, work):
    count = came.shape[0]
    core = meta[1]
    work[0:count] = came[...]
    copy_rows(count, work, lambda i: join[core, i], keep, lambda i: i)
    joined[...] = work[0:count]


def scatter_kernel(meta, arrive, goal, came, came_sibling, old, old_sibling, tiles, out, work, sem):
    core, chip = meta[1], meta[0] // 2
    count, rows = old.shape[0], tiles.shape[0]
    load = pltpu.make_async_copy(tiles, work.at[pl.ds(0, rows)], sem)
    load.start()
    load.wait()

    def scatter(table, values, k):
        copy_rows(count, work, lambda i: table[k, i], values, lambda i: i)

    @pl.when(chip == 0)
    def _():
        scatter(goal, old, core)
        scatter(goal, old_sibling, 1 - core)

    @pl.when(chip != 0)
    def _():
        scatter(arrive, came, core)
        scatter(arrive, came_sibling, 1 - core)

    store = pltpu.make_async_copy(work.at[pl.ds(0, rows)], out, sem)
    store.start()
    store.wait()


def relay_kernel(meta, came, own, held):
    place = lax.div(meta[2], 2)

    @pl.when(place == 0)
    def _():
        held[...] = own[...]

    @pl.when(place != 0)
    def _():
        held[...] = came[...]


def pass_kernel(came, held):
    held[...] = came[...]


def old_kernel(line, meta, *refs):
    held, other, old = refs[: len(refs) // 2], refs[len(refs) // 2 : -1], refs[-1]
    place = lax.div(meta[2], 2)
    chunk = held[0].shape[0]
    for h in range(line):

        @pl.when(place == h)
        def _(h=h):
            for p in range(old.shape[1] // chunk):
                old[0, p * chunk : (p + 1) * chunk] = held[p + h][...]
                old[1, p * chunk : (p + 1) * chunk] = other[p + h][...]


def by_chip_kernel(meta, *refs):
    out = refs[-1]
    for h, choice in enumerate(refs[:-1]):

        @pl.when(meta[0] // 2 == h)
        def _(choice=choice):
            out[...] = choice[...]


def by_place_kernel(meta, *refs):
    out = refs[-1]
    for h, choice in enumerate(refs[:-1]):

        @pl.when(lax.div(meta[2], 2) == h)
        def _(choice=choice):
            out[...] = choice[...]


def by_side_kernel(meta, mine, swapped, out):
    needed = 1 - lax.rem(meta[2], 2)

    @pl.when(meta[1] == needed)
    def _():
        out[...] = mine[...]

    @pl.when(meta[1] != needed)
    def _():
        out[...] = swapped[...]


def choose(hop, choices):
    value = flat(choices[0]).astype(F32)
    for h, other in enumerate(choices[1:], 1):
        value = jnp.where(hop == h, flat(other).astype(F32), value)
    return value.astype(BF16)


def fresh_kernel(chips, meta, hops, *refs):
    choices, (fresh, head, brought) = refs[:chips], refs[chips:]
    nb, part = fresh.shape[0], head.shape[0]
    core, chip = meta[1], meta[0] // 2
    fresh[...] = choose(hops[pl.ds(core * nb, nb)], [c[...] for c in choices])
    head[...] = fresh[pl.ds(pl.multiple_of(chip * part, part), part), :nb]
    if chips == 1:
        brought[...] = choices[0][...]
    for h in range(1, chips):

        @pl.when((chip == h) | ((chip == 0) & (h == 1)))
        def _(h=h):
            brought[...] = choices[h][...]


def raw(columns, nb):
    joined = jnp.concatenate(columns, axis=1)
    return joined.reshape(joined.shape[0], len(columns), nb)


def prep0_kernel(meta, lower, fresh, fresh_sibling, up0, top, work):
    core, column = meta[1], meta[2]
    nb = fresh.shape[0]

    @pl.when(core == 0)
    def _():
        work[...] = fresh[...]

    @pl.when(core != 0)
    def _():
        work[...] = fresh_sibling[...]

    shown = []
    for j in range(work.shape[1] // nb):
        cols = slice(j * nb, (j + 1) * nb)
        product = dot(lower[0], work[:, cols])
        show = product
        if j == 0:
            show = jnp.where(column == 0, work[:, cols].astype(F32), product)
            product = jnp.where(column == 0, 0.0, product)
        up0[:, cols] = product.astype(BF16)
        shown.append(show.astype(BF16))
    top[...] = raw(shown, nb)


def prep1_kernel(chips, meta, lower, upper, fresh, fresh_sibling, up0, *refs):
    heads, heads_sibling = refs[:chips], refs[chips : 2 * chips]
    up1, up0_panel, top, work, head = refs[2 * chips :]
    core, column, chip = meta[1], meta[2], meta[0] // 2
    nb, part = fresh.shape[0], heads[0].shape[0]
    for who, pieces in ((core, heads), (1 - core, heads_sibling)):
        for h, piece in enumerate(pieces):
            at = pl.multiple_of(lax.rem(chip + chips - h, chips) * part, part)
            head[who, pl.ds(at, part)] = piece[...]

    @pl.when(core == 1)
    def _():
        work[...] = fresh[...]

    @pl.when(core != 1)
    def _():
        work[...] = fresh_sibling[...]

    up0_panel[...] = dot(lower[0], head[0]).astype(BF16)
    factor = dot(head[1], upper[0]).astype(BF16)
    in_panel, next_panel = column == 0, column == 1
    shown = []
    for j in range(work.shape[1] // nb):
        cols = slice(j * nb, (j + 1) * nb)
        updated = (work[:, cols].astype(F32) - dot(factor, up0[:, cols])).astype(BF16)
        last = dot(lower[1], updated)
        show = last
        if j == 0:
            show = jnp.where(next_panel, updated.astype(F32), show)
            show = jnp.where(in_panel, factor.astype(F32), show)
            last = jnp.where(in_panel | next_panel, 0.0, last)
        up1[:, cols] = last.astype(BF16)
        shown.append(show.astype(BF16))
    top[...] = raw(shown, nb)


def update_kernel(
    first, count, line, meta, goal, old, old_sibling, upper, up0, up1, up0_panel, tiles, top0, top1, *rest
):
    spans = count + line - 1
    held, other = rest[:spans], rest[spans : 2 * spans]
    out, token, panels, block, result, panel_sem, block_sem, out_sem = rest[-8:]
    row, core, column, row_devices = meta[0], meta[1], meta[2], meta[3]
    side, place = lax.rem(column, 2), lax.div(column, 2)
    _, chunk, cb, nb = block.shape
    per_block = nb // chunk
    rows_of = lambda i: pl.ds((first + i) * chunk, chunk)

    def block_copy(i):
        return pltpu.make_async_copy(tiles.at[rows_of(i)], block.at[i], block_sem.at[i])

    def panel_copy(i, h, which):
        source = (held, other)[which][i + h]
        return pltpu.make_async_copy(source, panels.at[i, lax.rem(side + which, 2)], panel_sem.at[i, which])

    for i in range(count):
        block_copy(i).start()
        for h in range(line):

            @pl.when(place == h)
            def _(h=h, i=i):
                panel_copy(i, h, 0).start()
                panel_copy(i, h, 1).start()

    def from_factors(i):
        here = (first + i) * chunk + lax.broadcasted_iota(I32, (chunk, nb), 0)
        pick = jnp.where(here == goal[pl.ds(core, 1), :], 1.0, 0.0)
        pick_sibling = jnp.where(here == goal[pl.ds(1 - core, 1), :], 1.0, 0.0)
        moved = jnp.sum(pick + pick_sibling, axis=1, keepdims=True) > 0.5
        pick, pick_sibling = pick.astype(BF16), pick_sibling.astype(BF16)
        whole = []
        for k in range(2):
            which = lax.rem(k + side, 2)
            brought = dot(pick, old[which]) + dot(pick_sibling, old_sibling[which])
            whole.append(jnp.where(moved, brought, panels[i, k].astype(F32)))
        factor0 = dot(whole[0].astype(BF16), upper[0]).astype(BF16)
        below = (whole[1] - dot(factor0, up0_panel[...])).astype(BF16)
        factor1 = dot(below, upper[1]).astype(BF16)
        values = flat(block[i])
        columns = []
        for j in range(cb):
            cols = slice(j * nb, (j + 1) * nb)
            value = values[:, cols].astype(F32) - dot(factor0, up0[:, cols])
            value = value.astype(BF16).astype(F32) - dot(factor1, up1[:, cols])
            if j == 0:
                value = jnp.where(column == 0, factor0.astype(F32), value)
                value = jnp.where(column == 1, factor1.astype(F32), value)
            columns.append(value.astype(BF16))
        result[i] = raw(columns, nb)

    def out_copy(i):
        return pltpu.make_async_copy(result.at[i], out.at[rows_of(i)], out_sem.at[i])

    for i in range(count):
        block_copy(i).wait()
        panel_copy(i, 0, 0).wait()
        panel_copy(i, 0, 1).wait()
    for i in range(count):
        panel_row = (first + i) // per_block * row_devices + row
        if first + i < per_block:
            inside = pl.ds((first + i) * chunk, chunk)

            @pl.when(panel_row == 0)
            def _(i=i, inside=inside):
                copy = pltpu.make_async_copy(top0.at[inside], result.at[i], block_sem.at[i])
                copy.start()
                copy.wait()

            @pl.when(panel_row == 1)
            def _(i=i, inside=inside):
                copy = pltpu.make_async_copy(top1.at[inside], result.at[i], block_sem.at[i])
                copy.start()
                copy.wait()

            pl.when(panel_row >= 2)(functools.partial(from_factors, i))
        else:
            from_factors(i)
        out_copy(i).start()
    token[...] = jnp.zeros(token.shape, F32)
    for i in range(count):
        out_copy(i).wait()


def body(matrix, pivots, lower, upper):
    rb, nb, cb, _ = matrix.shape
    rows = rb * nb
    chunk = nb // 2
    pieces = rows // chunk
    row_devices = lax.axis_size("prow")
    col_devices = lax.axis_size("pcol")
    chips, line = row_devices // 2, col_devices // 2
    row = lax.axis_index("prow").astype(I32)
    column = lax.axis_index("pcol").astype(I32)
    meta = jnp.stack([row, row % 2, column, jnp.int32(row_devices)])
    tiles = matrix.reshape(rows, cb, nb)

    def to_sibling(value):
        return lax.ppermute(value, "prow", [(r, r ^ 1) for r in range(row_devices)])

    def to_neighbour(value):
        return lax.ppermute(value, "pcol", [(c, c ^ 1) for c in range(col_devices)])

    def to_chip(value, h):
        return lax.ppermute(value, "prow", [(r, (r + 2 * h) % row_devices) for r in range(row_devices)])

    def to_next(value):
        return lax.ppermute(value, "pcol", [(c, (c + 2) % col_devices) for c in range(col_devices)])

    order = []

    def run(kernel, operands, outs, also=(), **kwargs):
        after = tuple(order[-1:]) + tuple(also)
        results = call(kernel, operands, outs, after=after, **kwargs)
        order.append(results[-1])
        return results

    state = {}
    own = run(split_kernel, [(tiles, VMEM)], [(bf16(chunk, nb), VMEM)] * pieces)
    held, other, came = [], [], None

    def advance(step):
        nonlocal came
        if step == 0:
            piece = own[0]
        else:
            also = (other[step - 2],) if step >= 2 else ()
            out = [(bf16(chunk, nb), VMEM)]
            if step < pieces:
                operands = [(meta, SMEM), (came, VMEM), (own[step], VMEM)]
                (piece,) = run(relay_kernel, operands, out, also)
            else:
                (piece,) = run(pass_kernel, [(came, VMEM)], out, also)
        held.append(piece)
        if step < pieces + line - 2:
            came = to_next(piece)
        other.append(to_neighbour(piece))

    def gather():
        lanes = min(nb, 128)
        spread = jnp.broadcast_to(pivots[:, :, None], (2, nb, lanes))
        table = jax.ShapeDtypeStruct((2, nb), I32)
        send, keep, block0, join, arrive, goal, hops = run(
            gather_kernel,
            [(meta, SMEM), (pivots, VMEM), (spread, VMEM), (tiles, ANY)],
            [(bf16(nb, cb, nb), VMEM)] * 3 + [(table, VMEM)] * 4,
            scratch=[
                pltpu.VMEM(tiles.shape, BF16), pltpu.VMEM((2, nb), I32), pltpu.SMEM((2, nb), I32), DMA, DMA,
            ],
        )
        state.update(keep=keep, block0=block0, join=join, arrive=arrive, goal=goal)
        state["hops"] = hops.reshape(2 * nb, 1)
        state["sent"] = to_sibling(send)
        state["block0_sibling"] = to_sibling(block0)

    def join():
        (joined,) = run(
            join_kernel,
            [(meta, SMEM), (state["join"], SMEM), (state["keep"], VMEM), (state["sent"], VMEM)],
            [(bf16(nb, cb, nb), VMEM)],
            scratch=[pltpu.VMEM((nb + 8, cb, nb), BF16)],
        )
        state["choices"] = [joined] + [to_chip(joined, h) for h in range(1, chips)]

    flat_index = lambda r, c: r * col_devices + c
    both = ("prow", "pcol")
    part = nb // chips

    def fresh():
        new, head, brought = run(
            functools.partial(fresh_kernel, chips),
            [(meta, SMEM), (state["hops"], VMEM)] + [(c, VMEM) for c in state["choices"]],
            [(bf16(nb, cb * nb), VMEM), (bf16(part, nb), VMEM), (bf16(nb, cb, nb), VMEM)],
        )
        state["head"] = [head]
        for h in range(1, line):
            pairs = [
                (flat_index(r, c), flat_index(r, c + 2 * h))
                for c in range(2) for r in range(row_devices) if r % 2 != c
            ]
            state["head"].append(lax.ppermute(head, both, pairs))
        state["brought"] = (brought, to_sibling(brought))
        state["fresh"] = (new, to_sibling(new))

    def old():
        spans = range(nb // chunk + line - 1)
        (mine,) = run(
            functools.partial(old_kernel, line),
            [(meta, SMEM)] + [(held[i], VMEM) for i in spans] + [(other[i], VMEM) for i in spans],
            [(bf16(2, nb, nb), VMEM)],
        )
        state["old"] = [mine] + [to_chip(mine, h) for h in range(1, chips)]

    def old_here():
        (mine,) = run(
            by_chip_kernel, [(meta, SMEM)] + [(v, VMEM) for v in state["old"]], [(bf16(2, nb, nb), VMEM)]
        )
        state["old"] = (mine, to_sibling(mine))

    def head_here():
        (mine,) = run(
            by_place_kernel, [(meta, SMEM)] + [(v, VMEM) for v in state["head"]], [(bf16(part, nb), VMEM)]
        )
        pairs = [
            (flat_index(r, c), flat_index(r, c ^ 1))
            for c in range(col_devices) for r in range(row_devices) if r % 2 != c % 2
        ]
        state["head"] = (mine, lax.ppermute(mine, both, pairs))

    def head_around():
        (mine,) = run(
            by_side_kernel, [(meta, SMEM)] + [(v, VMEM) for v in state["head"]], [(bf16(part, nb), VMEM)]
        )
        heads = [mine] + [to_chip(mine, h) for h in range(1, chips)]
        state["heads"] = heads + [to_sibling(v) for v in heads]

    def scatter():
        sources = state["brought"] + (state["block0"], state["block0_sibling"])
        (state["moved"],) = run(
            scatter_kernel,
            [(meta, SMEM), (state["arrive"], SMEM), (state["goal"], SMEM)]
            + [(v, VMEM) for v in sources] + [(tiles, ANY)],
            [(bf16(rows, cb, nb), ANY)],
            scratch=[pltpu.VMEM((rows + 8, cb, nb), BF16), DMA],
        )

    def prep0():
        state["up0"], state["top0"] = run(
            prep0_kernel,
            [(meta, SMEM), (lower, VMEM)] + [(v, VMEM) for v in state["fresh"]],
            [(bf16(nb, cb * nb), VMEM), (bf16(nb, cb, nb), VMEM)],
            scratch=[pltpu.VMEM((nb, cb * nb), BF16)],
        )

    def prep1():
        state["up1"], state["up0_panel"], state["top1"] = run(
            functools.partial(prep1_kernel, chips),
            [(meta, SMEM), (lower, VMEM), (upper, VMEM)] + [(v, VMEM) for v in state["fresh"]]
            + [(state["up0"], VMEM)] + [(v, VMEM) for v in state["heads"]],
            [(bf16(nb, cb * nb), VMEM), (bf16(nb, nb), VMEM), (bf16(nb, cb, nb), VMEM)],
            scratch=[pltpu.VMEM((nb, cb * nb), BF16), pltpu.VMEM((2, nb, nb), BF16)],
        )

    def update(first, count):
        spans = range(first, first + count + line - 1)
        operands = [(meta, SMEM), (state["goal"], VMEM)] + [(v, VMEM) for v in state["old"]] + [(upper, VMEM)]
        operands += [(state[name], VMEM) for name in ("up0", "up1", "up0_panel")]
        operands += [(state[name], ANY) for name in ("moved", "top0", "top1")]
        operands += [(held[i], ANY) for i in spans] + [(other[i], ANY) for i in spans]
        aliases = {}
        if "result" in state:
            aliases = {len(operands): 0}
            operands.append((state["result"], ANY))
        state["result"], _ = run(
            functools.partial(update_kernel, first, count, line),
            operands,
            [(bf16(rows, cb, nb), ANY), (jax.ShapeDtypeStruct((8, 128), F32), VMEM)],
            scratch=[
                pltpu.VMEM((count, 2, chunk, nb), BF16),
                pltpu.VMEM((count, chunk, cb, nb), BF16),
                pltpu.VMEM((count, chunk, cb, nb), BF16),
                DMA((count, 2)), DMA((count,)), DMA((count,)),
            ],
            aliases=aliases,
            flops=2 * count * chunk * nb * nb * (7 + 2 * cb),
        )

    plan = [(0, gather), (1, join), (5, fresh), (max(5, line), old), (6, head_here), (6, scatter), (7, head_around)]
    plan += [(7, prep0), (8, old_here), (9, prep1)]
    group = 2
    for first in range(0, pieces, group):
        count = min(group, pieces - first)
        plan.append((max(9 + first // group, first + count + line - 2), functools.partial(update, first, count)))
    last = pieces + line - 2
    for step in range(last + 1):
        advance(step)
        while plan and (plan[0][0] <= step or step == last):
            plan.pop(0)[1]()
    return state["result"].reshape(matrix.shape)


def solution(mesh):
    placed = (P(None, "prow", None, "pcol"), P(), P(), P())
    return jax.shard_map(
        body, mesh=mesh, in_specs=placed, out_specs=P(None, "prow", None, "pcol"), check_vma=False
    )
```

time: 463 us -> 167 us (0.36)
  waiting for transfers between devices: 323 us -> 58.2 us
  local copies, waits for them, and re-layouts: 71.9 us -> 10.3 us
  Pallas kernels: 0 us -> 59.7 us
  starting transfers between devices: 0.31 us -> 35.7 us
  matrix products: 33.3 us -> 0 us
  other arithmetic: 20.9 us -> 0.08 us
  between operations: 13.3 us -> 0.89 us
    psum x4 -> x0, waiting for transfers between devices: 323 us -> none  [the longest x2 218 us: from_root(): return lax.psum(kept, axis)]
    pallas_call x0 -> x28, Pallas kernels: none -> 59.7 us  [call(): pl.pallas_call(ordered, out_shape=tuple((shape for shape, _ in outs)), in...]
    ppermute x0 -> x39, waiting for transfers between devices: none -> 58.2 us  [the longest x12 43.7 us: to_next(): lax.ppermute(value, 'pcol', [(c, (c + 2) % col_devices) for c in range(co...]
    ppermute x0 -> x39, starting transfers between devices: none -> 35.7 us  [the longest x13 23.5 us: to_neighbour(): return lax.ppermute(value, 'pcol', [(c, c ^ 1) for c in range(col_devices)])]
    dot_general x6 -> x0, matrix products: 33.3 us -> none  [the longest x2 20.2 us: body(): update = jnp.dot(factor, top_product, preferred_element_type=jnp.float32)]
    gather x4 -> x0, local copies, waits for them, and re-layouts: 30 us -> none  [the longest x2 16.3 us: collect_rows(): picked = jnp.take(local_tiles, position, axis=0)]
    scatter x2 -> x0, local copies, waits for them, and re-layouts: 23.6 us -> none  [place_rows(): return local_tiles.at[position].set(values, mode='drop')]
    scatter x4 -> x0, other arithmetic: 14.4 us -> none  [the longest x2 8.96 us: body(): local_tiles.at[:, col_start:col_start + block_width].set(new_panel)]
  transfers between devices with their start and end apart: 4 -> 39, of which waited for: 4 -> 14; matrix products, arithmetic and copies ran while one was open for 3% -> 1% of each run, Pallas kernels for 0% -> 26%
where the time goes in v3:
time: 167 us; the launch traced here: 165 us
  Pallas kernels  59.7 us (36%)
  waiting for transfers between devices  58.2 us (35%)
  starting transfers between devices  35.7 us (21%)
  local copies, waits for them, and re-layouts  10.3 us (6%)
    pallas_call x28, Pallas kernels, call(): pl.pallas_call(ordered, out_shape=tuple((shape for shape, _ in outs)), in...  59.7 us
    ppermute x12, waiting for transfers between devices, to_next(): lax.ppermute(value, 'pcol', [(c, (c + 2) % col_devices) for c in range(co...  43.7 us
    ppermute x13, starting transfers between devices, to_neighbour(): return lax.ppermute(value, 'pcol', [(c, c ^ 1) for c in range(col_devices)])  23.5 us
    unnamed x50, local copies, waits for them, and re-layouts  10.1 us
    ppermute x13, waiting for transfers between devices, to_neighbour(): return lax.ppermute(value, 'pcol', [(c, c ^ 1) for c in range(col_devices)])  7.47 us
    ppermute x3, waiting for transfers between devices, to_chip(): lax.ppermute(value, 'prow', [(r, (r + 2 * h) % row_devices) for r in rang...  6.99 us
    ppermute x12, starting transfers between devices, to_next(): lax.ppermute(value, 'pcol', [(c, (c + 2) % col_devices) for c in range(co...  4.33 us
    ppermute x3, starting transfers between devices, to_chip(): lax.ppermute(value, 'prow', [(r, (r + 2 * h) % row_devices) for r in rang...  3.84 us
  transfers between devices with their start and end apart: 39, of which 14 were waited for; matrix products, arithmetic and copies ran while one was open for 1% of the time, Pallas kernels for 26%

profile of v3, /device:TPU:0, one launch (start us, length us, event | category | flops | bytes accessed | tf_op | source)
XLA Modules:
  0.0 164.9 jit_solution(6810794041956585117)
XLA Ops:
  0.0 2.5 %copy-done = bf16[5,512,2,512]{3,2,1,0:T(2,128)(2,1)S(1)} copy-done((bf16[5,512,2,512]{3,2,1,0:T(2,128)(2,1)S(1)}, bf16[5,512,2,512]{3,2,1,0:T(2,128)(2,1)}, u32[]{:S(2)}) %copy-start) | copy-done | bytes 5242904
  3.2 0.7 copy-done.7
  4.2 2.8 %copy-done.1 = bf16[5,512,2,512]{3,2,1,0:T(2,128)(2,1)S(1)} copy-done((bf16[5,512,2,512]{3,2,1,0:T(2,128)(2,1)S(1)}, bf16[5,512,2,512]{3,2,1,0:T(2,128)(2,1)}, u32[]{:S(2)}) %copy-start.1) | copy-done | bytes 5242904
  7.0 8.0 %shard_map.47 = (bf16[512,2,512]{2,1,0:T(2,128)(2,1)S(1)}, bf16[512,2,512]{2,1,0:T(2,128)(2,1)S(1)}, bf16[512,2,512]{2,1,0:T(2,128)(2,1)}, s32[2,512]{1,0:T(2,12...) custom-call(s32[4]{0:T(128)S(1)} %pad_add_fusion.refs_0_, s32[2,512]{1,0:T(2,128)S(1)} %copy-done.21, ...), custom_call_target="tpu_custom_call" | custom-call | tf_op jit(solution)/shard_map/pallas_call | solution.py:37
  15.5 2.6 %collective-permute-start = (bf16[256,512]{1,0:T(8,128)(2,1)S(1)}, bf16[256,512]{1,0:T(8,128)(2,1)S(1)}, u32[]{:S(2)}, u32[]{:S(2)}) collective-permute-start(bf16[256,512]{1,0:T(8,128)(2,1)S(1)} %get-tuple-element.41.refs_1_.refs_11_), channel_id=1, source_target_pairs={{0,2},{1,3},{2,4},{3,5},{4,6},{5,7},{6,0},{7,1},{8,10},{9,11},{10,... | collective-permute-start | bytes 786440 | tf_op jit(solution)/shard_map/ppermute | solution.py:430
  18.2 1.5 collective-permute-start.3
  19.7 7.4 %collective-permute-done.refs_1_ = bf16[256,512]{1,0:T(8,128)(2,1)S(1)} collective-permute-done((bf16[256,512]{1,0:T(8,128)(2,1)S(1)}, bf16[256,512]{1,0:T(8,128)(2,1)S(1)}, u32[]{:S(2)}, u32[]{:S(2)}) %collective-permute-start) | collective-permute-done | bytes 262176 | tf_op jit(solution)/shard_map/ppermute | solution.py:430
  27.8 2.3 %shard_map.49.refs_3_.refs_2_ = bf16[512,2,512]{2,1,0:T(2,128)(2,1)S(1)} custom-call(s32[4]{0:T(128)S(1)} %pad_add_fusion.refs_0_, s32[2,512]{1,0:T(2,128)S(1)} %get-tuple-element.45.refs_1_, bf16[512,2,512]{2,1,0:T(2,128)(2,1)S(1)} %get-tuple-element.46.refs_2_, bf16[512,2,512]{2,1,0:T(2,128)(2,1)S(1)} %collective-permute-done.2.refs_3_, ...), custom_call_target="tpu_custom_call" | custom-call | tf_op jit(solution)/shard_map/pallas_call | solution.py:37
  30.1 1.6 collective-permute-start.10
  31.6 1.5 collective-permute-start.5
  33.2 4.4 %collective-permute-done.1.refs_1_ = bf16[256,512]{1,0:T(8,128)(2,1)S(1)} collective-permute-done((bf16[256,512]{1,0:T(8,128)(2,1)S(1)}, bf16[256,512]{1,0:T(8,128)(2,1)S(1)}, u32[]{:S(2)}, u32[]{:S(2)}) %collective-permute-start.1) | collective-permute-done | bytes 262176 | tf_op jit(solution)/shard_map/ppermute | solution.py:430
  37.6 0.9 copy-done.20
  39.3 1.4 collective-permute-start.7
  40.7 7.5 %collective-permute-done.4.refs_1_ = bf16[256,512]{1,0:T(8,128)(2,1)S(1)} collective-permute-done((bf16[256,512]{1,0:T(8,128)(2,1)S(1)}, bf16[256,512]{1,0:T(8,128)(2,1)S(1)}, u32[]{:S(2)}, u32[]{:S(2)}) %collective-permute-start.4) | collective-permute-done | bytes 262176 | tf_op jit(solution)/shard_map/ppermute | solution.py:430
  48.8 1.3 collective-permute-start.8
  50.1 6.9 %collective-permute-done.6.refs_1_ = bf16[256,512]{1,0:T(8,128)(2,1)S(1)} collective-permute-done((bf16[256,512]{1,0:T(8,128)(2,1)S(1)}, bf16[256,512]{1,0:T(8,128)(2,1)S(1)}, u32[]{:S(2)}, u32[]{:S(2)}) %collective-permute-start.6) | collective-permute-done | bytes 262176 | tf_op jit(solution)/shard_map/ppermute | solution.py:430
  57.7 1.0 copy.11
  58.7 7.2 %collective-permute-done.11.refs_1_ = bf16[256,512]{1,0:T(8,128)(2,1)} collective-permute-done((bf16[256,512]{1,0:T(8,128)(2,1)S(1)}, bf16[256,512]{1,0:T(8,128)(2,1)}, u32[]{:S(2)}, u32[]{:S(2)}) %collective-permute-start.11) | collective-permute-done | bytes 262176 | tf_op jit(solution)/shard_map/ppermute | solution.py:430
  65.9 0.9 copy-done.14
  66.9 1.0 shard_map.53.refs_4_.refs_14_.refs_12_
  67.9 1.0 copy-done.4
  68.9 2.3 %shard_map.54 = (bf16[512,1024]{1,0:T(8,128)(2,1)S(1)}, bf16[256,512]{1,0:T(8,128)(2,1)S(1)}, bf16[512,2,512]{2,1,0:T(2,128)(2,1)S(1)}) custom-call(s32[4]{0:T(128)S(1)} %pad_add_fusion.refs_0_, s32[1024,1]{1,0:T(8,128)S(1)} %bitcast.14, bf16[512,2,512]{2,1,0:T(2,128)(2,1)S(1)} %shard_map.49.refs_3_.refs_2_, ...), custom_call_target="tpu_custom_call" | custom-call | tf_op jit(solution)/shard_map/pallas_call | solution.py:37
  71.3 1.3 collective-permute-start.9
  73.3 6.8 %collective-permute-done.9.refs_10_.refs_4_.refs_20_.refs_18_.refs_16_ = bf16[256,512]{1,0:T(8,128)(2,1)S(1)} collective-permute-done((bf16[256,512]{1,0:T(8,128)(2,1)S(1)}, bf16[256,512]{1,0:T(8,128)(2,1)S(1)}, u32[]{:S(2)}, u32[]{:S(2)}) %collective-permute-start.9) | collective-permute-done | bytes 262176 | tf_op jit(solution)/shard_map/ppermute | solution.py:424
  80.7 1.3 collective-permute-start.12
  82.0 0.8 collective-permute-done.13.refs_1_
  84.8 4.0 %collective-permute-start.20 = (bf16[256,512]{1,0:T(8,128)(2,1)S(1)}, bf16[256,512]{1,0:T(8,128)(2,1)S(1)}, u32[]{:S(2)}, u32[]{:S(2)}) collective-permute-start(bf16[256,512]{1,0:T(8,128)(2,1)S(1)} %shard_map.53.refs_4_.refs_14_.refs_12_), channel_id=1, source_target_pairs={{0,1},{1,0},{2,3},{3,2},{4,5},{5,4},{6,7},{7,6},{8,9},{9,8},{10,11... | collective-permute-start | bytes 786440 | tf_op jit(solution)/shard_map/ppermute | solution.py:424
  89.4 1.3 collective-permute-start.23
  90.7 5.4 %shard_map.58.refs_3_.refs_8_ = bf16[2560,2,512]{2,1,0:T(2,128)(2,1)S(1)} custom-call(s32[4]{0:T(128)S(1)} %pad_add_fusion.refs_0_, s32[2,512]{1,0:T(2,128)S(1)} %get-tuple-element.54.refs_1_, s32[2,512]{1,0:T(2,128)S(1)} %get-tuple-element.40.refs_2_.refs_1_, bf16[512,2,512]{2,1,0:T(2,128)(2,1)S(1)} %get-tuple-element.51.refs_11_.refs_3_, ...), custom_call_target="tpu_custom_call" | custom-call | tf_op jit(solution)/shard_map/pallas_call | solution.py:37
  96.2 5.5 %collective-permute-start.24 = (bf16[256,512]{1,0:T(8,128)(2,1)S(1)}, bf16[256,512]{1,0:T(8,128)(2,1)S(1)}, u32[]{:S(2)}, u32[]{:S(2)}) collective-permute-start(bf16[256,512]{1,0:T(8,128)(2,1)S(1)} %shard_map.56.refs_5_.refs_15_.refs_13_.refs_11_), channel_id=1, source_target_pairs={{0,1},{1,0},{2,3},{3,2},{4,5},{5,4},{6,7},{7,6},{8,9},{9,8},{10,11... | collective-permute-start | bytes 786440 | tf_op jit(solution)/shard_map/ppermute | solution.py:424
  102.2 1.3 collective-permute-start.21
  104.1 2.0 %shard_map.61 = (bf16[512,1024]{1,0:T(8,128)(2,1)S(1)}, bf16[512,2,512]{2,1,0:T(2,128)(2,1)S(1)}) custom-call(s32[4]{0:T(128)S(1)} %pad_add_fusion.refs_0_, bf16[2,512,512]{2,1,0:T(8,128)(2,1)S(1)} %copy-done.3, bf16[512,1024]{1,0:T(8,128)(2,1)S(1)} %get-tuple-element.58.refs_2_.refs_3_, bf16[512,1024]{1,0:T(8,128)(2,1)S(1)} %collective-permute-done.22.refs_3_.refs_4_, ...), custom_call_target="tpu_custom_call" | custom-call | tf_op jit(solution)/shard_map/pallas_call | solution.py:37
  106.1 4.8 %collective-permute-done.21.refs_1_ = bf16[256,512]{1,0:T(8,128)(2,1)S(1)} collective-permute-done((bf16[256,512]{1,0:T(8,128)(2,1)S(1)}, bf16[256,512]{1,0:T(8,128)(2,1)S(1)}, u32[]{:S(2)}, u32[]{:S(2)}) %collective-permute-start.21) | collective-permute-done | bytes 262176 | tf_op jit(solution)/shard_map/ppermute | solution.py:430
  112.2 1.0 collective-permute-start.26
  113.2 0.7 collective-permute-start.30
  114.0 7.0 %collective-permute-done.26.refs_7_ = bf16[256,512]{1,0:T(8,128)(2,1)S(1)} collective-permute-done((bf16[256,512]{1,0:T(8,128)(2,1)S(1)}, bf16[256,512]{1,0:T(8,128)(2,1)S(1)}, u32[]{:S(2)}, u32[]{:S(2)}) %collective-permute-start.26) | collective-permute-done | bytes 262176 | tf_op jit(solution)/shard_map/ppermute | solution.py:427
  122.3 1.5 collective-permute-done.29.refs_1_
  124.5 1.4 collective-permute-start.34
  125.9 3.5 %shard_map.65 = (bf16[512,1024]{1,0:T(8,128)(2,1)S(1)}, bf16[512,512]{1,0:T(8,128)(2,1)S(1)}, bf16[512,2,512]{2,1,0:T(2,128)(2,1)S(1)}) custom-call(s32[4]{0:T(128)S(1)} %pad_add_fusion.refs_0_, bf16[2,512,512]{2,1,0:T(8,128)(2,1)S(1)} %copy-done.3, bf16[2,512,512]{2,1,0:T(8,128)(2,1)S(1)} %copy-done.2, ...), custom_call_target="tpu_custom_call" | custom-call | tf_op jit(solution)/shard_map/pallas_call | solution.py:37
  129.4 1.8 %shard_map.66 = (bf16[2560,2,512]{2,1,0:T(2,128)(2,1)}, f32[8,128]{1,0:T(8,128)S(1)}) custom-call(s32[4]{0:T(128)S(1)} %pad_add_fusion.refs_0_, s32[2,512]{1,0:T(2,128)S(1)} %get-tuple-element.40.refs_2_.refs_1_, bf16[2,512,512]{2,1,0:T(8,128)(2,1)S(1)} %shard_map.63.refs_3_.refs_2_, bf16[2,512,512]{2,1,0:T(8,128)(2,1)S(1)} %collective-permute-done.25.refs_3_, ...), custom_call_target="tpu_custom_call" | custom-call | flops 2952790016 | tf_op jit(solution)/shard_map/pallas_call | solution.py:37
  131.2 2.3 %collective-permute-done.31.refs_0_ = bf16[256,512]{1,0:T(8,128)(2,1)S(1)} collective-permute-done((bf16[256,512]{1,0:T(8,128)(2,1)S(1)}, bf16[256,512]{1,0:T(8,128)(2,1)S(1)}, u32[]{:S(2)}, u32[]{:S(2)}) %collective-permute-start.31) | collective-permute-done | bytes 262176 | tf_op jit(solution)/shard_map/ppermute | solution.py:430
  133.6 1.4 collective-permute-start.36
  135.0 6.2 %shard_map.68 = (bf16[2560,2,512]{2,1,0:T(2,128)(2,1)}, f32[8,128]{1,0:T(8,128)S(1)}) custom-call(s32[4]{0:T(128)S(1)} %pad_add_fusion.refs_0_, s32[2,512]{1,0:T(2,128)S(1)} %get-tuple-element.40.refs_2_.refs_1_, bf16[2,512,512]{2,1,0:T(8,128)(2,1)S(1)} %shard_map.63.refs_3_.refs_2_, ...), custom_call_target="tpu_custom_call", output_to_operand_aliasing={{0}: (21, {})} | custom-call | flops 2952790016 | tf_op jit(solution)/shard_map/pallas_call | solution.py:37
  141.8 1.4 collective-permute-start.37
  143.2 6.4 %shard_map.70 = (bf16[2560,2,512]{2,1,0:T(2,128)(2,1)}, f32[8,128]{1,0:T(8,128)S(1)}) custom-call(s32[4]{0:T(128)S(1)} %pad_add_fusion.refs_0_, s32[2,512]{1,0:T(2,128)S(1)} %get-tuple-element.40.refs_2_.refs_1_, bf16[2,512,512]{2,1,0:T(8,128)(2,1)S(1)} %shard_map.63.refs_3_.refs_2_, ...), custom_call_target="tpu_custom_call", output_to_operand_aliasing={{0}: (21, {})} | custom-call | flops 2952790016 | tf_op jit(solution)/shard_map/pallas_call | solution.py:37
  150.0 1.4 collective-permute-start.38
  151.4 6.2 %shard_map.72 = (bf16[2560,2,512]{2,1,0:T(2,128)(2,1)}, f32[8,128]{1,0:T(8,128)S(1)}) custom-call(s32[4]{0:T(128)S(1)} %pad_add_fusion.refs_0_, s32[2,512]{1,0:T(2,128)S(1)} %get-tuple-element.40.refs_2_.refs_1_, bf16[2,512,512]{2,1,0:T(8,128)(2,1)S(1)} %shard_map.63.refs_3_.refs_2_, ...), custom_call_target="tpu_custom_call", output_to_operand_aliasing={{0}: (21, {})} | custom-call | flops 2952790016 | tf_op jit(solution)/shard_map/pallas_call | solution.py:37
  157.6 7.0 %shard_map.73 = (bf16[2560,2,512]{2,1,0:T(2,128)(2,1)}, f32[8,128]{1,0:T(8,128)}) custom-call(s32[4]{0:T(128)S(1)} %pad_add_fusion.refs_0_, s32[2,512]{1,0:T(2,128)S(1)} %get-tuple-element.40.refs_2_.refs_1_, bf16[2,512,512]{2,1,0:T(8,128)(2,1)S(1)} %shard_map.63.refs_3_.refs_2_, ...), custom_call_target="tpu_custom_call", output_to_operand_aliasing={{0}: (21, {})} | custom-call | flops 2952790016 | tf_op jit(solution)/shard_map/pallas_call | solution.py:37
  (111 shorter events, 13.5 us)
Async XLA Ops:
  3.9 23.9 %copy-start.9 = (bf16[256,512]{1,0:T(8,128)(2,1)}, bf16[256,512]{1,0:T(8,128)(2,1)S(1)}, u32[]{:S(2)}) copy-start(bf16[256,512]{1,0:T(8,128)(2,1)S(1)} %get-tuple-element.53.refs_2_) | copy-start | bytes 786436
  3.9 23.9 %copy-start.11 = (bf16[256,512]{1,0:T(8,128)(2,1)}, bf16[256,512]{1,0:T(8,128)(2,1)S(1)}, u32[]{:S(2)}) copy-start(bf16[256,512]{1,0:T(8,128)(2,1)S(1)} %get-tuple-element.52.refs_2_) | copy-start | bytes 786436
  3.9 23.9 %copy-start.13 = (bf16[256,512]{1,0:T(8,128)(2,1)}, bf16[256,512]{1,0:T(8,128)(2,1)S(1)}, u32[]{:S(2)}) copy-start(bf16[256,512]{1,0:T(8,128)(2,1)S(1)} %get-tuple-element.50.refs_2_) | copy-start | bytes 786436
  3.9 23.9 %copy-start.15 = (bf16[256,512]{1,0:T(8,128)(2,1)}, bf16[256,512]{1,0:T(8,128)(2,1)S(1)}, u32[]{:S(2)}) copy-start(bf16[256,512]{1,0:T(8,128)(2,1)S(1)} %get-tuple-element.49.refs_2_) | copy-start | bytes 786436
  3.9 26.2 %copy-start.5 = (bf16[256,512]{1,0:T(8,128)(2,1)}, bf16[256,512]{1,0:T(8,128)(2,1)S(1)}, u32[]{:S(2)}) copy-start(bf16[256,512]{1,0:T(8,128)(2,1)S(1)} %get-tuple-element.39.refs_4_.refs_2_) | copy-start | bytes 786436
  15.0 33.2 %copy-start.18 = (bf16[256,512]{1,0:T(8,128)(2,1)S(1)}, bf16[256,512]{1,0:T(8,128)(2,1)}, u32[]{:S(2)}) copy-start(bf16[256,512]{1,0:T(8,128)(2,1)} %copy-done.17) | copy-start | bytes 786436
  15.0 12.7 %collective-permute-start.2 = (bf16[512,2,512]{2,1,0:T(2,128)(2,1)S(1)}, bf16[512,2,512]{2,1,0:T(2,128)(2,1)S(1)}, u32[]{:S(2)}, u32[]{:S(2)}) collective-permute-start(bf16[512,2,512]{2,1,0:T(2,128)(2,1)S(1)} %get-tuple-element.47), channel_id=1, source_target_pairs={{0,8},{8,0},{16,24},{24,16},{1,9},{9,1},{17,25},{25,17},{2,10},{10... | collective-permute-start | bytes 3145736 | tf_op jit(solution)/shard_map/ppermute | solution.py:421
  15.5 11.6 %collective-permute-start = (bf16[256,512]{1,0:T(8,128)(2,1)S(1)}, bf16[256,512]{1,0:T(8,128)(2,1)S(1)}, u32[]{:S(2)}, u32[]{:S(2)}) collective-permute-start(bf16[256,512]{1,0:T(8,128)(2,1)S(1)} %get-tuple-element.41.refs_1_.refs_11_), channel_id=1, source_target_pairs={{0,2},{1,3},{2,4},{3,5},{4,6},{5,7},{6,0},{7,1},{8,10},{9,11},{10,... | collective-permute-start | bytes 786440 | tf_op jit(solution)/shard_map/ppermute | solution.py:430
  18.2 15.0 %collective-permute-start.3 = (bf16[256,512]{1,0:T(8,128)(2,1)S(1)}, bf16[256,512]{1,0:T(8,128)(2,1)S(1)}, u32[]{:S(2)}, u32[]{:S(2)}) collective-permute-start(bf16[256,512]{1,0:T(8,128)(2,1)S(1)} %get-tuple-element.41.refs_1_.refs_11_), channel_id=1, source_target_pairs={{0,1},{1,0},{2,3},{3,2},{4,5},{5,4},{6,7},{7,6},{8,9},{9,8},{10,11... | collective-permute-start | bytes 786440 | tf_op jit(solution)/shard_map/ppermute | solution.py:424
  27.7 9.9 %collective-permute-start.1 = (bf16[256,512]{1,0:T(8,128)(2,1)S(1)}, bf16[256,512]{1,0:T(8,128)(2,1)S(1)}, u32[]{:S(2)}, u32[]{:S(2)}) collective-permute-start(bf16[256,512]{1,0:T(8,128)(2,1)S(1)} %shard_map.48.refs_4_.refs_2_.refs_12_), channel_id=1, source_target_pairs={{0,2},{1,3},{2,4},{3,5},{4,6},{5,7},{6,0},{7,1},{8,10},{9,11},{10,... | collective-permute-start | bytes 786440 | tf_op jit(solution)/shard_map/ppermute | solution.py:430
  27.8 29.2 %copy-start.16 = (bf16[256,512]{1,0:T(8,128)(2,1)S(1)}, bf16[256,512]{1,0:T(8,128)(2,1)}, u32[]{:S(2)}) copy-start(bf16[256,512]{1,0:T(8,128)(2,1)} %copy-done.15) | copy-start | bytes 786436
  30.1 37.8 %collective-permute-start.10 = (bf16[512,2,512]{2,1,0:T(2,128)(2,1)S(1)}, bf16[512,2,512]{2,1,0:T(2,128)(2,1)}, u32[]{:S(2)}, u32[]{:S(2)}) collective-permute-start(bf16[512,2,512]{2,1,0:T(2,128)(2,1)S(1)} %shard_map.49.refs_3_.refs_2_), channel_id=1, source_target_pairs={{0,16},{8,24},{16,0},{24,8},{1,17},{9,25},{17,1},{25,9},{2,18},{10... | collective-permute-start | bytes 3145736 | tf_op jit(solution)/shard_map/ppermute | solution.py:427
  31.6 9.1 %collective-permute-start.5 = (bf16[256,512]{1,0:T(8,128)(2,1)S(1)}, bf16[256,512]{1,0:T(8,128)(2,1)S(1)}, u32[]{:S(2)}, u32[]{:S(2)}) collective-permute-start(bf16[256,512]{1,0:T(8,128)(2,1)S(1)} %shard_map.48.refs_4_.refs_2_.refs_12_), channel_id=1, source_target_pairs={{0,1},{1,0},{2,3},{3,2},{4,5},{5,4},{6,7},{7,6},{8,9},{9,8},{10,11... | collective-permute-start | bytes 786440 | tf_op jit(solution)/shard_map/ppermute | solution.py:424
  39.1 9.1 %collective-permute-start.4 = (bf16[256,512]{1,0:T(8,128)(2,1)S(1)}, bf16[256,512]{1,0:T(8,128)(2,1)S(1)}, u32[]{:S(2)}, u32[]{:S(2)}) collective-permute-start(bf16[256,512]{1,0:T(8,128)(2,1)S(1)} %shard_map.50.refs_3_.refs_13_.refs_11_), channel_id=1, source_target_pairs={{0,2},{1,3},{2,4},{3,5},{4,6},{5,7},{6,0},{7,1},{8,10},{9,11},{10,... | collective-permute-start | bytes 786440 | tf_op jit(solution)/shard_map/ppermute | solution.py:430
  39.2 41.5 %collective-permute-start.16 = (bf16[512,2,512]{2,1,0:T(2,128)(2,1)}, bf16[512,2,512]{2,1,0:T(2,128)(2,1)}, u32[]{:S(2)}, u32[]{:S(2)}) collective-permute-start(bf16[512,2,512]{2,1,0:T(2,128)(2,1)} %get-tuple-element.55.refs_5_), channel_id=1, source_target_pairs={{0,8},{8,0},{16,24},{24,16},{1,9},{9,1},{17,25},{25,17},{2,10},{10... | collective-permute-start | bytes 3145736 | tf_op jit(solution)/shard_map/ppermute | solution.py:421
  39.3 10.8 %collective-permute-start.7 = (bf16[256,512]{1,0:T(8,128)(2,1)S(1)}, bf16[256,512]{1,0:T(8,128)(2,1)S(1)}, u32[]{:S(2)}, u32[]{:S(2)}) collective-permute-start(bf16[256,512]{1,0:T(8,128)(2,1)S(1)} %shard_map.50.refs_3_.refs_13_.refs_11_), channel_id=1, source_target_pairs={{0,1},{1,0},{2,3},{3,2},{4,5},{5,4},{6,7},{7,6},{8,9},{9,8},{10,11... | collective-permute-start | bytes 786440 | tf_op jit(solution)/shard_map/ppermute | solution.py:424
  48.8 8.2 %collective-permute-start.6 = (bf16[256,512]{1,0:T(8,128)(2,1)S(1)}, bf16[256,512]{1,0:T(8,128)(2,1)S(1)}, u32[]{:S(2)}, u32[]{:S(2)}) collective-permute-start(bf16[256,512]{1,0:T(8,128)(2,1)S(1)} %shard_map.51.refs_3_.refs_4_.refs_14_.refs_12_), channel_id=1, source_target_pairs={{0,2},{1,3},{2,4},{3,5},{4,6},{5,7},{6,0},{7,1},{8,10},{9,11},{10,... | collective-permute-start | bytes 786440 | tf_op jit(solution)/shard_map/ppermute | solution.py:430
  48.8 9.9 %collective-permute-start.8 = (bf16[256,512]{1,0:T(8,128)(2,1)S(1)}, bf16[256,512]{1,0:T(8,128)(2,1)S(1)}, u32[]{:S(2)}, u32[]{:S(2)}) collective-permute-start(bf16[256,512]{1,0:T(8,128)(2,1)S(1)} %shard_map.51.refs_3_.refs_4_.refs_14_.refs_12_), channel_id=1, source_target_pairs={{0,1},{1,0},{2,3},{3,2},{4,5},{5,4},{6,7},{7,6},{8,9},{9,8},{10,11... | collective-permute-start | bytes 786440 | tf_op jit(solution)/shard_map/ppermute | solution.py:424
  57.6 8.3 %collective-permute-start.11 = (bf16[256,512]{1,0:T(8,128)(2,1)S(1)}, bf16[256,512]{1,0:T(8,128)(2,1)}, u32[]{:S(2)}, u32[]{:S(2)}) collective-permute-start(bf16[256,512]{1,0:T(8,128)(2,1)S(1)} %shard_map.52.refs_3_.refs_5_.refs_15_.refs_13_.refs_11_), channel_id=1, source_target_pairs={{0,2},{1,3},{2,4},{3,5},{4,6},{5,7},{6,0},{7,1},{8,10},{9,11},{10,... | collective-permute-start | bytes 786440 | tf_op jit(solution)/shard_map/ppermute | solution.py:430
  58.7 25.5 %copy-start.12 = (bf16[256,512]{1,0:T(8,128)(2,1)S(1)}, bf16[256,512]{1,0:T(8,128)(2,1)}, u32[]{:S(2)}) copy-start(bf16[256,512]{1,0:T(8,128)(2,1)} %copy-done.11) | copy-start | bytes 786436
  71.3 18.1 %collective-permute-start.15 = (bf16[512,2,512]{2,1,0:T(2,128)(2,1)S(1)}, bf16[512,2,512]{2,1,0:T(2,128)(2,1)S(1)}, u32[]{:S(2)}, u32[]{:S(2)}) collective-permute-start(bf16[512,2,512]{2,1,0:T(2,128)(2,1)S(1)} %get-tuple-element.51.refs_11_.refs_3_), channel_id=1, source_target_pairs={{0,8},{8,0},{16,24},{24,16},{1,9},{9,1},{17,25},{25,17},{2,10},{10... | collective-permute-start | bytes 3145736 | tf_op jit(solution)/shard_map/ppermute | solution.py:421
  71.3 8.7 %collective-permute-start.9 = (bf16[256,512]{1,0:T(8,128)(2,1)S(1)}, bf16[256,512]{1,0:T(8,128)(2,1)S(1)}, u32[]{:S(2)}, u32[]{:S(2)}) collective-permute-start(bf16[256,512]{1,0:T(8,128)(2,1)S(1)} %shard_map.52.refs_3_.refs_5_.refs_15_.refs_13_.refs_11_), channel_id=1, source_target_pairs={{0,1},{1,0},{2,3},{3,2},{4,5},{5,4},{6,7},{7,6},{8,9},{9,8},{10,11... | collective-permute-start | bytes 786440 | tf_op jit(solution)/shard_map/ppermute | solution.py:424
  72.6 10.2 %collective-permute-start.13 = (bf16[256,512]{1,0:T(8,128)(2,1)S(1)}, bf16[256,512]{1,0:T(8,128)(2,1)S(1)}, u32[]{:S(2)}, u32[]{:S(2)}) collective-permute-start(bf16[256,512]{1,0:T(8,128)(2,1)S(1)} %shard_map.53.refs_4_.refs_14_.refs_12_), channel_id=1, source_target_pairs={{0,2},{1,3},{2,4},{3,5},{4,6},{5,7},{6,0},{7,1},{8,10},{9,11},{10,... | collective-permute-start | bytes 786440 | tf_op jit(solution)/shard_map/ppermute | solution.py:430
  72.6 10.8 %collective-permute-start.17 = (bf16[256,512]{1,0:T(8,128)(2,1)S(1)}, bf16[256,512]{1,0:T(8,128)(2,1)S(1)}, u32[]{:S(2)}, u32[]{:S(2)}) collective-permute-start(bf16[256,512]{1,0:T(8,128)(2,1)S(1)} %get-tuple-element.56.refs_1_), channel_id=1, source_target_pairs={{8,10},{24,26},{1,3},{17,19}} | collective-permute-start | bytes 786440 | tf_op jit(solution)/shard_map/ppermute | solution.py:503
  80.1 24.0 %collective-permute-start.22 = (bf16[512,1024]{1,0:T(8,128)(2,1)S(1)}, bf16[512,1024]{1,0:T(8,128)(2,1)S(1)}, u32[]{:S(2)}, u32[]{:S(2)}) collective-permute-start(bf16[512,1024]{1,0:T(8,128)(2,1)S(1)} %get-tuple-element.58.refs_2_.refs_3_), channel_id=1, source_target_pairs={{0,8},{8,0},{16,24},{24,16},{1,9},{9,1},{17,25},{25,17},{2,10},{10... | collective-permute-start | bytes 3145736 | tf_op jit(solution)/shard_map/ppermute | solution.py:421
  80.7 30.8 %collective-permute-start.12 = (bf16[2,512,512]{2,1,0:T(8,128)(2,1)S(1)}, bf16[2,512,512]{2,1,0:T(8,128)(2,1)S(1)}, u32[]{:S(2)}, u32[]{:S(2)}) collective-permute-start(bf16[2,512,512]{2,1,0:T(8,128)(2,1)S(1)} %shard_map.55.refs_3_.refs_1_), channel_id=1, source_target_pairs={{0,16},{8,24},{16,0},{24,8},{1,17},{9,25},{17,1},{25,9},{2,18},{10... | collective-permute-start | bytes 3145736 | tf_op jit(solution)/shard_map/ppermute | solution.py:427
  82.8 2.0 %collective-permute-start.18 = (bf16[256,512]{1,0:T(8,128)(2,1)S(1)}, bf16[256,512]{1,0:T(8,128)(2,1)S(1)}, u32[]{:S(2)}, u32[]{:S(2)}) collective-permute-start(bf16[256,512]{1,0:T(8,128)(2,1)S(1)} %get-tuple-element.56.refs_1_), channel_id=1, source_target_pairs={{8,12},{24,28},{1,5},{17,21}} | collective-permute-start | bytes 786440 | tf_op jit(solution)/shard_map/ppermute | solution.py:503
  83.5 5.3 %collective-permute-start.19 = (bf16[256,512]{1,0:T(8,128)(2,1)S(1)}, bf16[256,512]{1,0:T(8,128)(2,1)S(1)}, u32[]{:S(2)}, u32[]{:S(2)}) collective-permute-start(bf16[256,512]{1,0:T(8,128)(2,1)S(1)} %get-tuple-element.56.refs_1_), channel_id=1, source_target_pairs={{8,14},{24,30},{1,7},{17,23}} | collective-permute-start | bytes 786440 | tf_op jit(solution)/shard_map/ppermute | solution.py:503
  84.8 11.4 %collective-permute-start.20 = (bf16[256,512]{1,0:T(8,128)(2,1)S(1)}, bf16[256,512]{1,0:T(8,128)(2,1)S(1)}, u32[]{:S(2)}, u32[]{:S(2)}) collective-permute-start(bf16[256,512]{1,0:T(8,128)(2,1)S(1)} %shard_map.53.refs_4_.refs_14_.refs_12_), channel_id=1, source_target_pairs={{0,1},{1,0},{2,3},{3,2},{4,5},{5,4},{6,7},{7,6},{8,9},{9,8},{10,11... | collective-permute-start | bytes 786440 | tf_op jit(solution)/shard_map/ppermute | solution.py:424
  88.8 12.9 %collective-permute-start.14 = (bf16[256,512]{1,0:T(8,128)(2,1)S(1)}, bf16[256,512]{1,0:T(8,128)(2,1)S(1)}, u32[]{:S(2)}, u32[]{:S(2)}) collective-permute-start(bf16[256,512]{1,0:T(8,128)(2,1)S(1)} %shard_map.56.refs_5_.refs_15_.refs_13_.refs_11_), channel_id=1, source_target_pairs={{0,2},{1,3},{2,4},{3,5},{4,6},{5,7},{6,0},{7,1},{8,10},{9,11},{10,... | collective-permute-start | bytes 786440 | tf_op jit(solution)/shard_map/ppermute | solution.py:430
  89.4 14.1 %collective-permute-start.23 = (bf16[256,512]{1,0:T(8,128)(2,1)S(1)}, bf16[256,512]{1,0:T(8,128)(2,1)S(1)}, u32[]{:S(2)}, u32[]{:S(2)}) collective-permute-start(bf16[256,512]{1,0:T(8,128)(2,1)S(1)} %shard_map.57.refs_8_.refs_1_), channel_id=1, source_target_pairs={{8,9},{24,25},{1,0},{17,16},{10,11},{26,27},{3,2},{19,18},{12,13},... | collective-permute-start | bytes 786440 | tf_op jit(solution)/shard_map/ppermute | solution.py:530
  96.2 9.9 %collective-permute-start.24 = (bf16[256,512]{1,0:T(8,128)(2,1)S(1)}, bf16[256,512]{1,0:T(8,128)(2,1)S(1)}, u32[]{:S(2)}, u32[]{:S(2)}) collective-permute-start(bf16[256,512]{1,0:T(8,128)(2,1)S(1)} %shard_map.56.refs_5_.refs_15_.refs_13_.refs_11_), channel_id=1, source_target_pairs={{0,1},{1,0},{2,3},{3,2},{4,5},{5,4},{6,7},{7,6},{8,9},{9,8},{10,11... | collective-permute-start | bytes 786440 | tf_op jit(solution)/shard_map/ppermute | solution.py:424
  102.2 8.7 %collective-permute-start.21 = (bf16[256,512]{1,0:T(8,128)(2,1)S(1)}, bf16[256,512]{1,0:T(8,128)(2,1)S(1)}, u32[]{:S(2)}, u32[]{:S(2)}) collective-permute-start(bf16[256,512]{1,0:T(8,128)(2,1)S(1)} %shard_map.59.refs_3_.refs_14_.refs_12_), channel_id=1, source_target_pairs={{0,2},{1,3},{2,4},{3,5},{4,6},{5,7},{6,0},{7,1},{8,10},{9,11},{10,... | collective-permute-start | bytes 786440 | tf_op jit(solution)/shard_map/ppermute | solution.py:430
  104.1 21.8 %copy-start.2 = (bf16[2,512,512]{2,1,0:T(8,128)(2,1)S(1)}, bf16[2,512,512]{2,1,0:T(8,128)(2,1)}, u32[]{:S(2)}) copy-start(bf16[2,512,512]{2,1,0:T(8,128)(2,1)} %refs_4_.9) | copy-start | bytes 3145732
  112.1 17.2 %collective-permute-start.25 = (bf16[2,512,512]{2,1,0:T(8,128)(2,1)S(1)}, bf16[2,512,512]{2,1,0:T(8,128)(2,1)S(1)}, u32[]{:S(2)}, u32[]{:S(2)}) collective-permute-start(bf16[2,512,512]{2,1,0:T(8,128)(2,1)S(1)} %shard_map.63.refs_3_.refs_2_), channel_id=1, source_target_pairs={{0,8},{8,0},{16,24},{24,16},{1,9},{9,1},{17,25},{25,17},{2,10},{10... | collective-permute-start | bytes 3145736 | tf_op jit(solution)/shard_map/ppermute | solution.py:421
  112.2 8.7 %collective-permute-start.26 = (bf16[256,512]{1,0:T(8,128)(2,1)S(1)}, bf16[256,512]{1,0:T(8,128)(2,1)S(1)}, u32[]{:S(2)}, u32[]{:S(2)}) collective-permute-start(bf16[256,512]{1,0:T(8,128)(2,1)S(1)} %shard_map.60.refs_4_.refs_6_), channel_id=1, source_target_pairs={{0,16},{8,24},{16,0},{24,8},{1,17},{9,25},{17,1},{25,9},{2,18},{10... | collective-permute-start | bytes 786440 | tf_op jit(solution)/shard_map/ppermute | solution.py:427
  113.2 8.4 %collective-permute-start.30 = (bf16[256,512]{1,0:T(8,128)(2,1)S(1)}, bf16[256,512]{1,0:T(8,128)(2,1)S(1)}, u32[]{:S(2)}, u32[]{:S(2)}) collective-permute-start(bf16[256,512]{1,0:T(8,128)(2,1)S(1)} %shard_map.59.refs_3_.refs_14_.refs_12_), channel_id=1, source_target_pairs={{0,1},{1,0},{2,3},{3,2},{4,5},{5,4},{6,7},{7,6},{8,9},{9,8},{10,11... | collective-permute-start | bytes 786440 | tf_op jit(solution)/shard_map/ppermute | solution.py:424
  113.9 9.9 %collective-permute-start.29 = (bf16[256,512]{1,0:T(8,128)(2,1)S(1)}, bf16[256,512]{1,0:T(8,128)(2,1)S(1)}, u32[]{:S(2)}, u32[]{:S(2)}) collective-permute-start(bf16[256,512]{1,0:T(8,128)(2,1)S(1)} %shard_map.62.refs_3_.refs_15_.refs_13_.refs_11_), channel_id=1, source_target_pairs={{0,2},{1,3},{2,4},{3,5},{4,6},{5,7},{6,0},{7,1},{8,10},{9,11},{10,... | collective-permute-start | bytes 786440 | tf_op jit(solution)/shard_map/ppermute | solution.py:430
  113.9 10.5 %collective-permute-start.27 = (bf16[256,512]{1,0:T(8,128)(2,1)S(1)}, bf16[256,512]{1,0:T(8,128)(2,1)S(1)}, u32[]{:S(2)}, u32[]{:S(2)}) collective-permute-start(bf16[256,512]{1,0:T(8,128)(2,1)S(1)} %shard_map.60.refs_4_.refs_6_), channel_id=1, source_target_pairs={{0,8},{8,0},{16,24},{24,16},{1,9},{9,1},{17,25},{25,17},{2,10},{10... | collective-permute-start | bytes 786440 | tf_op jit(solution)/shard_map/ppermute | solution.py:421
  120.9 5.0 %collective-permute-start.28 = (bf16[256,512]{1,0:T(8,128)(2,1)S(1)}, bf16[256,512]{1,0:T(8,128)(2,1)S(1)}, u32[]{:S(2)}, u32[]{:S(2)}) collective-permute-start(bf16[256,512]{1,0:T(8,128)(2,1)S(1)} %collective-permute-done.26.refs_7_), channel_id=1, source_target_pairs={{0,8},{8,0},{16,24},{24,16},{1,9},{9,1},{17,25},{25,17},{2,10},{10... | collective-permute-start | bytes 786440 | tf_op jit(solution)/shard_map/ppermute | solution.py:421
  121.6 9.6 %collective-permute-start.32 = (bf16[256,512]{1,0:T(8,128)(2,1)S(1)}, bf16[256,512]{1,0:T(8,128)(2,1)S(1)}, u32[]{:S(2)}, u32[]{:S(2)}) collective-permute-start(bf16[256,512]{1,0:T(8,128)(2,1)S(1)} %shard_map.62.refs_3_.refs_15_.refs_13_.refs_11_), channel_id=1, source_target_pairs={{0,1},{1,0},{2,3},{3,2},{4,5},{5,4},{6,7},{7,6},{8,9},{9,8},{10,11... | collective-permute-start | bytes 786440 | tf_op jit(solution)/shard_map/ppermute | solution.py:424
  124.4 9.1 %collective-permute-start.31 = (bf16[256,512]{1,0:T(8,128)(2,1)S(1)}, bf16[256,512]{1,0:T(8,128)(2,1)S(1)}, u32[]{:S(2)}, u32[]{:S(2)}) collective-permute-start(bf16[256,512]{1,0:T(8,128)(2,1)S(1)} %shard_map.64.refs_10_.refs_14_.refs_12_), channel_id=1, source_target_pairs={{0,2},{1,3},{2,4},{3,5},{4,6},{5,7},{6,0},{7,1},{8,10},{9,11},{10,... | collective-permute-start | bytes 786440 | tf_op jit(solution)/shard_map/ppermute | solution.py:430
  124.5 16.7 %collective-permute-start.34 = (bf16[256,512]{1,0:T(8,128)(2,1)S(1)}, bf16[256,512]{1,0:T(8,128)(2,1)S(1)}, u32[]{:S(2)}, u32[]{:S(2)}) collective-permute-start(bf16[256,512]{1,0:T(8,128)(2,1)S(1)} %shard_map.64.refs_10_.refs_14_.refs_12_), channel_id=1, source_target_pairs={{0,1},{1,0},{2,3},{3,2},{4,5},{5,4},{6,7},{7,6},{8,9},{9,8},{10,11... | collective-permute-start | bytes 786440 | tf_op jit(solution)/shard_map/ppermute | solution.py:424
  133.5 8.2 %collective-permute-start.33 = (bf16[256,512]{1,0:T(8,128)(2,1)S(1)}, bf16[256,512]{1,0:T(8,128)(2,1)S(1)}, u32[]{:S(2)}, u32[]{:S(2)}) collective-permute-start(bf16[256,512]{1,0:T(8,128)(2,1)S(1)} %shard_map.67.refs_22_.refs_15_.refs_13_), channel_id=1, source_target_pairs={{0,2},{1,3},{2,4},{3,5},{4,6},{5,7},{6,0},{7,1},{8,10},{9,11},{10,... | collective-permute-start | bytes 786440 | tf_op jit(solution)/shard_map/ppermute | solution.py:430
  133.6 16.1 %collective-permute-start.36 = (bf16[256,512]{1,0:T(8,128)(2,1)S(1)}, bf16[256,512]{1,0:T(8,128)(2,1)S(1)}, u32[]{:S(2)}, u32[]{:S(2)}) collective-permute-start(bf16[256,512]{1,0:T(8,128)(2,1)S(1)} %shard_map.67.refs_22_.refs_15_.refs_13_), channel_id=1, source_target_pairs={{0,1},{1,0},{2,3},{3,2},{4,5},{5,4},{6,7},{7,6},{8,9},{9,8},{10,11... | collective-permute-start | bytes 786440 | tf_op jit(solution)/shard_map/ppermute | solution.py:424
  141.8 8.2 %collective-permute-start.35 = (bf16[256,512]{1,0:T(8,128)(2,1)S(1)}, bf16[256,512]{1,0:T(8,128)(2,1)S(1)}, u32[]{:S(2)}, u32[]{:S(2)}) collective-permute-start(bf16[256,512]{1,0:T(8,128)(2,1)S(1)} %shard_map.69.refs_22_.refs_14_), channel_id=1, source_target_pairs={{0,2},{1,3},{2,4},{3,5},{4,6},{5,7},{6,0},{7,1},{8,10},{9,11},{10,... | collective-permute-start | bytes 786440 | tf_op jit(solution)/shard_map/ppermute | solution.py:430
  141.8 15.8 %collective-permute-start.37 = (bf16[256,512]{1,0:T(8,128)(2,1)S(1)}, bf16[256,512]{1,0:T(8,128)(2,1)S(1)}, u32[]{:S(2)}, u32[]{:S(2)}) collective-permute-start(bf16[256,512]{1,0:T(8,128)(2,1)S(1)} %shard_map.69.refs_22_.refs_14_), channel_id=1, source_target_pairs={{0,1},{1,0},{2,3},{3,2},{4,5},{5,4},{6,7},{7,6},{8,9},{9,8},{10,11... | collective-permute-start | bytes 786440 | tf_op jit(solution)/shard_map/ppermute | solution.py:424
  150.0 7.6 %collective-permute-start.38 = (bf16[256,512]{1,0:T(8,128)(2,1)S(1)}, bf16[256,512]{1,0:T(8,128)(2,1)S(1)}, u32[]{:S(2)}, u32[]{:S(2)}) collective-permute-start(bf16[256,512]{1,0:T(8,128)(2,1)S(1)} %shard_map.71.refs_22_.refs_15_), channel_id=1, source_target_pairs={{0,1},{1,0},{2,3},{3,2},{4,5},{5,4},{6,7},{7,6},{8,9},{9,8},{10,11... | collective-permute-start | bytes 786440 | tf_op jit(solution)/shard_map/ppermute | solution.py:424
  (15 other events, 117.4 us)
